TPU v7x, 32 devices: a whole 2x2x4 slice. The times are simulated.
32 devices in a mesh: fsdp: 32 (over z, y, x, core).
Axes of the slice: x: 2, y: 2, z: 4, core: 2. Of those that a mesh axis runs over, the one named last changes fastest.
Arguments:
- tokens: bfloat16 [4096, 2048], P('fsdp'), may hold values from -6 to 6
- cotangent: bfloat16 [4096, 2048], P('fsdp'), may hold values from -6 to 6
- lengths: int32 [32, 4], P('fsdp'), may hold values from 1 to 64, 128 in all within a row
- routes: int32 [4096, 8], P('fsdp'), may hold values from 0 to 31, all different within a row; in each aligned block of 128 rows (0 to 127, 128 to 255, ...) at most 40 rows name the same one
- query_weight: bfloat16 [2048, 4096], P('fsdp'), may hold values from -0.125 to 0.125
- key_matrix: bfloat16 [2048, 512], P('fsdp'), may hold values from -0.125 to 0.125
- value_matrix: bfloat16 [2048, 512], P('fsdp'), may hold values from -0.125 to 0.125
- out_weight: bfloat16 [4096, 2048], P('fsdp'), may hold values from -0.375 to 0.375
- router_weight: bfloat16 [2048, 32], P('fsdp'), may hold values from -0.0625 to 0.0625
- expert_gate: bfloat16 [32, 2048, 768], P('fsdp'), may hold values from -0.125 to 0.125
- expert_up: bfloat16 [32, 2048, 768], P('fsdp'), may hold values from -0.125 to 0.125
- expert_down: bfloat16 [32, 768, 2048], P('fsdp'), may hold values from -0.875 to 0.875
- first_gain: float32 [2048], replicated, may hold values from 0.25 to 1.75
- second_gain: float32 [2048], replicated, may hold values from 0.25 to 1.75
- query_norm_gain: float32 [128], replicated, may hold values from 1 to 2
- key_gain: float32 [128], replicated, may hold values from 1 to 2
Outputs:
- output: bfloat16 [4096, 2048], P('fsdp')
- tokens_grad: float32 [4096, 2048], P('fsdp')
- query_grad: float32 [2048, 4096], P('fsdp')
- key_grad: float32 [2048, 512], P('fsdp')
- value_grad: float32 [2048, 512], P('fsdp')
- out_grad: float32 [4096, 2048], P('fsdp')
- router_grad: float32 [2048, 32], P('fsdp')
- gate_grad: float32 [32, 2048, 768], P('fsdp')
- up_grad: float32 [32, 2048, 768], P('fsdp')
- down_grad: float32 [32, 768, 2048], P('fsdp')
- first_gain_grad: float32 [2048], replicated
- second_gain_grad: float32 [2048], replicated
- query_gain_grad: float32 [128], replicated
- key_gain_grad: float32 [128], replicated
Inputs may be any that keep to these rules, and one draw needn't show every extreme that they name: `routes`: in each aligned block of 128 rows (the rows of one device) no expert is named by more than 40 rows. Each row of 4 lengths sums to 128.
All inputs are finite; a program needn't handle non-finite values.
Results may differ from a plain program's by a relative error of at most 0.015.
The roundings to bfloat16 on the way count: a program that leaves them out, or rounds other values in their place, can miss the bound.
Values may be sent and summed in bfloat16 or wider, within the bound.
No kernel may reach another device: no remote copies, remote signals or barrier semaphores. Data moves between devices by JAX's collectives and lax.ppermute only.
A program may use at most 320 MiB of HBM per device.

v0:
```python
import functools

import jax
import jax.numpy as jnp
from jax import lax
from jax.sharding import PartitionSpec as P

EPS = 1e-06
THETA = 1000000.0
NEGATIVE = -1e30
CONTRACT_ROWS = (((0,), (0,)), ((), ()))
CONTRACT_LAST = (((1,), (1,)), ((), ()))


def root_mean_square_norm(value_rows, gain):
    return (
        value_rows
        * lax.rsqrt(jnp.mean(value_rows * value_rows, axis=-1, keepdims=True) + EPS)
        * gain
    )


def sequence_layout(lengths, count_total):
    ends = jnp.cumsum(lengths)
    starts = ends - lengths
    places = jnp.arange(count_total, dtype=jnp.int32)
    member = ((places[:, None] >= starts[None, :]) & (places[:, None] < ends[None, :])).astype(
        jnp.int32
    )
    labels = jnp.arange(lengths.shape[0], dtype=jnp.int32)
    segment = jnp.sum(member * labels[None, :], axis=1)
    offset = jnp.sum(member * starts[None, :], axis=1)
    return (segment, places - offset)


def rotary_tables(position, width):
    half = width // 2
    inverse = jnp.power(THETA, -(jnp.arange(half, dtype=jnp.float32) * 2.0) / width)
    angle = position.astype(jnp.float32)[:, None] * inverse[None, :]
    angle = jnp.concatenate([angle, angle], axis=1)
    return (jnp.cos(angle), jnp.sin(angle))


def rotary_apply(value_rows, cosine_table, sine_table):
    half = value_rows.shape[-1] // 2
    turned = jnp.concatenate([-value_rows[..., half:], value_rows[..., :half]], axis=-1)
    return value_rows * cosine_table[:, None, :] + turned * sine_table[:, None, :]


def prepare(projected_query, projected_key, query_norm_gain, key_gain, cosine_table, sine_table):
    count_total = projected_query.shape[0]
    width = query_norm_gain.shape[0]
    query_rows = rotary_apply(
        root_mean_square_norm(projected_query.reshape(count_total, -1, width), query_norm_gain),
        cosine_table,
        sine_table,
    )
    key_rows = rotary_apply(
        root_mean_square_norm(projected_key.reshape(count_total, -1, width), key_gain),
        cosine_table,
        sine_table,
    )
    return (query_rows, key_rows)


def route_gates(logits, picks):
    peak = jnp.max(logits, axis=-1, keepdims=True)
    exponent = jnp.exp(logits - peak)
    shares = exponent / jnp.sum(exponent, axis=-1, keepdims=True)
    chosen = jnp.sum(shares[:, None, :] * picks, axis=-1)
    return chosen / jnp.sum(chosen, axis=-1, keepdims=True)


def swiglu(gate_part, up_part):
    return gate_part * jax.nn.sigmoid(gate_part) * up_part


def projection_sums(context_low, grad_attn_low):
    return lax.psum_scatter(
        lax.dot_general(
            context_low, grad_attn_low, CONTRACT_ROWS, preferred_element_type=jnp.float32
        ),
        "fsdp",
        scatter_dimension=0,
        tiled=True,
    )


def body(
    tokens,
    cotangent,
    lengths,
    routes,
    query_weight,
    key_matrix,
    value_matrix,
    out_weight,
    router_weight,
    expert_gate,
    expert_up,
    expert_down,
    first_gain,
    second_gain,
    query_norm_gain,
    key_gain,
):
    count_total, model = tokens.shape
    width = query_norm_gain.shape[0]
    heads = query_weight.shape[1] // width
    kv_heads = key_matrix.shape[1] // width
    head_group = heads // kv_heads
    choose = routes.shape[1]
    shards = lax.axis_size("fsdp")
    local_experts = expert_gate.shape[0]
    experts = shards * local_experts
    capacity = max(2, count_total * choose * 5 // (4 * experts))
    slots = experts * capacity
    scale = width ** (-0.5)
    attn_columns = heads * width
    kv_columns = kv_heads * width
    gathered = (
        lax.all_gather(query_weight, "fsdp", axis=0, tiled=True),
        lax.all_gather(key_matrix, "fsdp", axis=0, tiled=True),
        lax.all_gather(value_matrix, "fsdp", axis=0, tiled=True),
        lax.all_gather(router_weight, "fsdp", axis=0, tiled=True),
        lax.all_gather(out_weight, "fsdp", axis=0, tiled=True),
    )
    full_query, full_key, full_value, full_router, full_out = gathered
    inputs = tokens.astype(jnp.float32)
    normed_low = root_mean_square_norm(inputs, first_gain).astype(jnp.bfloat16)
    projected_query = jnp.dot(normed_low, full_query, preferred_element_type=jnp.float32)
    projected_key = jnp.dot(normed_low, full_key, preferred_element_type=jnp.float32)
    value_low = (
        jnp.dot(normed_low, full_value, preferred_element_type=jnp.float32)
        .astype(jnp.bfloat16)
        .reshape(count_total, kv_heads, width)
    )
    segment, position = sequence_layout(lengths[0], count_total)
    cosine_table, sine_table = rotary_tables(position, width)
    rotated, prepare_back = jax.vjp(
        functools.partial(prepare, cosine_table=cosine_table, sine_table=sine_table),
        projected_query,
        projected_key,
        query_norm_gain,
        key_gain,
    )
    query_low = rotated[0].astype(jnp.bfloat16).reshape(count_total, kv_heads, head_group, width)
    key_low = rotated[1].astype(jnp.bfloat16)
    places = jnp.arange(count_total, dtype=jnp.int32)
    allowed = (segment[:, None] == segment[None, :]) & (places[None, :] <= places[:, None])

    def score_table():
        raw = (
            jnp.einsum("ikgc,jkc->kgij", query_low, key_low, preferred_element_type=jnp.float32)
            * scale
        )
        return jnp.where(allowed, raw, NEGATIVE)

    scores = score_table()
    peak = jnp.max(scores, axis=-1, keepdims=True)
    log_total = peak + jnp.log(jnp.sum(jnp.exp(scores - peak), axis=-1, keepdims=True))
    shares_low = jnp.exp(scores - log_total).astype(jnp.bfloat16)
    context_low = (
        jnp.einsum("kgij,jkc->ikgc", shares_low, value_low, preferred_element_type=jnp.float32)
        .reshape(count_total, attn_columns)
        .astype(jnp.bfloat16)
    )
    hidden = inputs + jnp.dot(context_low, full_out, preferred_element_type=jnp.float32)
    second_low = root_mean_square_norm(hidden, second_gain).astype(jnp.bfloat16)
    logits = jnp.dot(second_low, full_router, preferred_element_type=jnp.float32)
    picks = (routes[:, :, None] == jnp.arange(experts, dtype=jnp.int32)[None, None, :]).astype(
        jnp.float32
    )
    gates, gates_back = jax.vjp(route_gates, logits, picks)
    flat_routes = routes.reshape(-1)
    hits = picks.reshape(count_total * choose, experts).astype(jnp.int32)
    rank = jnp.sum((jnp.cumsum(hits, axis=0) - hits) * hits, axis=1)
    place = flat_routes * capacity + rank
    owner = (
        jnp.full((slots,), count_total * choose, jnp.int32)
        .at[place]
        .set(jnp.arange(count_total * choose, dtype=jnp.int32))
    )
    source_rows = jnp.concatenate([second_low, jnp.zeros((1, model), jnp.bfloat16)], axis=0)[
        owner // choose
    ]
    received = lax.all_to_all(
        source_rows.reshape(shards, local_experts * capacity, model),
        "fsdp",
        split_axis=0,
        concat_axis=0,
        tiled=True,
    )
    received = received.reshape(shards, local_experts, capacity, model)
    gate_part = jnp.einsum(
        "sxcd,xdf->sxcf", received, expert_gate, preferred_element_type=jnp.float32
    )
    up_part = jnp.einsum("sxcd,xdf->sxcf", received, expert_up, preferred_element_type=jnp.float32)
    units, swiglu_back = jax.vjp(swiglu, gate_part, up_part)
    units_low = units.astype(jnp.bfloat16)
    result_low = jnp.einsum(
        "sxcf,xfd->sxcd", units_low, expert_down, preferred_element_type=jnp.float32
    ).astype(jnp.bfloat16)
    returned = lax.all_to_all(
        result_low.reshape(shards, local_experts * capacity, model),
        "fsdp",
        split_axis=0,
        concat_axis=0,
        tiled=True,
    )
    picked = returned.reshape(slots, model)[place].reshape(count_total, choose, model)
    output = (hidden + jnp.sum(gates[:, :, None] * picked.astype(jnp.float32), axis=1)).astype(
        jnp.bfloat16
    )
    grad_out = cotangent.astype(jnp.float32)
    grad_result = (
        (gates[:, :, None] * grad_out[:, None, :])
        .astype(jnp.bfloat16)
        .reshape(count_total * choose, model)
    )
    grad_gates = jnp.sum(grad_out[:, None, :] * picked.astype(jnp.float32), axis=-1)
    grad_slots = jnp.concatenate([grad_result, jnp.zeros((1, model), jnp.bfloat16)], axis=0)[owner]
    grad_received = lax.all_to_all(
        grad_slots.reshape(shards, local_experts * capacity, model),
        "fsdp",
        split_axis=0,
        concat_axis=0,
        tiled=True,
    )
    grad_received = grad_received.reshape(shards, local_experts, capacity, model)
    grad_units = jnp.einsum(
        "sxcd,xfd->sxcf", grad_received, expert_down, preferred_element_type=jnp.float32
    )
    down_grad = jnp.einsum(
        "sxcf,sxcd->xfd", units_low, grad_received, preferred_element_type=jnp.float32
    )
    grad_gate_part, grad_up_part = swiglu_back(grad_units)
    grad_gate_low = grad_gate_part.astype(jnp.bfloat16)
    grad_up_low = grad_up_part.astype(jnp.bfloat16)
    gate_grad = jnp.einsum(
        "sxcd,sxcf->xdf", received, grad_gate_low, preferred_element_type=jnp.float32
    )
    up_grad = jnp.einsum(
        "sxcd,sxcf->xdf", received, grad_up_low, preferred_element_type=jnp.float32
    )
    grad_rows = jnp.einsum(
        "sxcf,xdf->sxcd", grad_gate_low, expert_gate, preferred_element_type=jnp.float32
    )
    grad_rows = (
        grad_rows
        + jnp.einsum("sxcf,xdf->sxcd", grad_up_low, expert_up, preferred_element_type=jnp.float32)
    ).astype(jnp.bfloat16)
    grad_back = lax.all_to_all(
        grad_rows.reshape(shards, local_experts * capacity, model),
        "fsdp",
        split_axis=0,
        concat_axis=0,
        tiled=True,
    )
    grad_logits_low = gates_back(grad_gates)[0].astype(jnp.bfloat16)
    again = (
        lax.all_gather(query_weight, "fsdp", axis=0, tiled=True),
        lax.all_gather(key_matrix, "fsdp", axis=0, tiled=True),
        lax.all_gather(value_matrix, "fsdp", axis=0, tiled=True),
        lax.all_gather(router_weight, "fsdp", axis=0, tiled=True),
        lax.all_gather(out_weight, "fsdp", axis=0, tiled=True),
    )
    back_query, back_key, back_value, back_router, back_out = again
    grad_second = jnp.sum(
        grad_back.reshape(slots, model)[place]
        .reshape(count_total, choose, model)
        .astype(jnp.float32),
        axis=1,
    )
    grad_second = grad_second + lax.dot_general(
        grad_logits_low, back_router, CONTRACT_LAST, preferred_element_type=jnp.float32
    )
    second_vals, second_back = jax.vjp(root_mean_square_norm, hidden, second_gain)
    grad_hidden_part, second_gain_term = second_back(grad_second)
    grad_hidden = grad_out + grad_hidden_part
    grad_attn_low = grad_hidden.astype(jnp.bfloat16)
    grad_context_low = lax.dot_general(
        grad_attn_low, back_out, CONTRACT_LAST, preferred_element_type=jnp.float32
    ).astype(jnp.bfloat16)
    grad_context_low = grad_context_low.reshape(count_total, kv_heads, head_group, width)
    shares = jnp.exp(score_table() - log_total)
    grad_shares = jnp.einsum(
        "ikgc,jkc->kgij", grad_context_low, value_low, preferred_element_type=jnp.float32
    )
    grad_scores_low = (
        shares * (grad_shares - jnp.sum(shares * grad_shares, axis=-1, keepdims=True))
    ).astype(jnp.bfloat16)
    grad_rot_query = (
        jnp.einsum("kgij,jkc->ikgc", grad_scores_low, key_low, preferred_element_type=jnp.float32)
        * scale
    ).reshape(count_total, heads, width)
    grad_rot_key = (
        jnp.einsum("kgij,ikgc->jkc", grad_scores_low, query_low, preferred_element_type=jnp.float32)
        * scale
    )
    grad_value_low = (
        jnp.einsum(
            "kgij,ikgc->jkc", shares_low, grad_context_low, preferred_element_type=jnp.float32
        )
        .astype(jnp.bfloat16)
        .reshape(count_total, kv_columns)
    )
    grad_proj_query, grad_proj_key, query_gain_term, key_gain_term = prepare_back(
        (grad_rot_query, grad_rot_key)
    )
    grad_query_low = grad_proj_query.astype(jnp.bfloat16)
    grad_key_low = grad_proj_key.astype(jnp.bfloat16)
    grad_normed = lax.dot_general(
        grad_query_low, back_query, CONTRACT_LAST, preferred_element_type=jnp.float32
    )
    grad_normed = grad_normed + lax.dot_general(
        grad_key_low, back_key, CONTRACT_LAST, preferred_element_type=jnp.float32
    )
    grad_normed = grad_normed + lax.dot_general(
        grad_value_low, back_value, CONTRACT_LAST, preferred_element_type=jnp.float32
    )
    first_vals, first_back = jax.vjp(root_mean_square_norm, inputs, first_gain)
    grad_input_part, first_gain_term = first_back(grad_normed)
    tokens_grad = grad_hidden + grad_input_part
    parts = [
        lax.dot_general(
            normed_low, grad_query_low, CONTRACT_ROWS, preferred_element_type=jnp.float32
        ),
        lax.dot_general(
            normed_low, grad_key_low, CONTRACT_ROWS, preferred_element_type=jnp.float32
        ),
        lax.dot_general(
            normed_low, grad_value_low, CONTRACT_ROWS, preferred_element_type=jnp.float32
        ),
        lax.dot_general(
            second_low, grad_logits_low, CONTRACT_ROWS, preferred_element_type=jnp.float32
        ),
    ]
    front = lax.psum_scatter(
        jnp.concatenate(parts, axis=1), "fsdp", scatter_dimension=0, tiled=True
    )
    query_grad = front[:, :attn_columns]
    key_grad = front[:, attn_columns : attn_columns + kv_columns]
    value_grad = front[:, attn_columns + kv_columns : attn_columns + 2 * kv_columns]
    router_grad = front[:, attn_columns + 2 * kv_columns :]
    out_grad = projection_sums(context_low, grad_attn_low)
    gain_sums = lax.psum(
        (first_gain_term, second_gain_term, query_gain_term, key_gain_term), "fsdp"
    )
    return (
        output,
        tokens_grad,
        query_grad,
        key_grad,
        value_grad,
        out_grad,
        router_grad,
        gate_grad,
        up_grad,
        down_grad,
        gain_sums[0],
        gain_sums[1],
        gain_sums[2],
        gain_sums[3],
    )


def solution(mesh):
    placed = (
        P("fsdp", None),
        P("fsdp", None),
        P("fsdp", None),
        P("fsdp", None),
        P("fsdp", None),
        P("fsdp", None),
        P("fsdp", None),
        P("fsdp", None),
        P("fsdp", None),
        P("fsdp", None, None),
        P("fsdp", None, None),
        P("fsdp", None, None),
        P(),
        P(),
        P(),
        P(),
    )
    return jax.shard_map(
        body,
        mesh=mesh,
        in_specs=placed,
        out_specs=(
            P("fsdp", None),
            P("fsdp", None),
            P("fsdp", None),
            P("fsdp", None),
            P("fsdp", None),
            P("fsdp", None),
            P("fsdp", None),
            P("fsdp", None, None),
            P("fsdp", None, None),
            P("fsdp", None, None),
            P(),
            P(),
            P(),
            P(),
        ),
        check_vma=False,
    )
```

profile of v0, /device:TPU:0, one launch (start us, length us, event | category | flops | bytes accessed | tf_op | source)
XLA Modules:
  0.0 1823.3 jit_solution(10324505766547317549)
XLA Ops:
  13.1 44.3 %all-gather = bf16[32,64,32]{1,2,0:T(8,128)(2,1)S(1)} all-gather(bf16[1,64,32]{1,2,0:T(8,128)(2,1)} %bitcast.249), channel_id=1, replica_groups=mesh['fsdp'=32] {'fsdp'}, dimensions={0}, use_global_device_ids=true | all-gather | bytes 135168 | tf_op jit(solution)/shard_map/all_gather | solution.py:125
  58.9 9.0 reduce-window.11
  82.7 45.7 %all-gather.6.cloned.1.call-done = bf16[2048,512]{1,0:T(8,128)(2,1)} async-done(((bf16[64,512]{1,0:T(8,128)(2,1)}), bf16[2048,512]{1,0:T(8,128)(2,1)}) %all-gather.6.cloned.1.call-update) | async-done | bytes 2097168 | tf_op jit(solution)/shard_map/all_gather | solution.py:124
  133.8 111.2 %all-gather.10.cloned.1.call-done = bf16[2048,4096]{1,0:T(8,128)(2,1)} async-done(((bf16[64,4096]{1,0:T(8,128)(2,1)}), bf16[2048,4096]{1,0:T(8,128)(2,1)}) %all-gather.10.cloned.1.call-update) | async-done | bytes 16777232 | tf_op jit(solution)/shard_map/all_gather | solution.py:122
  245.0 14.5 multiply_reduce_fusion.2
  269.2 91.7 %all-gather.12.cloned.1.call-done = bf16[4096,2048]{1,0:T(8,128)(2,1)} async-done(((bf16[128,2048]{1,0:T(8,128)(2,1)}), bf16[4096,2048]{1,0:T(8,128)(2,1)}) %all-gather.12.cloned.1.call-update) | async-done | bytes 16777232 | tf_op jit(solution)/shard_map/all_gather | solution.py:126
  360.8 8.8 multiply_reduce_fusion.5
  376.5 13.6 gather_fusion.2
  395.7 11.9 gather_fusion
  407.7 102.9 %all-to-all-done.2 = bf16[32,40,2048]{2,1,0:T(8,128)(2,1)} async-done(((bf16[32,40,2048]{2,1,0:T(8,128)(2,1)}), bf16[32,40,2048]{2,1,0:T(8,128)(2,1)}, u32[]{:S(2)}, u32[]{:S(2)}) %all-to-all-start.2) | async-done | bytes 5242912 | tf_op jit(solution)/shard_map/all_to_all | solution.py:223
  514.6 9.7 fusion.11
  524.3 107.0 %all-to-all-done = bf16[32,40,2048]{2,1,0:T(8,128)(2,1)} async-done(((bf16[32,40,2048]{2,1,0:T(8,128)(2,1)}), bf16[32,40,2048]{2,1,0:T(8,128)(2,1)}, u32[]{:S(2)}, u32[]{:S(2)}) %all-to-all-start) | async-done | bytes 5242912 | tf_op jit(solution)/shard_map/all_to_all | solution.py:187
  631.3 7.3 fusion.15
  638.6 10.1 fusion.30
  653.1 8.1 add_convert_fusion
  665.1 7.5 convolution_convert_fusion.1
  672.6 109.2 %all-to-all-done.3 = bf16[32,40,2048]{2,1,0:T(8,128)(2,1)} async-done(((bf16[32,40,2048]{2,1,0:T(8,128)(2,1)}), bf16[32,40,2048]{2,1,0:T(8,128)(2,1)}, u32[]{:S(2)}, u32[]{:S(2)}) %all-to-all-start.3) | async-done | bytes 5242912 | tf_op jit(solution)/shard_map/all_to_all | solution.py:253
  787.2 12.0 gather_fusion.3
  805.3 96.9 %all-to-all-done.1 = bf16[32,40,2048]{2,1,0:T(8,128)(2,1)} async-done(((bf16[32,40,2048]{2,1,0:T(8,128)(2,1)}), bf16[32,40,2048]{2,1,0:T(8,128)(2,1)}, u32[]{:S(2)}, u32[]{:S(2)}) %all-to-all-start.1) | async-done | bytes 5242912 | tf_op jit(solution)/shard_map/all_to_all | solution.py:204
  902.2 12.1 gather_fusion.1
  914.3 6.3 fusion.1
  927.7 11.5 fusion.34
  955.8 13.4 fusion.77
  969.2 29.0 %pad_maximum_fusion = f32[2048,5152]{1,0:T(8,128)} fusion(f32[2048,32]{1,0:T(8,128)S(1)} %copy-done.23, f32[2048,512]{1,0:T(8,128)} %fusion.73, f32[2048,512]{1,0:T(8,128)} %fusion.75, f32[2048,4096]{1,0:T(8,128)} %fusion.77), kind=kLoop, calls=%fused_computation.5 | loop fusion | flops 31653888 | bytes 84410368 | tf_op jit(solution)/shard_map/concatenate | solution.py:340
  999.8 14.1 fusion.49
  1013.9 10.4 convolution_bitcast_fusion.2
  1024.4 8.8 convolution_bitcast_fusion.1
  1033.2 9.0 convolution_bitcast_fusion
  1042.2 11.7 fusion.93
  1058.5 42.5 %all-reduce.6 = (f32[2048]{0:T(1024)}, f32[2048]{0:T(1024)}, f32[128]{0:T(128)}, f32[128]{0:T(128)}) all-reduce(f32[2048]{0:T(1024)S(1)} %get-tuple-element.118, f32[2048]{0:T(1024)S(1)} %copy-done.54, f32[128]{0:T(128)S(1)} %get-tuple-element.114, f32[128]{0:T(128)S(1)} %get-tuple-element.120), channel_id=1, replica_groups=mesh['fsdp'=32] {'fsdp'}, use_global_device_ids=true, to_apply=%region_33.34 | all-reduce | flops 4352 | bytes 34816 | tf_op jit(solution)/shard_map/psum | solution.py:347
  1104.1 347.3 %reduce-scatter.3.cloned.1.call-done = f32[64,5152]{1,0:T(8,128)} async-done(((f32[2048,5152]{1,0:T(8,128)}), f32[64,5152]{1,0:T(8,128)}) %reduce-scatter.3.cloned.1.call-update) | async-done | bytes 1318928 | tf_op jit(solution)/shard_map/reduce_scatter | solution.py:339
  1456.8 359.4 %reduce-scatter.5.cloned.1.call-done = f32[128,2048]{1,0:T(8,128)} async-done(((f32[4096,2048]{1,0:T(8,128)}), f32[128,2048]{1,0:T(8,128)}) %reduce-scatter.5.cloned.1.call-update) | async-done | bytes 1048592 | tf_op jit(solution)/shard_map/reduce_scatter | solution.py:79
  (265 shorter events, 111.0 us)
Async XLA Ops:
  7.2 631.4 %copy-start = (bf16[1,2048,768]{2,1,0:T(8,128)(2,1)S(1)}, bf16[1,2048,768]{2,1,0:T(8,128)(2,1)}, u32[]{:S(2)}) copy-start(bf16[1,2048,768]{2,1,0:T(8,128)(2,1)} %param.25) | copy-start | bytes 9437188
  7.2 51.3 %copy-start.47 = (s32[128,8]{0,1:T(8,128)S(1)}, s32[128,8]{0,1:T(8,128)}, u32[]{:S(2)}) copy-start(s32[128,8]{0,1:T(8,128)} %param.19) | copy-start | bytes 12292
  7.2 51.5 %copy-start.65 = (s32[1,4]{1,0:T(1,128)S(1)}, s32[1,4]{1,0:T(1,128)}, u32[]{:S(2)}) copy-start(s32[1,4]{1,0:T(1,128)} %param.18) | copy-start | bytes 52
  7.2 69.5 %all-gather.8.cloned.1.call-start = ((), (), s32[]{:S(2)}) async-start(), calls=%async_computation.7 | async-start | bytes 2162688 | tf_op jit(solution)/shard_map/all_gather | solution.py:123
  8.0 120.5 %all-gather.6.cloned.1.call-start = ((), (), s32[]{:S(2)}) async-start(), calls=%async_computation.6 | async-start | bytes 2162688 | tf_op jit(solution)/shard_map/all_gather | solution.py:124
  8.7 68.0 %copy-start.36 = (f32[2048]{0:T(1024)S(1)}, f32[2048]{0:T(1024)}, u32[]{:S(2)}) copy-start(f32[2048]{0:T(1024)} %param.28) | copy-start | bytes 24580
  8.7 236.3 %all-gather.10.cloned.1.call-start = ((), (), s32[]{:S(2)}) async-start(), calls=%async_computation.8 | async-start | bytes 17301504 | tf_op jit(solution)/shard_map/all_gather | solution.py:122
  9.4 351.4 %all-gather.12.cloned.1.call-start = ((), (), s32[]{:S(2)}) async-start(), calls=%async_computation.9 | async-start | bytes 17301504 | tf_op jit(solution)/shard_map/all_gather | solution.py:126
  68.4 11.3 copy-start.56
  76.0 169.1 %copy-start.50 = (f32[128]{0:T(128)}, f32[128]{0:T(128)S(1)}, u32[]{:S(2)}) copy-start(f32[128]{0:T(128)S(1)} %fusion.70) | copy-start | bytes 1540
  80.8 178.7 %copy-start.21 = (f32[128,4,128]{0,2,1:T(8,128)}, f32[128,4,128]{0,2,1:T(8,128)S(1)}, u32[]{:S(2)}) copy-start(f32[128,4,128]{0,2,1:T(8,128)S(1)} %copy.235) | copy-start | bytes 786436
  133.8 130.7 %copy-start.26 = (bf16[128,4,128,1]{0,2,3,1:T(8,128)(2,1)}, bf16[128,4,128,1]{0,2,3,1:T(8,128)(2,1)S(1)}, u32[]{:S(2)}) copy-start(bf16[128,4,128,1]{0,2,3,1:T(8,128)(2,1)S(1)} %fusion.53) | copy-start | bytes 393220
  360.8 9.8 copy-start.45
  360.8 10.8 copy-start.28
  390.1 120.5 %all-to-all-start.2 = ((bf16[32,40,2048]{2,1,0:T(8,128)(2,1)}), bf16[32,40,2048]{2,1,0:T(8,128)(2,1)}, u32[]{:S(2)}, u32[]{:S(2)}) async-start(bf16[32,40,2048]{2,1,0:T(8,128)(2,1)} %bitcast.228), calls=%async_computation.2 | async-start | bytes 10485760 | tf_op jit(solution)/shard_map/all_to_all | solution.py:223
  510.6 120.7 %all-to-all-start = ((bf16[32,40,2048]{2,1,0:T(8,128)(2,1)}), bf16[32,40,2048]{2,1,0:T(8,128)(2,1)}, u32[]{:S(2)}, u32[]{:S(2)}) async-start(bf16[32,40,2048]{2,1,0:T(8,128)(2,1)} %bitcast.229), calls=%async_computation | async-start | bytes 10485760 | tf_op jit(solution)/shard_map/all_to_all | solution.py:187
  661.2 120.7 %all-to-all-start.3 = ((bf16[32,40,2048]{2,1,0:T(8,128)(2,1)}), bf16[32,40,2048]{2,1,0:T(8,128)(2,1)}, u32[]{:S(2)}, u32[]{:S(2)}) async-start(bf16[32,40,2048]{2,1,0:T(8,128)(2,1)} %add_convert_fusion), calls=%async_computation.3 | async-start | bytes 10485760 | tf_op jit(solution)/shard_map/all_to_all | solution.py:253
  672.6 112.9 %copy-start.57 = (s32[1024,1]{0,1:T(1,128)S(1)}, s32[1024,1]{0,1:T(1,128)}, u32[]{:S(2)}) copy-start(s32[1024,1]{0,1:T(1,128)} %copy-done.56) | copy-start | bytes 12292
  672.6 112.9 %copy-start.13 = (bf16[4,8,128,128]{2,3,1,0:T(8,128)(2,1)S(1)}, bf16[4,8,128,128]{2,3,1,0:T(8,128)(2,1)}, u32[]{:S(2)}) copy-start(bf16[4,8,128,128]{2,3,1,0:T(8,128)(2,1)} %copy-done.12) | copy-start | bytes 3145732
  781.9 120.4 %all-to-all-start.1 = ((bf16[32,40,2048]{2,1,0:T(8,128)(2,1)}), bf16[32,40,2048]{2,1,0:T(8,128)(2,1)}, u32[]{:S(2)}, u32[]{:S(2)}) async-start(bf16[32,40,2048]{2,1,0:T(8,128)(2,1)} %convolution_convert_fusion.1), calls=%async_computation.1 | async-start | bytes 10485760 | tf_op jit(solution)/shard_map/all_to_all | solution.py:204
  785.5 666.0 %reduce-scatter.3.cloned.1.call-start = ((), (), s32[]{:S(2)}) async-start(), calls=%async_computation.10 | async-start | bytes 44335104 | tf_op jit(solution)/shard_map/reduce_scatter | solution.py:339
  902.2 12.1 copy-start.16
  914.3 7.9 copy-start.8
  927.7 11.7 copy-start.30
  927.7 11.7 copy-start.41
  955.8 13.4 copy-start.23
  998.3 818.0 %reduce-scatter.5.cloned.1.call-start = ((), (), s32[]{:S(2)}) async-start(), calls=%async_computation.11 | async-start | bytes 34603008 | tf_op jit(solution)/shard_map/reduce_scatter | solution.py:79
  1013.9 10.4 copy-start.67
  1024.4 8.8 copy-start.66
  1033.2 9.0 copy-start.15
  1056.5 44.4 %copy-start.62 = (f32[128]{0:T(128)S(1)}, f32[128]{0:T(128)}, u32[]{:S(2)}) copy-start(f32[128]{0:T(128)} %copy-done.61) | copy-start | bytes 1540
  1100.9 715.3 %copy-start.1 = (bf16[1,2048,768]{2,1,0:T(8,128)(2,1)S(1)}, bf16[1,2048,768]{2,1,0:T(8,128)(2,1)}, u32[]{:S(2)}) copy-start(bf16[1,2048,768]{2,1,0:T(8,128)(2,1)} %param.25) | copy-start | bytes 9437188
  (48 other events, 95.7 us)
Sparse Core Ops, SparseCore 0:
  10.9 59.3 all-gather.7
  73.1 55.2 all-gather.5
  131.3 113.7 all-gather.9
  247.8 113.0 all-gather.11
  998.4 452.9 reduce-scatter.2
  1454.1 362.0 reduce-scatter.4
where the time goes:
time: 1830 us; the launch traced here: 1820 us
  waiting for transfers between devices  1370 us (75%)
  matrix products  172 us (9%)
  blocking collectives  86.8 us (5%)
  local copies, waits for them, and re-layouts  84.2 us (5%)
  other arithmetic  75.6 us (4%)
    reduce_scatter x1, waiting for transfers between devices, projection_sums(): lax.psum_scatter(lax.dot_general(context_low, grad_attn_low, CONTRACT_ROW...  359 us
    reduce_scatter x1, waiting for transfers between devices, body(): lax.psum_scatter(jnp.concatenate(parts, axis=1), 'fsdp', scatter_dimensio...  347 us
    all_gather x1, waiting for transfers between devices, body(): lax.all_gather(query_weight, 'fsdp', axis=0, tiled=True)  111 us
    all_to_all x1, waiting for transfers between devices, body(): lax.all_to_all(grad_rows.reshape(shards, local_experts * capacity, model)...  109 us
    all_to_all x1, waiting for transfers between devices, body(): lax.all_to_all(source_rows.reshape(shards, local_experts * capacity, mode...  107 us
    all_to_all x1, waiting for transfers between devices, body(): lax.all_to_all(grad_slots.reshape(shards, local_experts * capacity, model...  103 us
    all_to_all x1, waiting for transfers between devices, body(): lax.all_to_all(result_low.reshape(shards, local_experts * capacity, model...  96.9 us
    all_gather x1, waiting for transfers between devices, body(): lax.all_gather(out_weight, 'fsdp', axis=0, tiled=True)  91.7 us
  transfers between devices with their start and end apart: 10, of which 9 were waited for; matrix products, arithmetic and copies ran while one was open for 9% of the time, Pallas kernels for 0%

commit v1 on v0

v1 whole, which is shorter than its diff:
```python
import functools

import jax
import jax.numpy as jnp
from jax import lax
from jax.sharding import PartitionSpec as P

EPS = 1e-06
THETA = 1000000.0
NEGATIVE = -1e30
CORES = 2
LANES = 128
CONTRACT_ROWS = (((0,), (0,)), ((), ()))
CONTRACT_LAST = (((1,), (1,)), ((), ()))


def root_mean_square_norm(value_rows, gain):
    return (
        value_rows
        * lax.rsqrt(jnp.mean(value_rows * value_rows, axis=-1, keepdims=True) + EPS)
        * gain
    )


def sequence_layout(lengths, count_total):
    ends = jnp.cumsum(lengths)
    starts = ends - lengths
    places = jnp.arange(count_total, dtype=jnp.int32)
    member = ((places[:, None] >= starts[None, :]) & (places[:, None] < ends[None, :])).astype(
        jnp.int32
    )
    labels = jnp.arange(lengths.shape[0], dtype=jnp.int32)
    segment = jnp.sum(member * labels[None, :], axis=1)
    offset = jnp.sum(member * starts[None, :], axis=1)
    return (segment, places - offset)


def rotary_tables(position, width):
    half = width // 2
    inverse = jnp.power(THETA, -(jnp.arange(half, dtype=jnp.float32) * 2.0) / width)
    angle = position.astype(jnp.float32)[:, None] * inverse[None, :]
    angle = jnp.concatenate([angle, angle], axis=1)
    return (jnp.cos(angle), jnp.sin(angle))


def rotary_apply(value_rows, cosine_table, sine_table):
    half = value_rows.shape[-1] // 2
    turned = jnp.concatenate([-value_rows[..., half:], value_rows[..., :half]], axis=-1)
    return value_rows * cosine_table[:, None, :] + turned * sine_table[:, None, :]


def prepare(projected_query, projected_key, query_norm_gain, key_gain, cosine_table, sine_table):
    count_total = projected_query.shape[0]
    width = query_norm_gain.shape[0]
    query_rows = rotary_apply(
        root_mean_square_norm(projected_query.reshape(count_total, -1, width), query_norm_gain),
        cosine_table,
        sine_table,
    )
    key_rows = rotary_apply(
        root_mean_square_norm(projected_key.reshape(count_total, -1, width), key_gain),
        cosine_table,
        sine_table,
    )
    return (query_rows, key_rows)


def round_up(number, step):
    return -(-number // step) * step


def body(
    tokens,
    cotangent,
    lengths,
    routes,
    query_weight,
    key_matrix,
    value_matrix,
    out_weight,
    router_weight,
    expert_gate,
    expert_up,
    expert_down,
    first_gain,
    second_gain,
    query_norm_gain,
    key_gain,
):
    f32, bf16 = jnp.float32, jnp.bfloat16
    count, model = tokens.shape
    width = query_norm_gain.shape[0]
    heads = query_weight.shape[1] // width
    kv_heads = key_matrix.shape[1] // width
    head_group = heads // kv_heads
    choose = routes.shape[1]
    shards = lax.axis_size("fsdp")
    experts = shards * expert_gate.shape[0]
    capacity = max(2, count * choose * 5 // (4 * experts))
    scale = width ** (-0.5)

    chips = kv_heads
    plane = chips * CORES
    outer = shards // plane
    span = outer // chips
    me = lax.axis_index("fsdp")
    my_core = me % CORES
    my_outer = me // plane
    four = [
        [o * plane + m * CORES + c for m in range(chips)]
        for o in range(outer)
        for c in range(CORES)
    ]
    eight = [[o * plane + j for j in range(plane)] for o in range(outer)]

    def swap_core(value):
        return lax.ppermute(value, "fsdp", [(i, i ^ 1) for i in range(shards)])

    def swap_chip(value, r):
        return lax.ppermute(value, "fsdp", [(i, i ^ (r * CORES)) for i in range(shards)])

    def shift_outer(value, s):
        return lax.ppermute(
            value,
            "fsdp",
            [(i, ((i // plane + s) % outer) * plane + i % plane) for i in range(shards)],
        )

    def exchange(value, groups):
        return lax.all_to_all(
            value, "fsdp", split_axis=0, concat_axis=0, tiled=True, axis_index_groups=groups
        )

    def gather_chips(value):
        return [value] + [swap_chip(value, r) for r in range(1, chips)]

    def gather_outer(value):
        return [value] + [shift_outer(value, s) for s in range(1, outer)]

    def ring_outer(value):
        pieces = [value]
        for _ in range(1, outer):
            pieces.append(shift_outer(pieces[-1], 1))
        return pieces

    def scatter_outer(value):
        total = lax.dynamic_index_in_dim(value, my_outer, 0, keepdims=False).astype(f32)
        for s in range(1, outer):
            part = lax.dynamic_index_in_dim(value, (my_outer + s) % outer, 0, keepdims=False)
            total = total + shift_outer(part, s).astype(f32)
        return total

    def sum_everywhere(value):
        value = value + swap_core(value)
        value = sum([swap_chip(value, r) for r in range(1, chips)], value)
        return sum([shift_outer(value, s) for s in range(1, outer)], value)

    depth = query_weight.shape[0]
    group_columns = head_group * width
    columns = group_columns + 2 * width
    cut = jnp.concatenate(
        [
            query_weight.reshape(depth, chips, group_columns),
            key_matrix.reshape(depth, chips, width),
            value_matrix.reshape(depth, chips, width),
        ],
        axis=2,
    ).transpose(1, 0, 2)
    cut = exchange(cut, four)
    full_front = jnp.zeros((outer, chips, CORES, depth, columns), bf16)
    for s, piece in enumerate(gather_outer(cut)):
        place = (my_outer - s) % outer
        other = swap_core(piece)
        full_front = lax.dynamic_update_slice(
            full_front, piece[None, :, None], (place, 0, my_core, 0, 0)
        )
        full_front = lax.dynamic_update_slice(
            full_front, other[None, :, None], (place, 0, 1 - my_core, 0, 0)
        )
    full_front = full_front.reshape(model, columns)

    rows_out = out_weight.shape[0]
    stacked = jnp.zeros((outer, rows_out, model), bf16)
    for s, piece in enumerate(gather_outer(out_weight)):
        stacked = lax.dynamic_update_slice(stacked, piece[None], ((my_outer - s) % outer, 0, 0))
    mine = exchange(stacked.reshape(chips, span * rows_out, model), four)
    mine = mine.reshape(chips, span, rows_out, model)
    other = swap_core(mine)
    full_out = jnp.where(
        my_core == 0, jnp.stack([mine, other], axis=1), jnp.stack([other, mine], axis=1)
    )
    full_out = full_out.transpose(2, 0, 1, 3, 4).reshape(group_columns, model)
    full_router = lax.all_gather(router_weight, "fsdp", axis=0, tiled=True)

    mask = jnp.sum(
        (routes[:, :, None] == jnp.arange(experts, dtype=jnp.int32)[None, None, :]).astype(f32),
        axis=1,
    )
    mask_width = round_up(experts, LANES)
    cotangent_wide = jnp.concatenate(
        [cotangent, jnp.pad(mask.astype(bf16), ((0, 0), (0, mask_width - experts)))], axis=1
    )
    earlier = jnp.tril(jnp.ones((count, count), bf16), -1)
    picks, cotangent_rows = [], []
    for piece in gather_outer(cotangent_wide):
        piece_mask = piece[:, model : model + experts]
        rank = jnp.dot(earlier, piece_mask, preferred_element_type=f32)
        local_mask = lax.dynamic_slice_in_dim(piece_mask, my_outer * plane, plane, axis=1)
        local_rank = lax.dynamic_slice_in_dim(rank, my_outer * plane, plane, axis=1)
        pick = (
            (local_rank.T[:, None, :] == jnp.arange(capacity, dtype=f32)[None, :, None])
            & (local_mask.T[:, None, :] > 0)
        ).astype(bf16)
        pick = pick.reshape(plane * capacity, count)
        picks.append(pick)
        sent = jnp.dot(pick, piece[:, :model], preferred_element_type=f32).astype(bf16)
        sent = exchange(sent.reshape(plane, capacity, model), eight)
        cotangent_rows.append(sent.reshape(plane * capacity, model))

    inputs = tokens.astype(f32)
    token_parts = gather_chips(tokens)
    length_parts = gather_chips(lengths)
    normed_low = jnp.concatenate(
        [root_mean_square_norm(part.astype(f32), first_gain).astype(bf16) for part in token_parts],
        axis=0,
    )
    together = chips * count
    projected = jnp.dot(normed_low, full_front, preferred_element_type=f32)
    value_low = projected[:, group_columns + width :].astype(bf16).reshape(chips, count, width)
    layouts = [sequence_layout(part[0], count) for part in length_parts]
    segment = jnp.stack([layout[0] for layout in layouts])
    position = jnp.concatenate([layout[1] for layout in layouts])
    cosine_table, sine_table = rotary_tables(position, width)
    rotated, prepare_back = jax.vjp(
        functools.partial(prepare, cosine_table=cosine_table, sine_table=sine_table),
        projected[:, :group_columns],
        projected[:, group_columns : group_columns + width],
        query_norm_gain,
        key_gain,
    )
    query_low = rotated[0].astype(bf16).reshape(chips, count, head_group, width)
    key_low = rotated[1].astype(bf16).reshape(chips, count, width)
    places = jnp.arange(count, dtype=jnp.int32)
    allowed = (segment[:, :, None] == segment[:, None, :]) & (
        places[None, None, :] <= places[None, :, None]
    )
    allowed = allowed[:, None]

    def score_table():
        raw = jnp.einsum("bigc,bjc->bgij", query_low, key_low, preferred_element_type=f32) * scale
        return jnp.where(allowed, raw, NEGATIVE)

    scores = score_table()
    peak = jnp.max(scores, axis=-1, keepdims=True)
    log_total = peak + jnp.log(jnp.sum(jnp.exp(scores - peak), axis=-1, keepdims=True))
    shares_low = jnp.exp(scores - log_total).astype(bf16)
    context_low = (
        jnp.einsum("bgij,bjc->bigc", shares_low, value_low, preferred_element_type=f32)
        .reshape(together, group_columns)
        .astype(bf16)
    )
    attended = jnp.dot(context_low, full_out, preferred_element_type=f32)
    attended = attended.reshape(chips, count, model)
    hidden = inputs + attended[0]
    for r in range(1, chips):
        hidden = hidden + swap_chip(attended[r].astype(bf16), r).astype(f32)

    second_low = root_mean_square_norm(hidden, second_gain).astype(bf16)
    logits = jnp.dot(second_low, full_router, preferred_element_type=f32)
    exponent = jnp.exp(logits - jnp.max(logits, axis=-1, keepdims=True))
    prob = exponent / jnp.sum(exponent, axis=-1, keepdims=True)
    chosen = prob * mask
    chosen_sum = jnp.sum(chosen, axis=-1, keepdims=True)
    gates = chosen / chosen_sum

    def two_parts(value):
        high = value.astype(bf16)
        low = (value - high.astype(f32)).astype(bf16)
        return high, low

    pair_width = round_up(2 * experts, LANES)
    pair_pad = jnp.zeros((count, pair_width - 2 * experts), bf16)
    second_wide = jnp.concatenate([second_low, *two_parts(gates), pair_pad], axis=1)

    slots = plane * capacity
    gate_weight, up_weight, down_weight = expert_gate[0], expert_up[0], expert_down[0]
    pair_column = jnp.arange(pair_width, dtype=jnp.int32)[None, :]
    high_column = (pair_column == me).astype(f32)
    low_column = (pair_column == me + experts).astype(f32)
    received, units_list, gate_grads, up_grads = [], [], [], []
    moved_sum, grad_sum = None, None
    for s, piece in enumerate(ring_outer(second_wide)):
        sent = jnp.dot(picks[s], piece, preferred_element_type=f32).astype(bf16)
        wide = exchange(sent.reshape(plane, capacity, -1), eight).reshape(slots, -1)
        rows = wide[:, :model]
        row_gate = jnp.sum(
            wide[:, model:].astype(f32) * (high_column + low_column), axis=1, keepdims=True
        )
        gate_part = jnp.dot(rows, gate_weight, preferred_element_type=f32)
        up_part = jnp.dot(rows, up_weight, preferred_element_type=f32)
        grad_units_raw = lax.dot_general(
            cotangent_rows[s], down_weight, CONTRACT_LAST, preferred_element_type=f32
        )
        sig = jax.nn.sigmoid(gate_part)
        silu = gate_part * sig
        units = silu * up_part
        gate_change = jnp.sum(units * grad_units_raw, axis=1, keepdims=True)
        gated_units = (row_gate * units).astype(bf16)
        grad_units = row_gate * grad_units_raw
        grad_gate_low = (grad_units * up_part * sig * (1.0 + gate_part * (1.0 - sig))).astype(bf16)
        grad_up_low = (grad_units * silu).astype(bf16)
        grad_rows = lax.dot_general(
            grad_gate_low, gate_weight, CONTRACT_LAST, preferred_element_type=f32
        ) + lax.dot_general(grad_up_low, up_weight, CONTRACT_LAST, preferred_element_type=f32)
        change_high, change_low = two_parts(gate_change)
        change_wide = change_high.astype(f32) * high_column + change_low.astype(f32) * low_column
        back = jnp.concatenate([grad_rows.astype(bf16), change_wide.astype(bf16)], axis=1)
        back = exchange(back.reshape(plane, capacity, -1), eight).reshape(slots, -1)
        back = lax.dot_general(picks[s], back, CONTRACT_ROWS, preferred_element_type=f32)
        moved = jnp.dot(gated_units, down_weight, preferred_element_type=f32).astype(bf16)
        moved = exchange(moved.reshape(plane, capacity, -1), eight).reshape(slots, -1)
        moved = lax.dot_general(picks[s], moved, CONTRACT_ROWS, preferred_element_type=f32)
        if s == 0:
            grad_sum, moved_sum = back, moved
        else:
            grad_sum = grad_sum + shift_outer(back.astype(bf16), -s).astype(f32)
            moved_sum = moved_sum + shift_outer(moved.astype(bf16), -s).astype(f32)
        received.append(rows)
        units_list.append(gated_units)
        gate_grads.append(grad_gate_low)
        up_grads.append(grad_up_low)
    output = (hidden + moved_sum).astype(bf16)
    all_rows = jnp.concatenate(received, axis=0)
    all_cotangent = jnp.concatenate(cotangent_rows, axis=0)
    gate_grad = lax.dot_general(
        all_rows, jnp.concatenate(gate_grads, axis=0), CONTRACT_ROWS, preferred_element_type=f32
    )[None]
    up_grad = lax.dot_general(
        all_rows, jnp.concatenate(up_grads, axis=0), CONTRACT_ROWS, preferred_element_type=f32
    )[None]
    down_grad = lax.dot_general(
        jnp.concatenate(units_list, axis=0),
        all_cotangent,
        CONTRACT_ROWS,
        preferred_element_type=f32,
    )[None]

    pairs = grad_sum[:, model : model + 2 * experts]
    grad_gates = pairs[:, :experts] + pairs[:, experts:]
    grad_chosen = (
        mask * (grad_gates - jnp.sum(gates * grad_gates, axis=-1, keepdims=True)) / chosen_sum
    )
    grad_logits_low = (
        prob * (grad_chosen - jnp.sum(prob * grad_chosen, axis=-1, keepdims=True))
    ).astype(bf16)
    grad_second = grad_sum[:, :model] + lax.dot_general(
        grad_logits_low, full_router, CONTRACT_LAST, preferred_element_type=f32
    )
    router_grad = lax.psum_scatter(
        lax.dot_general(second_low, grad_logits_low, CONTRACT_ROWS, preferred_element_type=f32),
        "fsdp",
        scatter_dimension=0,
        tiled=True,
    )
    _, second_back = jax.vjp(root_mean_square_norm, hidden, second_gain)
    grad_hidden_part, second_gain_term = second_back(grad_second)
    grad_hidden = cotangent.astype(f32) + grad_hidden_part
    grad_attn_low = jnp.concatenate(gather_chips(grad_hidden.astype(bf16)), axis=0)

    grad_context_low = (
        lax.dot_general(grad_attn_low, full_out, CONTRACT_LAST, preferred_element_type=f32)
        .astype(bf16)
        .reshape(chips, count, head_group, width)
    )
    out_part = lax.dot_general(
        context_low, grad_attn_low, CONTRACT_ROWS, preferred_element_type=f32
    ).astype(bf16)
    out_part = out_part.reshape(span, chips, CORES, rows_out, model)
    out_keep = lax.dynamic_index_in_dim(out_part, my_core, 2, keepdims=False)
    out_send = lax.dynamic_index_in_dim(out_part, 1 - my_core, 2, keepdims=False)
    out_half = (out_keep.astype(f32) + swap_core(out_send).astype(f32)).astype(bf16)
    out_half = exchange(out_half.transpose(1, 0, 2, 3), four)
    out_grad = scatter_outer(out_half.reshape(outer, rows_out, model))

    shares = jnp.exp(score_table() - log_total)
    grad_shares = jnp.einsum(
        "bigc,bjc->bgij", grad_context_low, value_low, preferred_element_type=f32
    )
    grad_scores_low = (
        shares * (grad_shares - jnp.sum(shares * grad_shares, axis=-1, keepdims=True))
    ).astype(bf16)
    grad_rot_query = (
        jnp.einsum("bgij,bjc->bigc", grad_scores_low, key_low, preferred_element_type=f32) * scale
    ).reshape(together, head_group, width)
    grad_rot_key = (
        jnp.einsum("bgij,bigc->bjc", grad_scores_low, query_low, preferred_element_type=f32)
        * scale
    ).reshape(together, 1, width)
    grad_value_low = (
        jnp.einsum("bgij,bigc->bjc", shares_low, grad_context_low, preferred_element_type=f32)
        .astype(bf16)
        .reshape(together, width)
    )
    grad_proj_query, grad_proj_key, query_gain_term, key_gain_term = prepare_back(
        (grad_rot_query, grad_rot_key)
    )
    grad_front_low = jnp.concatenate(
        [grad_proj_query.astype(bf16), grad_proj_key.astype(bf16), grad_value_low], axis=1
    )
    front_part = lax.dot_general(
        normed_low, grad_front_low, CONTRACT_ROWS, preferred_element_type=f32
    ).astype(bf16)
    front_part = front_part.reshape(outer, chips, CORES, depth, columns)
    front_keep = lax.dynamic_index_in_dim(front_part, my_core, 2, keepdims=False)
    front_send = lax.dynamic_index_in_dim(front_part, 1 - my_core, 2, keepdims=False)
    front_half = (front_keep.astype(f32) + swap_core(front_send).astype(f32)).astype(bf16)
    front = exchange(scatter_outer(front_half).astype(bf16), four).astype(f32)
    query_grad = front[:, :, :group_columns].transpose(1, 0, 2).reshape(depth, -1)
    key_grad = (
        front[:, :, group_columns : group_columns + width].transpose(1, 0, 2).reshape(depth, -1)
    )
    value_grad = front[:, :, group_columns + width :].transpose(1, 0, 2).reshape(depth, -1)

    grad_normed_part = lax.dot_general(
        grad_front_low, full_front, CONTRACT_LAST, preferred_element_type=f32
    ).reshape(chips, count, model)
    grad_normed = grad_normed_part[0]
    for r in range(1, chips):
        grad_normed = grad_normed + swap_chip(grad_normed_part[r].astype(bf16), r).astype(f32)
    _, first_back = jax.vjp(root_mean_square_norm, inputs, first_gain)
    grad_input_part, first_gain_term = first_back(grad_normed)
    tokens_grad = grad_hidden + grad_input_part
    gain_sums = sum_everywhere(
        jnp.concatenate(
            [first_gain_term, second_gain_term, query_gain_term, key_gain_term]
        ).reshape(-1, LANES)
    ).reshape(-1)
    return (
        output,
        tokens_grad,
        query_grad,
        key_grad,
        value_grad,
        out_grad,
        router_grad,
        gate_grad,
        up_grad,
        down_grad,
        gain_sums[:model],
        gain_sums[model : 2 * model],
        gain_sums[2 * model : 2 * model + width],
        gain_sums[2 * model + width :],
    )


def solution(mesh):
    rows = P("fsdp", None)
    blocks = P("fsdp", None, None)
    placed = (rows,) * 9 + (blocks,) * 3 + (P(),) * 4
    return jax.shard_map(
        body,
        mesh=mesh,
        in_specs=placed,
        out_specs=(rows,) * 7 + (blocks,) * 3 + (P(),) * 4,
        check_vma=False,
    )
```

time: 1830 us -> 1060 us (0.58)
  waiting for transfers between devices: 1370 us -> 457 us
  starting transfers between devices: 15.5 us -> 162 us
  local copies, waits for them, and re-layouts: 84.2 us -> 106 us
  blocking collectives: 86.8 us -> 67 us
    reduce_scatter x2 -> x0, waiting for transfers between devices: 707 us -> none  [the longest x1 359 us: projection_sums(): lax.psum_scatter(lax.dot_general(context_low, grad_attn_low, CONTRACT_ROW...]
    all_to_all x4 -> x20, waiting for transfers between devices: 416 us -> 88.4 us  [exchange(): lax.all_to_all(value, 'fsdp', split_axis=0, concat_axis=0, tiled=True, ax...]
    ppermute x0 -> x53, waiting for transfers between devices: none -> 259 us  [the longest x27 224 us: shift_outer(): lax.ppermute(value, 'fsdp', [(i, (i // plane + s) % outer * plane + i % p...]
    all_gather x4 -> x0, waiting for transfers between devices: 249 us -> none  [the longest x1 111 us: body(): lax.all_gather(query_weight, 'fsdp', axis=0, tiled=True)]
    unnamed x6 -> x2, waiting for transfers between devices: 2.61 us -> 109 us
    ppermute x0 -> x53, starting transfers between devices: none -> 76.3 us  [the longest x27 55 us: shift_outer(): lax.ppermute(value, 'fsdp', [(i, (i // plane + s) % outer * plane + i % p...]
    all_to_all x4 -> x20, starting transfers between devices: 15.2 us -> 86.1 us  [exchange(): lax.all_to_all(value, 'fsdp', split_axis=0, concat_axis=0, tiled=True, ax...]
    gather x4 -> x0, local copies, waits for them, and re-layouts: 49.5 us -> none  [the longest x1 13.6 us: body(): jnp.concatenate([grad_result, jnp.zeros((1, model), jnp.bfloat16)], axis=0)]
  transfers between devices with their start and end apart: 10 -> 74, of which waited for: 9 -> 34; matrix products, arithmetic and copies ran while one was open for 9% -> 27% of each run, Pallas kernels for 0% -> 0%
where the time goes in v1:
time: 1060 us; the launch traced here: 1050 us
  waiting for transfers between devices  457 us (43%)
  matrix products  168 us (16%)
  starting transfers between devices  162 us (15%)
  local copies, waits for them, and re-layouts  106 us (10%)
  other arithmetic  75.1 us (7%)
  blocking collectives  67 us (6%)
  between operations  16.4 us (2%)
    ppermute x27, waiting for transfers between devices, shift_outer(): lax.ppermute(value, 'fsdp', [(i, (i // plane + s) % outer * plane + i % p...  224 us
    unnamed x2, waiting for transfers between devices  109 us
    all_to_all x20, waiting for transfers between devices, exchange(): lax.all_to_all(value, 'fsdp', split_axis=0, concat_axis=0, tiled=True, ax...  88.4 us
    all_to_all x20, starting transfers between devices, exchange(): lax.all_to_all(value, 'fsdp', split_axis=0, concat_axis=0, tiled=True, ax...  86.1 us
    all_gather x1, blocking collectives, body(): full_router = lax.all_gather(router_weight, 'fsdp', axis=0, tiled=True)  67 us
    ppermute x27, starting transfers between devices, shift_outer(): lax.ppermute(value, 'fsdp', [(i, (i // plane + s) % outer * plane + i % p...  55 us
    ppermute x18, waiting for transfers between devices, swap_chip(): lax.ppermute(value, 'fsdp', [(i, i ^ r * CORES) for i in range(shards)])  35.2 us
    unnamed x304, local copies, waits for them, and re-layouts  27.3 us
  transfers between devices with their start and end apart: 74, of which 34 were waited for; matrix products, arithmetic and copies ran while one was open for 27% of the time, Pallas kernels for 0%

profile of v1, /device:TPU:0, one launch (start us, length us, event | category | flops | bytes accessed | tf_op | source)
XLA Modules:
  0.0 1052.4 jit_solution(1528202970335745864)
XLA Ops:
  34.2 11.4 %collective-permute-done.12 = s32[1,4]{1,0:T(1,128)S(1)} collective-permute-done((s32[1,4]{1,0:T(1,128)S(1)}, s32[1,4]{1,0:T(1,128)S(1)}, u32[]{:S(2)}, u32[]{:S(2)}) %collective-permute-start.12) | collective-permute-done | bytes 48 | tf_op jit(solution)/shard_map/ppermute | solution.py:120
  86.4 27.6 %collective-permute-done.6 = bf16[4,64,1280]{2,1,0:T(8,128)(2,1)S(1)} collective-permute-done((bf16[4,64,1280]{2,1,0:T(8,128)(2,1)}, bf16[4,64,1280]{2,1,0:T(8,128)(2,1)S(1)}, u32[]{:S(2)}, u32[]{:S(2)}) %collective-permute-start.6) | collective-permute-done | bytes 655392 | tf_op jit(solution)/shard_map/ppermute | solution.py:123
  123.0 5.5 fusion.185
  177.8 67.0 %all-gather = bf16[32,64,32]{1,2,0:T(8,128)(2,1)S(1)} all-gather(bf16[1,64,32]{1,2,0:T(8,128)(2,1)S(1)} %bitcast.526), channel_id=1, replica_groups=mesh['fsdp'=32] {'fsdp'}, dimensions={0}, use_global_device_ids=true | all-gather | bytes 135168 | tf_op jit(solution)/shard_map/all_gather | solution.py:193
  258.7 25.2 %collective-permute-done.26 = bf16[128,2176]{0,1:T(8,128)(2,1)S(1)} collective-permute-done((bf16[128,2176]{0,1:T(8,128)(2,1)S(1)}, bf16[128,2176]{0,1:T(8,128)(2,1)S(1)}, u32[]{:S(2)}, u32[]{:S(2)}) %collective-permute-start.26) | collective-permute-done | bytes 557088 | tf_op jit(solution)/shard_map/ppermute | solution.py:123
  284.4 17.9 %collective-permute-done.23 = bf16[128,2176]{0,1:T(8,128)(2,1)S(1)} collective-permute-done((bf16[128,2176]{0,1:T(8,128)(2,1)S(1)}, bf16[128,2176]{0,1:T(8,128)(2,1)S(1)}, u32[]{:S(2)}, u32[]{:S(2)}) %collective-permute-start.23) | collective-permute-done | bytes 557088 | tf_op jit(solution)/shard_map/ppermute | solution.py:123
  312.0 15.6 %all-to-all-done.16 = bf16[8,40,2048]{2,1,0:T(8,128)(2,1)} async-done(((bf16[8,40,2048]{2,1,0:T(8,128)(2,1)}), bf16[8,40,2048]{2,1,0:T(8,128)(2,1)}, u32[]{:S(2)}, u32[]{:S(2)}) %all-to-all-start.16) | async-done | bytes 1310752 | tf_op jit(solution)/shard_map/all_to_all | solution.py:130
  334.5 15.6 %all-to-all-done.14 = bf16[8,40,2048]{2,1,0:T(8,128)(2,1)} async-done(((bf16[8,40,2048]{2,1,0:T(8,128)(2,1)}), bf16[8,40,2048]{2,1,0:T(8,128)(2,1)}, u32[]{:S(2)}, u32[]{:S(2)}) %all-to-all-start.14) | async-done | bytes 1310752 | tf_op jit(solution)/shard_map/all_to_all | solution.py:130
  357.0 15.6 %all-to-all-done.12 = bf16[8,40,2048]{2,1,0:T(8,128)(2,1)} async-done(((bf16[8,40,2048]{2,1,0:T(8,128)(2,1)}), bf16[8,40,2048]{2,1,0:T(8,128)(2,1)}, u32[]{:S(2)}, u32[]{:S(2)}) %all-to-all-start.12) | async-done | bytes 1310752 | tf_op jit(solution)/shard_map/all_to_all | solution.py:130
  381.1 14.0 %all-to-all-done.10 = bf16[8,40,2048]{2,1,0:T(8,128)(2,1)} async-done(((bf16[8,40,2048]{2,1,0:T(8,128)(2,1)}), bf16[8,40,2048]{2,1,0:T(8,128)(2,1)}, u32[]{:S(2)}, u32[]{:S(2)}) %all-to-all-start.10) | async-done | bytes 1310752 | tf_op jit(solution)/shard_map/all_to_all | solution.py:130
  404.8 15.9 %collective-permute-done.21 = bf16[128,2176]{0,1:T(8,128)(2,1)S(1)} collective-permute-done((bf16[128,2176]{0,1:T(8,128)(2,1)S(1)}, bf16[128,2176]{0,1:T(8,128)(2,1)S(1)}, u32[]{:S(2)}, u32[]{:S(2)}) %collective-permute-start.21) | collective-permute-done | bytes 557088 | tf_op jit(solution)/shard_map/ppermute | solution.py:123
  428.3 17.0 %collective-permute-done.24 = bf16[128,2176]{0,1:T(8,128)(2,1)} collective-permute-done((bf16[128,2176]{0,1:T(8,128)(2,1)}, bf16[128,2176]{0,1:T(8,128)(2,1)}, u32[]{:S(2)}, u32[]{:S(2)}) %collective-permute-start.24) | collective-permute-done | bytes 557088 | tf_op jit(solution)/shard_map/ppermute | solution.py:123
  464.1 4.6 fusion.16
  552.8 7.0 convolution_bitcast_fusion.1
  564.1 8.4 convolution_bitcast_fusion
  572.5 10.7 %all-to-all-done.15 = bf16[8,40,2176]{2,1,0:T(8,128)(2,1)S(1)} async-done(((bf16[8,40,2176]{2,1,0:T(8,128)(2,1)}), bf16[8,40,2176]{2,1,0:T(8,128)(2,1)S(1)}, u32[]{:S(2)}, u32[]{:S(2)}) %all-to-all-start.15) | async-done | bytes 1392672 | tf_op jit(solution)/shard_map/all_to_all | solution.py:130
  586.8 8.5 fusion.10
  598.2 7.6 all-to-all-done.13
  621.9 7.4 all-to-all-done.11
  633.7 6.8 collective-permute-done.30
  663.4 10.8 %collective-permute-done.33 = bf16[128,2048]{0,1:T(8,128)(2,1)S(1)} collective-permute-done((bf16[128,2048]{0,1:T(8,128)(2,1)}, bf16[128,2048]{0,1:T(8,128)(2,1)S(1)}, u32[]{:S(2)}, u32[]{:S(2)}) %collective-permute-start.33) | collective-permute-done | bytes 524320 | tf_op jit(solution)/shard_map/ppermute | solution.py:120
  675.8 4.7 fusion.134
  705.2 7.1 fusion.329
  713.5 4.9 all-to-all-start.5
  748.5 10.6 %collective-permute-start.28 = (bf16[128,2048]{0,1:T(8,128)(2,1)}, bf16[128,2048]{0,1:T(8,128)(2,1)S(1)}, u32[]{:S(2)}, u32[]{:S(2)}) collective-permute-start(bf16[128,2048]{0,1:T(8,128)(2,1)} %fusion.102), channel_id=1, source_target_pairs={{0,8},{1,9},{2,10},{3,11},{4,12},{5,13},{6,14},{7,15},{8,16},{9,17... | collective-permute-start | bytes 1572872 | tf_op jit(solution)/shard_map/ppermute | solution.py:123
  759.1 9.3 collective-permute-start.25
  776.6 17.4 %collective-permute-done.25 = bf16[128,2048]{0,1:T(8,128)(2,1)S(1)} collective-permute-done((bf16[128,2048]{0,1:T(8,128)(2,1)}, bf16[128,2048]{0,1:T(8,128)(2,1)S(1)}, u32[]{:S(2)}, u32[]{:S(2)}) %collective-permute-start.25) | collective-permute-done | bytes 524320 | tf_op jit(solution)/shard_map/ppermute | solution.py:123
  797.2 109.2 %reduce-scatter.4.cloned.1.call-done = f32[64,32]{1,0:T(8,128)} async-done(((f32[2048,32]{1,0:T(8,128)}), f32[64,32]{1,0:T(8,128)}) %reduce-scatter.4.cloned.1.call-update) | async-done | bytes 8208
  938.7 8.0 collective-permute-done.41
  946.7 39.6 %collective-permute-done.40 = bf16[4,64,1280]{2,1,0:T(8,128)(2,1)} collective-permute-done((bf16[4,64,1280]{2,1,0:T(8,128)(2,1)}, bf16[4,64,1280]{2,1,0:T(8,128)(2,1)}, u32[]{:S(2)}, u32[]{:S(2)}) %collective-permute-start.40) | collective-permute-done | bytes 655392 | tf_op jit(solution)/shard_map/ppermute | solution.py:123
  1002.8 6.0 collective-permute-done.45
  1008.7 33.9 %collective-permute-done.44 = bf16[128,2048]{1,0:T(8,128)(2,1)} collective-permute-done((bf16[128,2048]{1,0:T(8,128)(2,1)}, bf16[128,2048]{1,0:T(8,128)(2,1)}, u32[]{:S(2)}, u32[]{:S(2)}) %collective-permute-start.44) | collective-permute-done | bytes 524320 | tf_op jit(solution)/shard_map/ppermute | solution.py:123
  (642 shorter events, 465.4 us)
Async XLA Ops:
  7.2 54.2 %collective-permute-start.13 = (bf16[128,2048]{1,0:T(8,128)(2,1)}, bf16[128,2048]{1,0:T(8,128)(2,1)}, u32[]{:S(2)}, u32[]{:S(2)}) collective-permute-start(bf16[128,2048]{1,0:T(8,128)(2,1)} %param.23), channel_id=1, source_target_pairs={{0,8},{1,9},{2,10},{3,11},{4,12},{5,13},{6,14},{7,15},{8,16},{9,17... | collective-permute-start | bytes 1572872 | tf_op jit(solution)/shard_map/ppermute | solution.py:123
  10.3 54.4 %collective-permute-start.14 = (bf16[128,2048]{1,0:T(8,128)(2,1)}, bf16[128,2048]{1,0:T(8,128)(2,1)}, u32[]{:S(2)}, u32[]{:S(2)}) collective-permute-start(bf16[128,2048]{1,0:T(8,128)(2,1)} %param.23), channel_id=1, source_target_pairs={{0,16},{1,17},{2,18},{3,19},{4,20},{5,21},{6,22},{7,23},{8,24},{9,... | collective-permute-start | bytes 1572872 | tf_op jit(solution)/shard_map/ppermute | solution.py:123
  12.9 53.7 %collective-permute-start.15 = (bf16[128,2048]{1,0:T(8,128)(2,1)}, bf16[128,2048]{1,0:T(8,128)(2,1)}, u32[]{:S(2)}, u32[]{:S(2)}) collective-permute-start(bf16[128,2048]{1,0:T(8,128)(2,1)} %param.23), channel_id=1, source_target_pairs={{0,24},{1,25},{2,26},{3,27},{4,28},{5,29},{6,30},{7,31},{8,0},{9,1... | collective-permute-start | bytes 1572872 | tf_op jit(solution)/shard_map/ppermute | solution.py:123
  20.4 36.1 %all-to-all-start = ((bf16[4,64,1280]{2,1,0:T(8,128)(2,1)}), bf16[4,64,1280]{2,1,0:T(8,128)(2,1)}, u32[]{:S(2)}, u32[]{:S(2)}) async-start(bf16[4,64,1280]{2,1,0:T(8,128)(2,1)} %copy.173), calls=%async_computation | async-start | bytes 1310720 | tf_op jit(solution)/shard_map/all_to_all | solution.py:130
  26.7 47.1 %collective-permute-start = (bf16[128,2048]{0,1:T(8,128)(2,1)}, bf16[128,2048]{0,1:T(8,128)(2,1)}, u32[]{:S(2)}, u32[]{:S(2)}) collective-permute-start(bf16[128,2048]{0,1:T(8,128)(2,1)} %copy.169), channel_id=1, source_target_pairs={{0,2},{1,3},{2,0},{3,1},{4,6},{5,7},{6,4},{7,5},{8,10},{9,11},{10,... | collective-permute-start | bytes 1572872 | tf_op jit(solution)/shard_map/ppermute | solution.py:120
  64.7 49.8 %collective-permute-start.3 = (bf16[4,64,1280]{2,1,0:T(8,128)(2,1)}, bf16[4,64,1280]{2,1,0:T(8,128)(2,1)}, u32[]{:S(2)}, u32[]{:S(2)}) collective-permute-start(bf16[4,64,1280]{2,1,0:T(8,128)(2,1)} %all-to-all-done), channel_id=1, source_target_pairs={{0,1},{1,0},{2,3},{3,2},{4,5},{5,4},{6,7},{7,6},{8,9},{9,8},{10,11... | collective-permute-start | bytes 1966088 | tf_op jit(solution)/shard_map/ppermute | solution.py:117
  69.1 81.6 %all-to-all-start.1 = ((bf16[4,128,2048]{2,1,0:T(8,128)(2,1)}), bf16[4,128,2048]{2,1,0:T(8,128)(2,1)}, u32[]{:S(2)}, u32[]{:S(2)}) async-start(bf16[4,128,2048]{2,1,0:T(8,128)(2,1)} %bitcast_dynamic-update-slice_fusion.8), calls=%async_computation.1 | async-start | bytes 4194304 | tf_op jit(solution)/shard_map/all_to_all | solution.py:130
  73.7 40.2 %collective-permute-start.6 = (bf16[4,64,1280]{2,1,0:T(8,128)(2,1)}, bf16[4,64,1280]{2,1,0:T(8,128)(2,1)S(1)}, u32[]{:S(2)}, u32[]{:S(2)}) collective-permute-start(bf16[4,64,1280]{2,1,0:T(8,128)(2,1)} %all-to-all-done), channel_id=1, source_target_pairs={{0,16},{1,17},{2,18},{3,19},{4,20},{5,21},{6,22},{7,23},{8,24},{9,... | collective-permute-start | bytes 1966088 | tf_op jit(solution)/shard_map/ppermute | solution.py:123
  75.5 38.4 %collective-permute-start.8 = (bf16[4,64,1280]{2,1,0:T(8,128)(2,1)}, bf16[4,64,1280]{2,1,0:T(8,128)(2,1)S(1)}, u32[]{:S(2)}, u32[]{:S(2)}) collective-permute-start(bf16[4,64,1280]{2,1,0:T(8,128)(2,1)} %all-to-all-done), channel_id=1, source_target_pairs={{0,24},{1,25},{2,26},{3,27},{4,28},{5,29},{6,30},{7,31},{8,0},{9,1... | collective-permute-start | bytes 1966088 | tf_op jit(solution)/shard_map/ppermute | solution.py:123
  86.4 32.1 %collective-permute-start.5 = (bf16[4,64,1280]{2,1,0:T(8,128)(2,1)}, bf16[4,64,1280]{2,1,0:T(8,128)(2,1)S(1)}, u32[]{:S(2)}, u32[]{:S(2)}) collective-permute-start(bf16[4,64,1280]{2,1,0:T(8,128)(2,1)} %collective-permute-done.4), channel_id=1, source_target_pairs={{0,1},{1,0},{2,3},{3,2},{4,5},{5,4},{6,7},{7,6},{8,9},{9,8},{10,11... | collective-permute-start | bytes 1966088 | tf_op jit(solution)/shard_map/ppermute | solution.py:117
  174.3 77.2 %collective-permute-start.19 = (bf16[128,2048]{0,1:T(8,128)(2,1)}, bf16[128,2048]{0,1:T(8,128)(2,1)}, u32[]{:S(2)}, u32[]{:S(2)}) collective-permute-start(bf16[128,2048]{0,1:T(8,128)(2,1)} %get-tuple-element.81), channel_id=1, source_target_pairs={{0,6},{1,7},{2,4},{3,5},{4,2},{5,3},{6,0},{7,1},{8,14},{9,15},{10,... | collective-permute-start | bytes 1572872 | tf_op jit(solution)/shard_map/ppermute | solution.py:120
  175.8 75.7 %collective-permute-start.18 = (bf16[128,2048]{0,1:T(8,128)(2,1)}, bf16[128,2048]{0,1:T(8,128)(2,1)}, u32[]{:S(2)}, u32[]{:S(2)}) collective-permute-start(bf16[128,2048]{0,1:T(8,128)(2,1)} %get-tuple-element.82), channel_id=1, source_target_pairs={{0,4},{1,5},{2,6},{3,7},{4,0},{5,1},{6,2},{7,3},{8,12},{9,13},{10,... | collective-permute-start | bytes 1572872 | tf_op jit(solution)/shard_map/ppermute | solution.py:120
  177.3 74.3 %collective-permute-start.17 = (bf16[128,2048]{0,1:T(8,128)(2,1)}, bf16[128,2048]{0,1:T(8,128)(2,1)}, u32[]{:S(2)}, u32[]{:S(2)}) collective-permute-start(bf16[128,2048]{0,1:T(8,128)(2,1)} %get-tuple-element.80), channel_id=1, source_target_pairs={{0,2},{1,3},{2,0},{3,1},{4,6},{5,7},{6,4},{7,5},{8,10},{9,11},{10,... | collective-permute-start | bytes 1572872 | tf_op jit(solution)/shard_map/ppermute | solution.py:120
  258.4 43.9 %collective-permute-start.23 = (bf16[128,2176]{0,1:T(8,128)(2,1)S(1)}, bf16[128,2176]{0,1:T(8,128)(2,1)S(1)}, u32[]{:S(2)}, u32[]{:S(2)}) collective-permute-start(bf16[128,2176]{0,1:T(8,128)(2,1)S(1)} %fusion.180), channel_id=1, source_target_pairs={{0,16},{1,17},{2,18},{3,19},{4,20},{5,21},{6,22},{7,23},{8,24},{9,... | collective-permute-start | bytes 1671176 | tf_op jit(solution)/shard_map/ppermute | solution.py:123
  395.1 28.9 %all-to-all-start.2 = ((bf16[8,40,2176]{2,1,0:T(8,128)(2,1)}), bf16[8,40,2176]{2,1,0:T(8,128)(2,1)}, u32[]{:S(2)}, u32[]{:S(2)}) async-start(bf16[8,40,2176]{2,1,0:T(8,128)(2,1)} %bitcast.511), calls=%async_computation.2 | async-start | bytes 2785280 | tf_op jit(solution)/shard_map/all_to_all | solution.py:130
  423.9 28.6 %all-to-all-start.4 = ((bf16[8,40,2176]{2,1,0:T(8,128)(2,1)}), bf16[8,40,2176]{2,1,0:T(8,128)(2,1)}, u32[]{:S(2)}, u32[]{:S(2)}) async-start(bf16[8,40,2176]{2,1,0:T(8,128)(2,1)} %bitcast.495), calls=%async_computation.4 | async-start | bytes 2785280 | tf_op jit(solution)/shard_map/all_to_all | solution.py:130
  598.2 35.5 %collective-permute-start.31 = (bf16[128,2176]{0,1:T(8,128)(2,1)}, bf16[128,2176]{0,1:T(8,128)(2,1)}, u32[]{:S(2)}, u32[]{:S(2)}) collective-permute-start(bf16[128,2176]{0,1:T(8,128)(2,1)} %fusion.15), channel_id=1, source_target_pairs={{0,8},{1,9},{2,10},{3,11},{4,12},{5,13},{6,14},{7,15},{8,16},{9,17... | collective-permute-start | bytes 1671176 | tf_op jit(solution)/shard_map/ppermute | solution.py:123
  611.8 28.7 %collective-permute-start.30 = (bf16[128,2176]{0,1:T(8,128)(2,1)}, bf16[128,2176]{0,1:T(8,128)(2,1)}, u32[]{:S(2)}, u32[]{:S(2)}) collective-permute-start(bf16[128,2176]{0,1:T(8,128)(2,1)} %fusion.14), channel_id=1, source_target_pairs={{0,16},{1,17},{2,18},{3,19},{4,20},{5,21},{6,22},{7,23},{8,24},{9,... | collective-permute-start | bytes 1671176 | tf_op jit(solution)/shard_map/ppermute | solution.py:123
  653.1 60.4 %all-to-all-start.7 = ((bf16[8,40,2048]{2,1,0:T(8,128)(2,1)}), bf16[8,40,2048]{2,1,0:T(8,128)(2,1)}, u32[]{:S(2)}, u32[]{:S(2)}) async-start(bf16[8,40,2048]{2,1,0:T(8,128)(2,1)} %bitcast.82), calls=%async_computation.7 | async-start | bytes 2621440 | tf_op jit(solution)/shard_map/all_to_all | solution.py:130
  726.1 33.0 %collective-permute-start.36 = (bf16[128,2048]{0,1:T(8,128)(2,1)}, bf16[128,2048]{0,1:T(8,128)(2,1)}, u32[]{:S(2)}, u32[]{:S(2)}) collective-permute-start(bf16[128,2048]{0,1:T(8,128)(2,1)} %get-tuple-element.77), channel_id=1, source_target_pairs={{0,4},{1,5},{2,6},{3,7},{4,0},{5,1},{6,2},{7,3},{8,12},{9,13},{10,... | collective-permute-start | bytes 1572872 | tf_op jit(solution)/shard_map/ppermute | solution.py:120
  726.6 41.8 %collective-permute-start.35 = (bf16[128,2048]{0,1:T(8,128)(2,1)}, bf16[128,2048]{0,1:T(8,128)(2,1)}, u32[]{:S(2)}, u32[]{:S(2)}) collective-permute-start(bf16[128,2048]{0,1:T(8,128)(2,1)} %get-tuple-element.75), channel_id=1, source_target_pairs={{0,2},{1,3},{2,0},{3,1},{4,6},{5,7},{6,4},{7,5},{8,10},{9,11},{10,... | collective-permute-start | bytes 1572872 | tf_op jit(solution)/shard_map/ppermute | solution.py:120
  728.4 195.7 %collective-permute-start.38 = (bf16[4,4,64,1280]{3,2,1,0:T(8,128)(2,1)}, bf16[4,4,64,1280]{3,2,1,0:T(8,128)(2,1)}, u32[]{:S(2)}, u32[]{:S(2)}) collective-permute-start(bf16[4,4,64,1280]{3,2,1,0:T(8,128)(2,1)} %dynamic-slice_bitcast_fusion), channel_id=1, source_target_pairs={{0,1},{1,0},{2,3},{3,2},{4,5},{5,4},{6,7},{7,6},{8,9},{9,8},{10,11... | collective-permute-start | bytes 7864328 | tf_op jit(solution)/shard_map/ppermute | solution.py:117
  735.5 179.7 %collective-permute-start.42 = (bf16[1,4,128,2048]{3,2,1,0:T(8,128)(2,1)}, bf16[1,4,128,2048]{3,2,1,0:T(8,128)(2,1)}, u32[]{:S(2)}, u32[]{:S(2)}) collective-permute-start(bf16[1,4,128,2048]{3,2,1,0:T(8,128)(2,1)} %dynamic-slice_bitcast_fusion.1), channel_id=1, source_target_pairs={{0,1},{1,0},{2,3},{3,2},{4,5},{5,4},{6,7},{7,6},{8,9},{9,8},{10,11... | collective-permute-start | bytes 6291464 | tf_op jit(solution)/shard_map/ppermute | solution.py:117
  737.3 39.3 %all-to-all-start.3 = ((bf16[8,40,2048]{2,1,0:T(8,128)(2,1)}), bf16[8,40,2048]{2,1,0:T(8,128)(2,1)}, u32[]{:S(2)}, u32[]{:S(2)}) async-start(bf16[8,40,2048]{2,1,0:T(8,128)(2,1)} %bitcast.512), calls=%async_computation.3 | async-start | bytes 2621440 | tf_op jit(solution)/shard_map/all_to_all | solution.py:130
  741.7 164.7 %reduce-scatter.4.cloned.1.call-start = ((), (), s32[]{:S(2)}) async-start(), calls=%async_computation.21 | async-start | bytes 1081344
  759.1 34.9 %collective-permute-start.25 = (bf16[128,2048]{0,1:T(8,128)(2,1)}, bf16[128,2048]{0,1:T(8,128)(2,1)S(1)}, u32[]{:S(2)}, u32[]{:S(2)}) collective-permute-start(bf16[128,2048]{0,1:T(8,128)(2,1)} %fusion.101), channel_id=1, source_target_pairs={{0,16},{1,17},{2,18},{3,19},{4,20},{5,21},{6,22},{7,23},{8,24},{9,... | collective-permute-start | bytes 1572872 | tf_op jit(solution)/shard_map/ppermute | solution.py:123
  776.5 131.3 %collective-permute-start.46 = (f32[34,128]{1,0:T(8,128)S(1)}, f32[34,128]{1,0:T(8,128)S(1)}, u32[]{:S(2)}, u32[]{:S(2)}) collective-permute-start(f32[34,128]{1,0:T(8,128)S(1)} %maximum_bitcast_fusion.1), channel_id=1, source_target_pairs={{0,1},{1,0},{2,3},{3,2},{4,5},{5,4},{6,7},{7,6},{8,9},{9,8},{10,11... | collective-permute-start | bytes 52232 | tf_op jit(solution)/shard_map/ppermute | solution.py:117
  919.7 69.2 %all-to-all-start.19 = ((bf16[4,1,128,2048]{3,2,1,0:T(8,128)(2,1)}), bf16[4,1,128,2048]{3,2,1,0:T(8,128)(2,1)}, u32[]{:S(2)}, u32[]{:S(2)}) async-start(bf16[4,1,128,2048]{3,2,1,0:T(8,128)(2,1)} %fusion.104), calls=%async_computation.19 | async-start | bytes 4194304 | tf_op jit(solution)/shard_map/all_to_all | solution.py:130
  931.2 55.1 %collective-permute-start.40 = (bf16[4,64,1280]{2,1,0:T(8,128)(2,1)}, bf16[4,64,1280]{2,1,0:T(8,128)(2,1)}, u32[]{:S(2)}, u32[]{:S(2)}) collective-permute-start(bf16[4,64,1280]{2,1,0:T(8,128)(2,1)} %get-tuple-element.69), channel_id=1, source_target_pairs={{0,16},{1,17},{2,18},{3,19},{4,20},{5,21},{6,22},{7,23},{8,24},{9,... | collective-permute-start | bytes 1966088 | tf_op jit(solution)/shard_map/ppermute | solution.py:123
  931.8 54.4 %collective-permute-start.39 = (bf16[4,64,1280]{2,1,0:T(8,128)(2,1)}, bf16[4,64,1280]{2,1,0:T(8,128)(2,1)}, u32[]{:S(2)}, u32[]{:S(2)}) collective-permute-start(bf16[4,64,1280]{2,1,0:T(8,128)(2,1)} %get-tuple-element.67), channel_id=1, source_target_pairs={{0,8},{1,9},{2,10},{3,11},{4,12},{5,13},{6,14},{7,15},{8,16},{9,17... | collective-permute-start | bytes 1966088 | tf_op jit(solution)/shard_map/ppermute | solution.py:123
  995.9 46.7 %collective-permute-start.44 = (bf16[128,2048]{1,0:T(8,128)(2,1)}, bf16[128,2048]{1,0:T(8,128)(2,1)}, u32[]{:S(2)}, u32[]{:S(2)}) collective-permute-start(bf16[128,2048]{1,0:T(8,128)(2,1)} %get-tuple-element.74), channel_id=1, source_target_pairs={{0,16},{1,17},{2,18},{3,19},{4,20},{5,21},{6,22},{7,23},{8,24},{9,... | collective-permute-start | bytes 1572872 | tf_op jit(solution)/shard_map/ppermute | solution.py:123
  997.4 45.2 %collective-permute-start.43 = (bf16[128,2048]{1,0:T(8,128)(2,1)}, bf16[128,2048]{1,0:T(8,128)(2,1)}, u32[]{:S(2)}, u32[]{:S(2)}) collective-permute-start(bf16[128,2048]{1,0:T(8,128)(2,1)} %get-tuple-element.72), channel_id=1, source_target_pairs={{0,8},{1,9},{2,10},{3,11},{4,12},{5,13},{6,14},{7,15},{8,16},{9,17... | collective-permute-start | bytes 1572872 | tf_op jit(solution)/shard_map/ppermute | solution.py:123
  (189 other events, 2823.3 us)
Sparse Core Ops, SparseCore 0:
  773.3 133.0 reduce-scatter.3

commit v2 on v1

v2 whole, which is shorter than its diff:
```python
import functools

import jax
import jax.numpy as jnp
from jax import lax
from jax.experimental import pallas as pl
from jax.experimental.pallas import tpu as pltpu
from jax.sharding import PartitionSpec as P

EPS = 1e-06
THETA = 1000000.0
NEGATIVE = -1e30
CORES = 2
LANES = 128
FLOPS_A_MICRO = 1_000_000_000
BYTES_A_MICRO = 2_000_000
VMEM_BYTES = 32 * 1024 * 1024
MORE_BYTES = 50 * 1024 * 1024
CONTRACT_ROWS = (((0,), (0,)), ((), ()))
CONTRACT_LAST = (((1,), (1,)), ((), ()))


def root_mean_square_norm(value_rows, gain):
    return (
        value_rows
        * lax.rsqrt(jnp.mean(value_rows * value_rows, axis=-1, keepdims=True) + EPS)
        * gain
    )


def sequence_layout(lengths, count_total):
    ends = jnp.cumsum(lengths)
    starts = ends - lengths
    places = jnp.arange(count_total, dtype=jnp.int32)
    member = ((places[:, None] >= starts[None, :]) & (places[:, None] < ends[None, :])).astype(
        jnp.int32
    )
    labels = jnp.arange(lengths.shape[0], dtype=jnp.int32)
    segment = jnp.sum(member * labels[None, :], axis=1)
    offset = jnp.sum(member * starts[None, :], axis=1)
    return (segment, places - offset)


def rotary_tables(position, width):
    half = width // 2
    inverse = jnp.power(THETA, -(jnp.arange(half, dtype=jnp.float32) * 2.0) / width)
    angle = position.astype(jnp.float32)[:, None] * inverse[None, :]
    angle = jnp.concatenate([angle, angle], axis=1)
    return (jnp.cos(angle), jnp.sin(angle))


def call(kernel, outs, vmem=VMEM_BYTES, micros=0, **specs):
    if micros:
        specs["cost_estimate"] = pl.CostEstimate(
            flops=micros * FLOPS_A_MICRO, bytes_accessed=micros * BYTES_A_MICRO, transcendentals=0
        )
    return pl.pallas_call(
        kernel,
        out_shape=outs,
        compiler_params=pltpu.CompilerParams(vmem_limit_bytes=vmem),
        **specs,
    )


def turned_sine(sine_table):
    half = sine_table.shape[1] // 2
    return jnp.concatenate([-sine_table[:, :half], sine_table[:, half:]], axis=1)


def head_rotated(value, gain, cosine, sine):
    normal = (
        value * lax.rsqrt(jnp.mean(value * value, axis=-1, keepdims=True) + EPS) * gain
    )
    return normal * cosine + pltpu.roll(normal, value.shape[1] // 2, 1) * sine


def head_shares(query, key, allowed, scale):
    scores = lax.dot_general(query, key, CONTRACT_LAST, preferred_element_type=jnp.float32)
    scores = jnp.where(allowed, scores * scale, NEGATIVE)
    exponent = jnp.exp(scores - jnp.max(scores, axis=-1, keepdims=True))
    return exponent / jnp.sum(exponent, axis=-1, keepdims=True)


def norm_kernel(outer, my_outer, *refs):
    *parts, gain, order, out, normed = refs
    count = parts[0].shape[0]
    span = order.shape[0]
    half = span // CORES
    for b, part in enumerate(parts):
        normed[b * count : (b + 1) * count, :] = root_mean_square_norm(
            part[...].astype(jnp.float32), gain[...]
        ).astype(jnp.bfloat16)
    for s in range(outer):
        start = lax.rem(my_outer[0] + (outer - s), outer) * span
        block = normed[:, pl.ds(pl.multiple_of(start, LANES), span)]
        block = jnp.dot(block, order[...], preferred_element_type=jnp.float32)
        block = block.astype(jnp.bfloat16)
        for k in range(CORES):
            first = (k * outer + s) * half
            out[:, first : first + half] = block[:, k * half : (k + 1) * half]


def project_kernel(normed, *refs):
    *pieces, out = refs
    rows = pieces[0].shape[0]
    total = jnp.zeros(out.shape, jnp.float32)
    for i, piece in enumerate(pieces):
        total += jnp.dot(
            normed[:, i * rows : (i + 1) * rows], piece[...], preferred_element_type=jnp.float32
        )
    out[...] = total


def project_back_kernel(my_outer, grad, own, other, order, out):
    f32, bf16 = jnp.float32, jnp.bfloat16
    block = jnp.concatenate(
        [
            lax.dot_general(grad[...], part[0], CONTRACT_LAST, preferred_element_type=f32)
            for part in (own, other)
        ],
        axis=1,
    ).astype(bf16)
    out[...] = lax.dot_general(
        block, order[...], CONTRACT_LAST, preferred_element_type=f32
    ).astype(bf16)


def tokens_back_kernel(tokens, own, *refs):
    *others, hidden_grad, gain, tokens_grad, gain_grad = refs
    f32 = jnp.float32
    grad = own[...].astype(f32)
    for other in others:
        grad = grad + other[...].astype(f32)
    value = tokens[...].astype(f32)
    root = lax.rsqrt(jnp.mean(value * value, axis=-1, keepdims=True) + EPS)
    normal = value * root
    gain_grad[...] = jnp.sum(grad * normal, axis=0, keepdims=True)
    grad = grad * gain[...]
    tokens_grad[...] = hidden_grad[...] + root * (
        grad - normal * jnp.mean(normal * grad, axis=-1, keepdims=True)
    )


def attend_kernel(scale, front, cosine, sine, allowed, query_gain, key_gain, order, *outs):
    query_out, key_out, value_out, context_out, context = outs
    width = cosine.shape[1]
    heads = query_out.shape[1] // width
    bf16 = jnp.bfloat16
    cos, sin = cosine[...], sine[...]
    open_places = allowed[...] > 0.0
    key = head_rotated(
        front[:, heads * width : (heads + 1) * width], key_gain[...], cos, sin
    ).astype(bf16)
    value = front[:, (heads + 1) * width :].astype(bf16)
    key_out[...] = key
    value_out[...] = value
    for h in range(heads):
        part = slice(h * width, (h + 1) * width)
        query = head_rotated(front[:, part], query_gain[...], cos, sin).astype(bf16)
        query_out[:, part] = query
        shares = head_shares(query, key, open_places, scale).astype(bf16)
        context[:, part] = jnp.dot(
            shares, value, preferred_element_type=jnp.float32
        ).astype(bf16)
    context_out[...] = jnp.dot(
        context[...], order[...], preferred_element_type=jnp.float32
    ).astype(bf16)


def head_back(grad, value, gain, cosine, sine):
    grad = grad * cosine + pltpu.roll(grad * sine, value.shape[1] // 2, 1)
    root = lax.rsqrt(jnp.mean(value * value, axis=-1, keepdims=True) + EPS)
    normal = value * root
    gain_grad = jnp.sum(grad * normal, axis=0, keepdims=True)
    grad = grad * gain
    grad = root * (grad - normal * jnp.mean(normal * grad, axis=-1, keepdims=True))
    return grad, gain_grad


def attend_back_kernel(
    scale, front, query_in, key_in, value_in, grad_own, grad_other, cosine, sine, allowed, *rest
):
    query_gain, key_gain, order, front_grad, gain_grads, context_grad = rest
    half = grad_own.shape[1]
    context_grad[...] = (
        lax.dot_general(
            grad_own[...], order[:, :half], CONTRACT_LAST, preferred_element_type=jnp.float32
        )
        + lax.dot_general(
            grad_other[...], order[:, half:], CONTRACT_LAST, preferred_element_type=jnp.float32
        )
    ).astype(jnp.bfloat16)
    width = cosine.shape[1]
    heads = query_in.shape[1] // width
    f32, bf16 = jnp.float32, jnp.bfloat16
    cos, sin = cosine[...], sine[...]
    open_places = allowed[...] > 0.0
    key, value = key_in[...], value_in[...]
    key_total = jnp.zeros(key.shape, f32)
    value_total = jnp.zeros(key.shape, f32)
    gain_total = jnp.zeros((1, width), f32)
    for h in range(heads):
        part = slice(h * width, (h + 1) * width)
        query, grad = query_in[:, part], context_grad[:, part]
        shares = head_shares(query, key, open_places, scale)
        grad_shares = lax.dot_general(grad, value, CONTRACT_LAST, preferred_element_type=f32)
        grad_scores = (
            shares * (grad_shares - jnp.sum(shares * grad_shares, axis=-1, keepdims=True))
        ).astype(bf16)
        value_total += lax.dot_general(
            shares.astype(bf16), grad, CONTRACT_ROWS, preferred_element_type=f32
        )
        key_total += lax.dot_general(
            grad_scores, query, CONTRACT_ROWS, preferred_element_type=f32
        )
        grad_query = jnp.dot(grad_scores, key, preferred_element_type=f32) * scale
        grad_query, gain_grad = head_back(grad_query, front[:, part], query_gain[...], cos, sin)
        front_grad[:, part] = grad_query.astype(bf16)
        gain_total += gain_grad
    part = slice(heads * width, (heads + 1) * width)
    grad_key, key_gain_grad = head_back(
        key_total * scale, front[:, part], key_gain[...], cos, sin
    )
    front_grad[:, part] = grad_key.astype(bf16)
    front_grad[:, (heads + 1) * width :] = value_total.astype(bf16)

    @pl.when(pl.program_id(0) == 0)
    def _():
        gain_grads[...] = jnp.zeros(gain_grads.shape, f32)

    gain_grads[0:1, :] += gain_total
    gain_grads[1:2, :] += key_gain_grad


def router_kernel(experts, *refs):
    tokens, own, *others, gain, router, mask, hidden_out, wide_out, prob_out, gates_out = refs
    f32, bf16 = jnp.float32, jnp.bfloat16
    model = tokens.shape[1]
    lanes = mask.shape[1]
    hidden = tokens[...].astype(f32) + own[...]
    for other in others:
        hidden = hidden + other[...].astype(f32)
    hidden_out[...] = hidden
    second = root_mean_square_norm(hidden, gain[...]).astype(bf16)
    wide_out[:, :model] = second
    logits = jnp.dot(second, router[...], preferred_element_type=f32)
    column = lax.broadcasted_iota(jnp.int32, logits.shape, 1)
    logits = jnp.where(column < experts, logits, NEGATIVE)
    exponent = jnp.exp(logits - jnp.max(logits, axis=-1, keepdims=True))
    prob = exponent / jnp.sum(exponent, axis=-1, keepdims=True)
    chosen = prob * mask[...]
    gates = chosen / jnp.sum(chosen, axis=-1, keepdims=True)
    prob_out[...] = prob
    gates_out[...] = gates
    high = gates.astype(bf16).astype(f32)
    low = gates - high
    if 2 * experts <= lanes:
        wide_out[:, model:] = (high + pltpu.roll(low, experts, 1)).astype(bf16)
    else:
        wide_out[:, model : model + lanes] = high.astype(bf16)
        wide_out[:, model + lanes :] = low.astype(bf16)


def router_back_kernel(experts, *refs):
    own, near, came, cotangent, hidden, gain, router, mask, prob, gates, *outs = refs
    hidden_grad, attn_grad, logits_grad, gain_grad = outs
    f32, bf16 = jnp.float32, jnp.bfloat16
    model = cotangent.shape[1]
    lanes = mask.shape[1]
    pairs = own[:, model:] + near[:, model:].astype(f32) + came[:, model:].astype(f32)
    if 2 * experts <= lanes:
        grad_gates = pairs + pltpu.roll(pairs, lanes - experts, 1)
    else:
        grad_gates = pairs[:, :lanes] + pairs[:, lanes:]
    chosen_sum = jnp.sum(prob[...] * mask[...], axis=-1, keepdims=True)
    grad_gates = jnp.where(mask[...] > 0.0, grad_gates, 0.0)
    grad_chosen = (
        mask[...]
        * (grad_gates - jnp.sum(gates[...] * grad_gates, axis=-1, keepdims=True))
        / chosen_sum
    )
    grad_logits = (
        prob[...] * (grad_chosen - jnp.sum(prob[...] * grad_chosen, axis=-1, keepdims=True))
    ).astype(bf16)
    logits_grad[...] = grad_logits
    grad = (
        own[:, :model]
        + near[:, :model].astype(f32)
        + came[:, :model].astype(f32)
        + lax.dot_general(grad_logits, router[...], CONTRACT_LAST, preferred_element_type=f32)
    )
    value = hidden[...]
    root = lax.rsqrt(jnp.mean(value * value, axis=-1, keepdims=True) + EPS)
    normal = value * root
    gain_grad[...] = jnp.sum(grad * normal, axis=0, keepdims=True)
    grad = grad * gain[...]
    grad = cotangent[...].astype(f32) + root * (
        grad - normal * jnp.mean(normal * grad, axis=-1, keepdims=True)
    )
    hidden_grad[...] = grad
    attn_grad[...] = grad.astype(bf16)


def pick_kernel(capacity, own, partner, near, earlier, *outs):
    *parts, picks = outs
    f32, bf16 = jnp.float32, jnp.bfloat16
    rows, model = parts[0].shape
    count = own.shape[0]
    masks = [
        lax.dot_general(near[...], side[:, model:], CONTRACT_LAST, preferred_element_type=f32)
        for side in (own, partner)
    ]
    ranks = [jnp.dot(m.astype(bf16), earlier[...], preferred_element_type=f32) for m in masks]
    mask = jnp.concatenate(masks, axis=1)
    rank = jnp.concatenate([ranks[0], ranks[1] + capacity], axis=1)
    place = lax.broadcasted_iota(jnp.int32, (rows, CORES * count), 0).astype(f32)
    for r in range(len(parts)):
        hit = (place == rank[r : r + 1, :]) & (mask[r : r + 1, :] > 0.5)
        picks[r * rows : (r + 1) * rows, :] = jnp.where(hit, 1.0, 0.0).astype(bf16)
    both = jnp.concatenate([own[:, :model], partner[:, :model]], axis=0)
    chosen = jnp.dot(picks[...], both, preferred_element_type=f32).astype(bf16)
    for r, part in enumerate(parts):
        part[...] = chosen[r * rows : (r + 1) * rows, :]


def send_kernel(picks, own, partner, *parts):
    rows = parts[0].shape[0]
    both = jnp.concatenate([own[...], partner[...]], axis=0)
    chosen = jnp.dot(picks[...], both, preferred_element_type=jnp.float32).astype(jnp.bfloat16)
    for r, part in enumerate(parts):
        part[...] = chosen[r * rows : (r + 1) * rows, :]


def settle_kernel(picks, *refs):
    *parts, own, partner = refs
    count = own.shape[0]
    rows = jnp.concatenate([part[...] for part in parts], axis=0)
    total = lax.dot_general(
        picks[...], rows, CONTRACT_ROWS, preferred_element_type=jnp.float32
    )
    own[...] = total[:count, :]
    partner[...] = total[count:, :].astype(jnp.bfloat16)


def move_kernel(units, weight, *parts):
    rows = parts[0].shape[0]
    moved = jnp.dot(units[...], weight[...], preferred_element_type=jnp.float32)
    for r, part in enumerate(parts):
        part[...] = moved[r * rows : (r + 1) * rows, :].astype(jnp.bfloat16)


def expert_kernel(chips, experts, me, *refs):
    f32, bf16 = jnp.float32, jnp.bfloat16
    came, given = refs[:chips], refs[chips : 2 * chips]
    gate_weight, up_weight, down_weight = refs[2 * chips : 2 * chips + 3]
    back = refs[2 * chips + 3 : 3 * chips + 3]
    units_out, gate_out, up_out, rows, grads, row_gate, change, total = refs[3 * chips + 3 :]
    size, model = came[0].shape[0], rows.shape[1]
    step = pl.program_id(0)
    column = lax.broadcasted_iota(jnp.int32, (size, came[0].shape[1] - model), 1)
    high_column, low_column = column == me[0], column == me[0] + experts

    @pl.when(step == 0)
    def _():
        for r in range(chips):
            part = slice(r * size, (r + 1) * size)
            rows[part, :] = came[r][:, :model]
            grads[part, :] = given[r][...]
            side = jnp.where(high_column | low_column, came[r][:, model:].astype(f32), 0.0)
            row_gate[part, :] = jnp.sum(side, axis=1, keepdims=True)
        change[...] = jnp.zeros(change.shape, f32)
        total[...] = jnp.zeros(total.shape, f32)

    gate_part = jnp.dot(rows[...], gate_weight[...], preferred_element_type=f32)
    up_part = jnp.dot(rows[...], up_weight[...], preferred_element_type=f32)
    raw = lax.dot_general(
        grads[...], down_weight[...], CONTRACT_LAST, preferred_element_type=f32
    )
    sig = 1.0 / (1.0 + jnp.exp(-gate_part))
    silu = gate_part * sig
    units = silu * up_part
    change[...] += jnp.sum(units * raw, axis=1, keepdims=True)
    units_out[...] = (row_gate[...] * units).astype(bf16)
    grad_units = row_gate[...] * raw
    gate_grad = (grad_units * up_part * sig * (1.0 + gate_part * (1.0 - sig))).astype(bf16)
    up_grad = (grad_units * silu).astype(bf16)
    gate_out[...] = gate_grad
    up_out[...] = up_grad
    total[...] += lax.dot_general(
        gate_grad, gate_weight[...], CONTRACT_LAST, preferred_element_type=f32
    ) + lax.dot_general(up_grad, up_weight[...], CONTRACT_LAST, preferred_element_type=f32)

    @pl.when(step == pl.num_programs(0) - 1)
    def _():
        for r in range(chips):
            part = slice(r * size, (r + 1) * size)
            back[r][:, :model] = total[part, :].astype(bf16)
            high = change[part, :].astype(bf16).astype(f32)
            low = change[part, :] - high
            back[r][:, model:] = (
                jnp.where(high_column, high, 0.0) + jnp.where(low_column, low, 0.0)
            ).astype(bf16)


def expert_grad_kernel(outer, chips, *refs):
    f32 = jnp.float32
    parts = outer * chips
    rows, grads = refs[:parts], refs[parts : 2 * parts]
    units, gates, ups = (
        refs[2 * parts + i * outer : 2 * parts + (i + 1) * outer] for i in range(3)
    )
    gate_out, up_out, down_out, left, right, all_units, all_gates, all_ups = refs[
        2 * parts + 3 * outer :
    ]
    size = rows[0].shape[0]
    for i in range(parts):
        part = slice(i * size, (i + 1) * size)
        left[part, :] = rows[i][...]
        right[part, :] = grads[i][...]
    size = units[0].shape[0]

    @pl.when(pl.program_id(0) == 0)
    def _():
        for s in range(outer):
            part = slice(s * size, (s + 1) * size)
            all_units[part, :] = units[s][...]
            all_gates[part, :] = gates[s][...]
            all_ups[part, :] = ups[s][...]

    def product(a, b):
        return lax.dot_general(a[...], b[...], CONTRACT_ROWS, preferred_element_type=f32)

    gate_out[...] = product(left, all_gates)
    up_out[...] = product(left, all_ups)
    down_out[...] = product(all_units, right)


def round_up(number, step):
    return -(-number // step) * step


def after(value, *others):
    return lax.optimization_barrier((value, *others))[0]


def body(
    tokens,
    cotangent,
    lengths,
    routes,
    query_weight,
    key_matrix,
    value_matrix,
    out_weight,
    router_weight,
    expert_gate,
    expert_up,
    expert_down,
    first_gain,
    second_gain,
    query_norm_gain,
    key_gain,
):
    f32, bf16, i32 = jnp.float32, jnp.bfloat16, jnp.int32
    shape = jax.ShapeDtypeStruct
    fence = lax.optimization_barrier
    count, model = tokens.shape
    width = query_norm_gain.shape[0]
    heads = query_weight.shape[1] // width
    kv_heads = key_matrix.shape[1] // width
    head_group = heads // kv_heads
    choose = routes.shape[1]
    shards = lax.axis_size("fsdp")
    experts = shards * expert_gate.shape[0]
    capacity = max(2, count * choose * 5 // (4 * experts))
    scale = width ** (-0.5)

    chips = kv_heads
    plane = chips * CORES
    outer = shards // plane
    span = outer // chips
    me = lax.axis_index("fsdp")
    my_core = me % CORES
    my_chip = (me // CORES) % chips
    my_outer = me // plane
    me_scalar = me.reshape(1)
    outer_scalar = my_outer.reshape(1)
    smem = pl.BlockSpec(memory_space=pltpu.SMEM)
    vmem = pl.BlockSpec(memory_space=pltpu.VMEM)

    def swap_core(value):
        return lax.ppermute(value, "fsdp", [(i, i ^ 1) for i in range(shards)])

    def swap_chip(value, r):
        if r == 0:
            return value
        return lax.ppermute(value, "fsdp", [(i, i ^ (r * CORES)) for i in range(shards)])

    def shift_outer(value, s=1):
        if s == 0:
            return value
        return lax.ppermute(
            value,
            "fsdp",
            [(i, ((i // plane + s) % outer) * plane + i % plane) for i in range(shards)],
        )

    def gather_chips(value):
        return [swap_chip(value, r) for r in range(chips)]

    def spread(parts):
        return [swap_chip(part, r) for r, part in enumerate(parts)]

    def ring_reduce(part):
        total = part(1)
        for s in range(2, outer):
            total = shift_outer(total.astype(bf16)).astype(f32) + part(s)
        return part(0), shift_outer(total.astype(bf16))

    def scatter_outer(take):
        total = take(my_outer)
        for s in range(1, outer):
            total = total + shift_outer(take((my_outer + s) % outer), s)
        return total

    def by_chip(parts):
        parts = jnp.stack(parts)
        return [
            lax.dynamic_index_in_dim(parts, my_chip ^ m, 0, keepdims=False) for m in range(chips)
        ]

    depth = query_weight.shape[0]
    group_columns = head_group * width
    half_columns = group_columns // CORES
    columns = group_columns + 2 * width
    rows_out = out_weight.shape[0]

    def arrival_order(length, block, inner):
        place = jnp.arange(length, dtype=i32)
        went_to = (
            (
                ((place // block % CORES) ^ my_core) * chips
                + ((place // (block * CORES) % chips) ^ my_chip)
            )
            * inner
            + place // (block * plane)
        ) * block + place % block
        return (went_to[:, None] == place[None, :]).astype(bf16)

    front_order = arrival_order(plane * depth, depth, 1)
    out_order = arrival_order(group_columns, rows_out, span)

    lanes = round_up(experts, LANES)
    pair_width = round_up(2 * experts, LANES)
    mask = jnp.sum(
        (routes[:, :, None] == jnp.arange(lanes, dtype=i32)[None, None, :]).astype(f32), axis=1
    )
    near = jnp.arange(2 * chips, dtype=i32)
    near = jnp.where(
        near < chips, my_outer * plane + (my_chip ^ near) * CORES + my_core, -1
    )
    near = (near[:, None] == jnp.arange(lanes, dtype=i32)[None, :]).astype(bf16)
    earlier = jnp.triu(jnp.ones((count, count), bf16), 1)
    part_rows = round_up(CORES * capacity, 16)
    slots = chips * part_rows

    def dispatch_first(piece, partner):
        *parts, picks = call(
            functools.partial(pick_kernel, capacity),
            [shape((part_rows, model), bf16)] * chips + [shape((slots, CORES * count), bf16)],
        )(piece, partner, near, earlier)
        return parts, picks

    def dispatch(picks, piece, partner):
        return call(send_kernel, [shape((part_rows, piece.shape[1]), bf16)] * chips)(
            picks, piece, partner
        )

    def settle(picks, parts):
        columns_of = parts[0].shape[1]
        return call(
            settle_kernel, (shape((count, columns_of), f32), shape((count, columns_of), bf16))
        )(picks, *parts)

    cut = []
    for r in range(chips):
        target = my_chip ^ r
        part = [
            lax.dynamic_slice_in_dim(query_weight, target * group_columns, group_columns, 1),
            lax.dynamic_slice_in_dim(key_matrix, target * width, width, 1),
            lax.dynamic_slice_in_dim(value_matrix, target * width, width, 1),
        ]
        cut.append(swap_chip(jnp.concatenate(part, axis=1), r))
    cut = jnp.concatenate(cut, axis=0)
    front_pieces, front_others = [cut], []
    out_pieces = [out_weight, shift_outer(out_weight)]
    cotangent_wide = jnp.concatenate([cotangent, mask.astype(bf16)], axis=1)
    cotangent_pieces, cotangent_parts, picks = [cotangent_wide], [], []

    def send_cotangent(piece, partner):
        parts, pick = dispatch_first(piece, partner)
        cotangent_parts.append(spread(parts))
        picks.append(pick)

    router_parts = router_weight.reshape(1, depth * experts)
    for t in range(2, outer + 1):
        (
            front_pieces[-1],
            out_pieces[-1],
            tokens,
            lengths,
            router_parts,
            cotangent_pieces[0],
        ) = fence(
            (
                front_pieces[-1],
                out_pieces[-1],
                tokens,
                lengths,
                router_parts,
                cotangent_pieces[0],
            )
        )
        front_pieces.append(shift_outer(front_pieces[-1]))
        front_others.append(swap_core(front_pieces[-2]))
        if t < outer:
            out_pieces.append(shift_outer(out_pieces[-1]))
        if t == 2:
            token_parts = gather_chips(tokens)
            length_parts = gather_chips(lengths)
            router_parts = jnp.concatenate([router_parts, swap_core(router_parts)], axis=0)
            cotangent_partner = swap_core(cotangent_pieces[0])
        if t == 3:
            router_parts = jnp.concatenate(gather_chips(router_parts), axis=0)
            send_cotangent(cotangent_pieces[0], cotangent_partner)
    cotangent_pieces.append(shift_outer(cotangent_pieces[0]))
    stacked = jnp.stack(out_pieces)
    out_own = []
    for r in range(chips):
        part = [
            lax.dynamic_index_in_dim(
                stacked,
                (my_outer + outer - ((my_chip ^ r) * span + u)) % outer,
                0,
                keepdims=False,
            )
            for u in range(span)
        ]
        out_own.append(swap_chip(jnp.concatenate(part, axis=0), r))

    together = chips * count
    first_gain_row, second_gain_row = first_gain[None, :], second_gain[None, :]
    query_gain_row, key_gain_row = query_norm_gain[None, :], key_gain[None, :]
    normed_low = call(
        functools.partial(norm_kernel, outer),
        shape((together, model), bf16),
        in_specs=[smem] + [vmem] * (chips + 2),
        scratch_shapes=[pltpu.VMEM((together, model), bf16)],
    )(outer_scalar, *token_parts, first_gain_row, front_order)
    layouts = [sequence_layout(part[0], count) for part in length_parts]
    segment = jnp.stack([layout[0] for layout in layouts])
    position = jnp.concatenate([layout[1] for layout in layouts])
    cosine_table, sine_table = rotary_tables(position, width)
    sine_table = turned_sine(sine_table)
    places = jnp.arange(count, dtype=i32)
    allowed = (segment[:, :, None] == segment[:, None, :]) & (
        places[None, None, :] <= places[None, :, None]
    )
    allowed = allowed.astype(f32).reshape(together, count)
    (
        front_pieces[-1],
        cotangent_pieces[-1],
        router_parts,
        out_own,
        normed_low,
        cosine_table,
        sine_table,
        allowed,
        out_order,
        cotangent_parts[0],
    ) = fence(
        (
            front_pieces[-1],
            cotangent_pieces[-1],
            router_parts,
            out_own,
            normed_low,
            cosine_table,
            sine_table,
            allowed,
            out_order,
            cotangent_parts[0],
        )
    )
    front_others.append(swap_core(front_pieces[-1]))
    router_parts = jnp.concatenate([shift_outer(router_parts, s) for s in range(outer)], axis=0)
    out_own = jnp.concatenate(out_own, axis=0)
    out_other = swap_core(out_own)
    cotangent_partner = swap_core(cotangent_pieces[1])
    for s in range(2, outer - 1):
        cotangent_pieces.append(shift_outer(cotangent_pieces[-1]))
    tile = 2 * width
    projected = call(
        project_kernel,
        shape((together, columns), f32),
        grid=(columns // tile,),
        in_specs=[pl.BlockSpec((together, model), lambda n: (0, 0))]
        + [pl.BlockSpec((chips * depth, tile), lambda n: (0, n))] * (CORES * outer),
        out_specs=pl.BlockSpec((together, tile), lambda n: (0, n)),
    )(normed_low, *front_pieces, *front_others)

    def blocks(columns_of):
        return pl.BlockSpec((count, columns_of), lambda b: (b, 0))

    once = pl.BlockSpec((1, width), lambda b: (0, 0))
    order_once = pl.BlockSpec((group_columns, group_columns), lambda b: (0, 0))
    query_low, key_low, value_low, context_low = call(
        functools.partial(attend_kernel, scale),
        (
            shape((together, group_columns), bf16),
            shape((together, width), bf16),
            shape((together, width), bf16),
            shape((together, group_columns), bf16),
        ),
        micros=13,
        grid=(chips,),
        in_specs=[
            blocks(columns),
            blocks(width),
            blocks(width),
            blocks(count),
            once,
            once,
            order_once,
        ],
        out_specs=[blocks(group_columns), blocks(width), blocks(width), blocks(group_columns)],
        scratch_shapes=[pltpu.VMEM((count, group_columns), bf16)],
    )(projected, cosine_table, sine_table, allowed, query_gain_row, key_gain_row, out_order)
    send_cotangent(after(cotangent_pieces[1], context_low), cotangent_partner)
    device = jnp.arange(shards, dtype=i32)
    came_from = ((my_outer - device // plane) % outer) * plane + (
        (device % plane) ^ (me % plane)
    )
    full_router = jnp.dot(
        (came_from[:, None] == device[None, :]).astype(bf16),
        router_parts,
        preferred_element_type=f32,
    )
    full_router = full_router.astype(bf16).reshape(model, experts)
    router_wide = jnp.pad(full_router, ((0, 0), (0, lanes - experts)))

    context_low, out_own, out_other, cotangent_pieces[-1], router_wide = fence(
        (context_low, out_own, out_other, cotangent_pieces[-1], router_wide)
    )
    context_own, context_other = context_low[:, :half_columns], context_low[:, half_columns:]

    def attended(first, last):
        return jnp.dot(
            context_own[first:last], out_own, preferred_element_type=f32
        ) + jnp.dot(context_other[first:last], out_other, preferred_element_type=f32)

    away = attended(count, together).astype(bf16)
    arrived = [swap_chip(away[(r - 1) * count : r * count], r) for r in range(1, chips)]
    home = attended(0, count)
    cotangent_pieces.append(shift_outer(cotangent_pieces[-1]))
    for s in range(2, outer - 1):
        send_cotangent(after(cotangent_pieces[s], away), swap_core(cotangent_pieces[s]))
    arrived, home, cotangent_pieces[-1], cotangent_parts = fence(
        (arrived, home, cotangent_pieces[-1], cotangent_parts)
    )
    send_cotangent(cotangent_pieces[-1], swap_core(cotangent_pieces[-1]))
    hidden, second_wide, prob, gates = call(
        functools.partial(router_kernel, experts),
        (
            shape((count, model), f32),
            shape((count, model + pair_width), bf16),
            shape((count, lanes), f32),
            shape((count, lanes), f32),
        ),
    )(tokens, home, *arrived, second_gain_row, router_wide, mask)

    gate_weight, up_weight, down_weight = expert_gate[0], expert_up[0], expert_down[0]
    hidden_units = gate_weight.shape[1]
    unit_tile = 2 * LANES

    def expert(came, given):
        part = pl.BlockSpec((part_rows, model + pair_width), lambda f: (0, 0))
        units = pl.BlockSpec((slots, unit_tile), lambda f: (0, f))
        outs = call(
            functools.partial(expert_kernel, chips, experts),
            [shape((part_rows, model + pair_width), bf16)] * chips
            + [shape((slots, hidden_units), bf16)] * 3,
            vmem=MORE_BYTES,
            micros=13,
            grid=(hidden_units // unit_tile,),
            in_specs=[smem]
            + [part] * chips
            + [pl.BlockSpec((part_rows, model), lambda f: (0, 0))] * chips
            + [pl.BlockSpec((model, unit_tile), lambda f: (0, f))] * 2
            + [pl.BlockSpec((unit_tile, model), lambda f: (f, 0))],
            out_specs=[part] * chips + [units] * 3,
            scratch_shapes=[
                pltpu.VMEM((slots, model), bf16),
                pltpu.VMEM((slots, model), bf16),
                pltpu.VMEM((slots, 1), f32),
                pltpu.VMEM((slots, 1), f32),
                pltpu.VMEM((slots, model), f32),
            ],
        )(me_scalar, *came, *given, gate_weight, up_weight, down_weight)
        return outs[:chips], (came, given, *outs[chips:])

    second_pieces = [second_wide]
    for s in range(1, outer):
        second_pieces.append(shift_outer(second_pieces[-1]))
    backs, kept = [], []
    sent = dispatch(picks[0], second_pieces[0], swap_core(second_pieces[0]))
    for s in range(outer):
        came = spread(sent)
        if s + 1 < outer:
            piece = second_pieces[s + 1]
            partner = swap_core(piece)
            if s:
                piece = after(piece, *backs[s - 1])
            sent = dispatch(picks[s + 1], piece, partner)
            came, sent, cotangent_parts = fence((came, sent, cotangent_parts))
        back, keep = expert(came, cotangent_parts[s])
        backs.append(back)
        kept.append(keep)

    returned, latest = {}, ()
    for s in [*range(1, outer), 0]:
        parts = spread(fence((backs[s], latest))[0])
        latest = tuple(parts[1:])
        own, partner = settle(picks[s], parts)
        returned[s] = (own, swap_core(partner))
    grad_own, grad_came = ring_reduce(
        lambda s: returned[s][0] + returned[s][1].astype(f32) if s else returned[0]
    )

    def move(s, *others):
        return call(move_kernel, [shape((part_rows, model), bf16)] * chips)(
            after(kept[s][2], *others), down_weight
        )

    moved = {s: spread(move(s, *latest)) for s in range(1, outer - 1)}

    grad_hidden, grad_hidden_low, grad_logits_low, second_gain_term = call(
        functools.partial(router_back_kernel, experts),
        (
            shape((count, model), f32),
            shape((count, model), bf16),
            shape((count, lanes), bf16),
            shape((1, model), f32),
        ),
    )(
        *grad_own,
        grad_came,
        cotangent,
        hidden,
        second_gain_row,
        router_wide,
        mask,
        prob,
        gates,
    )
    grad_attn_parts = gather_chips(grad_hidden_low)
    kept_late = [fence((keep, grad_hidden_low))[0] for keep in kept]
    total_slots = outer * slots
    row_tile = pl.BlockSpec((part_rows, unit_tile), lambda i: (0, i))
    unit_once = pl.BlockSpec((slots, hidden_units), lambda i: (0, 0))
    gate_grad, up_grad, down_grad = call(
        functools.partial(expert_grad_kernel, outer, chips),
        (
            shape((model, hidden_units), f32),
            shape((model, hidden_units), f32),
            shape((hidden_units, model), f32),
        ),
        vmem=MORE_BYTES,
        micros=18,
        grid=(model // unit_tile,),
        in_specs=[row_tile] * (2 * outer * chips) + [unit_once] * (3 * outer),
        out_specs=[
            pl.BlockSpec((unit_tile, hidden_units), lambda i: (i, 0)),
            pl.BlockSpec((unit_tile, hidden_units), lambda i: (i, 0)),
            pl.BlockSpec((hidden_units, unit_tile), lambda i: (0, i)),
        ],
        scratch_shapes=[pltpu.VMEM((total_slots, unit_tile), bf16)] * 2
        + [pltpu.VMEM((total_slots, hidden_units), bf16)] * 3,
    )(
        *[part for i in range(2) for keep in kept_late for part in keep[i]],
        *[keep[i] for i in range(2, 5) for keep in kept_late],
    )


    def settled(s, parts):
        own, partner = settle(picks[s], parts)
        return own + swap_core(partner).astype(f32)

    moved_step = shift_outer(settled(1, after(moved[1], gate_grad)).astype(bf16))
    (
        grad_attn_parts,
        gate_grad,
        up_grad,
        down_grad,
        moved,
    ) = fence((grad_attn_parts, gate_grad, up_grad, down_grad, moved))

    grad_attn_low = jnp.concatenate(grad_attn_parts, axis=0)
    out_send, out_keep = (
        lax.dot_general(
            context, grad_attn_low, CONTRACT_ROWS, preferred_element_type=f32
        ).astype(bf16)
        for context in (context_other, context_own)
    )
    out_swapped = swap_core(out_send)
    grad_context_own, grad_context_other = (
        lax.dot_general(
            grad_attn_low, weight, CONTRACT_LAST, preferred_element_type=f32
        ).astype(bf16)
        for weight in (out_own, out_other)
    )
    out_half = (out_keep.astype(f32) + out_swapped.astype(f32)).astype(bf16)
    out_half = out_half.reshape(chips, span * rows_out, model)
    out_came = [swap_chip(out_half[r], r) for r in range(chips)]
    grad_context_own = after(grad_context_own, out_half)
    for s in range(2, outer - 1):
        moved_step = shift_outer((moved_step.astype(f32) + settled(s, moved[s])).astype(bf16))
    moved_last = spread(move(outer - 1, grad_context_other))
    grad_front_low, gain_terms = call(
        functools.partial(attend_back_kernel, scale),
        (shape((together, columns), bf16), shape((2, width), f32)),
        micros=18,
        grid=(chips,),
        in_specs=[
            blocks(columns),
            blocks(group_columns),
            blocks(width),
            blocks(width),
            blocks(half_columns),
            blocks(half_columns),
            blocks(width),
            blocks(width),
            blocks(count),
            once,
            once,
            order_once,
        ],
        out_specs=[blocks(columns), pl.BlockSpec((2, width), lambda b: (0, 0))],
        scratch_shapes=[pltpu.VMEM((count, group_columns), bf16)],
    )(
        projected,
        query_low,
        key_low,
        value_low,
        grad_context_own,
        grad_context_other,
        cosine_table,
        sine_table,
        allowed,
        query_gain_row,
        key_gain_row,
        out_order,
    )

    grad_front_low, gain_terms, out_came, moved_last, moved_step = fence(
        (grad_front_low, gain_terms, out_came, moved_last, moved_step)
    )

    half_model = model // CORES
    front_send, front_keep = (
        lax.dot_general(
            normed_low[:, k * half_model : (k + 1) * half_model],
            grad_front_low,
            CONTRACT_ROWS,
            preferred_element_type=f32,
        ).astype(bf16)
        for k in (1, 0)
    )
    front_half = (front_keep.astype(f32) + swap_core(front_send).astype(f32)).astype(bf16)
    front_half = front_half.reshape(outer, chips * depth, columns)
    moved_step = shift_outer(
        (moved_step.astype(f32) + settled(outer - 1, moved_last)).astype(bf16)
    )
    out_whole = jnp.stack(out_came).reshape(outer, rows_out, model)
    router_part = lax.dot_general(
        after(grad_logits_low, front_send)[:, :experts],
        second_wide[:, :model],
        CONTRACT_ROWS,
        preferred_element_type=f32,
    )
    router_part = scatter_outer(
        lambda o: lax.dynamic_slice_in_dim(router_part, o * (plane * depth), plane * depth, 1)
    )

    def out_slice(s):
        target = (my_outer - s) % outer
        return lax.dynamic_index_in_dim(
            out_whole, ((target // span) ^ my_chip) * span + target % span, 0, keepdims=False
        )

    def next_step(step, part):
        return shift_outer((step.astype(f32) + part.astype(f32)).astype(bf16))

    out_first = out_slice(1)
    front_half, grad_front_late, out_first = fence((front_half, grad_front_low, out_first))
    front_step, out_step = shift_outer(front_half[1]), shift_outer(out_first)
    piece_block = pl.BlockSpec((1, chips * depth, columns), lambda s, o: (s, 0, 0))
    grad_normed = pl.pallas_call(
        project_back_kernel,
        out_shape=shape((together, model), bf16),
        grid_spec=pltpu.PrefetchScalarGridSpec(
            num_scalar_prefetch=1,
            grid=(outer,),
            in_specs=[
                pl.BlockSpec((together, columns), lambda s, o: (0, 0)),
                piece_block,
                piece_block,
                pl.BlockSpec((plane * depth, plane * depth), lambda s, o: (0, 0)),
            ],
            out_specs=pl.BlockSpec(
                (together, plane * depth), lambda s, o: (0, lax.rem(o[0] + outer - s, outer))
            ),
        ),
        compiler_params=pltpu.CompilerParams(vmem_limit_bytes=VMEM_BYTES),
    )(
        outer_scalar,
        grad_front_late,
        jnp.stack(front_pieces),
        jnp.stack(front_others),
        front_order,
    )
    came = [swap_chip(grad_normed[r * count : (r + 1) * count], r) for r in range(1, chips)]
    grad_home = grad_normed[:count]
    front_step, out_step, came, grad_home, moved_step, router_part = fence(
        (front_step, out_step, came, grad_home, moved_step, router_part)
    )
    for s in range(2, outer):
        front_step = next_step(front_step, front_half[s])
        out_step = next_step(out_step, out_slice(s))
        if s == 2:
            moved_home = spread(move(0, moved_step))
            tokens_grad, first_gain_term = call(
                tokens_back_kernel,
                (shape((count, model), f32), shape((1, model), f32)),
            )(tokens, grad_home, *came, grad_hidden, first_gain_row)
            gain_sums = jnp.concatenate(
                [first_gain_term.reshape(-1), second_gain_term.reshape(-1), gain_terms.reshape(-1)]
            ).reshape(-1, LANES)
            gain_sums = gain_sums + swap_core(gain_sums)
            router_part = sum(
                [
                    swap_chip(
                        lax.dynamic_slice_in_dim(
                            router_part, (my_chip ^ r) * (CORES * depth), CORES * depth, 1
                        ),
                        r,
                    )
                    for r in range(chips)
                ]
            )
            front_step, out_step, moved_home, gain_sums, tokens_grad, router_part = fence(
                (front_step, out_step, moved_home, gain_sums, tokens_grad, router_part)
            )
            router_grad = (
                lax.dynamic_slice_in_dim(router_part, my_core * depth, depth, 1)
                + swap_core(lax.dynamic_slice_in_dim(router_part, (1 - my_core) * depth, depth, 1))
            ).T
            gain_sums = sum([swap_chip(gain_sums, r) for r in range(1, chips)], gain_sums)
            output = (hidden + settled(0, moved_home) + moved_step.astype(f32)).astype(bf16)
        else:
            front_step, out_step = fence((front_step, out_step))
    gain_sums, output, front_step, out_step = fence((gain_sums, output, front_step, out_step))
    gain_sums = sum([shift_outer(gain_sums, s) for s in range(1, outer)], gain_sums).reshape(-1)
    front = (front_step.astype(f32) + front_half[0].astype(f32)).astype(bf16)
    front = front.reshape(chips, depth, columns)
    front = by_chip([swap_chip(front[r], r) for r in range(chips)])
    out_grad = out_step.astype(f32) + out_slice(0).astype(f32)

    def lay_out(first, last):
        return jnp.concatenate([part[:, first:last] for part in front], axis=1).astype(f32)

    query_grad = lay_out(0, group_columns)
    key_grad = lay_out(group_columns, group_columns + width)
    value_grad = lay_out(group_columns + width, columns)
    return (
        output,
        tokens_grad,
        query_grad,
        key_grad,
        value_grad,
        out_grad,
        router_grad,
        gate_grad[None],
        up_grad[None],
        down_grad[None],
        gain_sums[:model],
        gain_sums[model : 2 * model],
        gain_sums[2 * model : 2 * model + width],
        gain_sums[2 * model + width :],
    )


def solution(mesh):
    rows = P("fsdp", None)
    blocks = P("fsdp", None, None)
    placed = (rows,) * 9 + (blocks,) * 3 + (P(),) * 4
    return jax.shard_map(
        body,
        mesh=mesh,
        in_specs=placed,
        out_specs=(rows,) * 7 + (blocks,) * 3 + (P(),) * 4,
        check_vma=False,
    )
```

time: 1060 us -> 733 us (0.69)
  Pallas kernels: 0 us -> 146 us
  waiting for transfers between devices: 457 us -> 311 us
  matrix products: 168 us -> 24.2 us
  blocking collectives: 67 us -> 0 us
  other arithmetic: 75.1 us -> 33.5 us
  local copies, waits for them, and re-layouts: 106 us -> 67.1 us
  starting transfers between devices: 162 us -> 138 us
  between operations: 16.4 us -> 3.65 us
    ppermute x18 -> x84, waiting for transfers between devices: 35.2 us -> 204 us  [swap_chip(): lax.ppermute(value, 'fsdp', [(i, i ^ r * CORES) for i in range(shards)])]
    pallas_call x0 -> x33, Pallas kernels: none -> 146 us  [the longest x4 53.4 us: expert(): call(functools.partial(expert_kernel, chips, experts), [shape((part_rows,...]
    dot_general x61 -> x12, matrix products: 167 us -> 24.2 us  [the longest x2 5.79 us: body(): lax.dot_general(grad_attn_low, weight, CONTRACT_LAST, preferred_element_t...]
    ppermute x27 -> x33, waiting for transfers between devices: 224 us -> 107 us  [shift_outer(): lax.ppermute(value, 'fsdp', [(i, (i // plane + s) % outer * plane + i % p...]
    unnamed x2 -> x0, waiting for transfers between devices: 109 us -> none
    all_to_all x20 -> x0, waiting for transfers between devices: 88.4 us -> none  [exchange(): lax.all_to_all(value, 'fsdp', split_axis=0, concat_axis=0, tiled=True, ax...]
    all_to_all x20 -> x0, starting transfers between devices: 86.1 us -> none  [exchange(): lax.all_to_all(value, 'fsdp', split_axis=0, concat_axis=0, tiled=True, ax...]
    ppermute x18 -> x84, starting transfers between devices: 20.6 us -> 104 us  [swap_chip(): lax.ppermute(value, 'fsdp', [(i, i ^ r * CORES) for i in range(shards)])]
  transfers between devices with their start and end apart: 74 -> 143, of which waited for: 34 -> 52; matrix products, arithmetic and copies ran while one was open for 27% -> 9% of each run, Pallas kernels for 0% -> 20%
where the time goes in v2:
time: 733 us; the launch traced here: 724 us
  waiting for transfers between devices  311 us (42%)
  Pallas kernels  146 us (20%)
  starting transfers between devices  138 us (19%)
  local copies, waits for them, and re-layouts  67.1 us (9%)
  other arithmetic  33.5 us (5%)
  matrix products  24.2 us (3%)
    ppermute x84, waiting for transfers between devices, swap_chip(): lax.ppermute(value, 'fsdp', [(i, i ^ r * CORES) for i in range(shards)])  204 us
    ppermute x33, waiting for transfers between devices, shift_outer(): lax.ppermute(value, 'fsdp', [(i, (i // plane + s) % outer * plane + i % p...  107 us
    ppermute x84, starting transfers between devices, swap_chip(): lax.ppermute(value, 'fsdp', [(i, i ^ r * CORES) for i in range(shards)])  104 us
    pallas_call x4, Pallas kernels, expert(): call(functools.partial(expert_kernel, chips, experts), [shape((part_rows,...  53.4 us
    unnamed x346, local copies, waits for them, and re-layouts  53.3 us
    ppermute x33, starting transfers between devices, shift_outer(): lax.ppermute(value, 'fsdp', [(i, (i // plane + s) % outer * plane + i % p...  30.6 us
    pallas_call x1, Pallas kernels, body(): call(functools.partial(expert_grad_kernel, outer, chips), (shape((model,...  21 us
    pallas_call x1, Pallas kernels, body(): call(functools.partial(attend_back_kernel, scale), (shape((together, colu...  18.6 us
  transfers between devices with their start and end apart: 143, of which 52 were waited for; matrix products, arithmetic and copies ran while one was open for 9% of the time, Pallas kernels for 20%

profile of v2, /device:TPU:0, one launch (start us, length us, event | category | flops | bytes accessed | tf_op | source)
XLA Modules:
  0.0 724.4 jit_solution(10438435433821867432)
XLA Ops:
  15.8 7.6 %collective-permute-done.3 = bf16[128,2048]{1,0:T(8,128)(2,1)} collective-permute-done((bf16[128,2048]{1,0:T(8,128)(2,1)S(1)}, bf16[128,2048]{1,0:T(8,128)(2,1)}, u32[]{:S(2)}, u32[]{:S(2)}) %collective-permute-start.3) | collective-permute-done | bytes 524320 | tf_op jit(solution)/shard_map/ppermute | solution.py:502
  30.9 28.2 %collective-permute-done.5 = bf16[128,2048]{1,0:T(8,128)(2,1)} collective-permute-done((bf16[128,2048]{1,0:T(8,128)(2,1)}, bf16[128,2048]{1,0:T(8,128)(2,1)}, u32[]{:S(2)}, u32[]{:S(2)}) %collective-permute-start.5) | collective-permute-done | bytes 524320 | tf_op jit(solution)/shard_map/ppermute | solution.py:502
  70.1 18.6 %collective-permute-done.8 = bf16[128,2048]{1,0:T(8,128)(2,1)S(1)} collective-permute-done((bf16[128,2048]{1,0:T(8,128)(2,1)}, bf16[128,2048]{1,0:T(8,128)(2,1)S(1)}, u32[]{:S(2)}, u32[]{:S(2)}) %collective-permute-start.8) | collective-permute-done | bytes 524320 | tf_op jit(solution)/shard_map/ppermute | solution.py:502
  117.7 10.0 %collective-permute-done.16 = bf16[128,2048]{1,0:T(8,128)(2,1)S(1)} collective-permute-done((bf16[128,2048]{1,0:T(8,128)(2,1)S(1)}, bf16[128,2048]{1,0:T(8,128)(2,1)S(1)}, u32[]{:S(2)}, u32[]{:S(2)}) %collective-permute-start.16) | collective-permute-done | bytes 524320 | tf_op jit(solution)/shard_map/ppermute | solution.py:497
  151.6 13.5 %shard_map.266 = (bf16[512,1024]{1,0:T(8,128)(2,1)S(1)}, bf16[512,128]{1,0:T(8,128)(2,1)S(1)}, bf16[512,128]{1,0:T(8,128)(2,1)S(1)}, bf16[512,1024]{1,0:T(8,128)(2,1)S(1)}) custom-call(f32[512,1280]{1,0:T(8,128)S(1)} %shard_map.265.front, f32[512,128]{1,0:T(8,128)S(1)} %copy-done.59, f32[512,128]{1,0:T(8,128)S(1)} %copy-done.61, f32[512,128]{1,0:T(8,128)S(1)} %copy-done.63, ...), custom_call_target="tpu_custom_call" | custom-call | flops 12999999488 | bytes 26000000 | tf_op jit(solution)/shard_map/pallas_call | solution.py:717
  185.7 12.7 %collective-permute-done.43.refs_7_.refs_23_ = bf16[80,2048]{1,0:T(8,128)(2,1)S(1)} collective-permute-done((bf16[80,2048]{1,0:T(8,128)(2,1)S(1)}, bf16[80,2048]{1,0:T(8,128)(2,1)S(1)}, u32[]{:S(2)}, u32[]{:S(2)}) %collective-permute-start.43) | collective-permute-done | bytes 327712 | tf_op jit(solution)/shard_map/ppermute | solution.py:497
  200.3 8.8 %collective-permute-done.37.refs_3_ = bf16[128,2048]{1,0:T(8,128)(2,1)S(1)} collective-permute-done((bf16[128,2048]{1,0:T(8,128)(2,1)S(1)}, bf16[128,2048]{1,0:T(8,128)(2,1)S(1)}, u32[]{:S(2)}, u32[]{:S(2)}) %collective-permute-start.37) | collective-permute-done | bytes 524320 | tf_op jit(solution)/shard_map/ppermute | solution.py:497
  216.6 6.7 collective-permute-done.46.refs_6_.refs_26_
  226.8 15.5 %collective-permute-done.52.own = bf16[128,2176]{1,0:T(8,128)(2,1)S(1)} collective-permute-done((bf16[128,2176]{1,0:T(8,128)(2,1)S(1)}, bf16[128,2176]{1,0:T(8,128)(2,1)S(1)}, u32[]{:S(2)}, u32[]{:S(2)}) %collective-permute-start.52) | collective-permute-done | bytes 557088 | tf_op jit(solution)/shard_map/ppermute | solution.py:502
  246.8 7.6 %collective-permute-done.55.refs_5_.refs_29_ = bf16[80,2048]{1,0:T(8,128)(2,1)S(1)} collective-permute-done((bf16[80,2048]{1,0:T(8,128)(2,1)S(1)}, bf16[80,2048]{1,0:T(8,128)(2,1)S(1)}, u32[]{:S(2)}, u32[]{:S(2)}) %collective-permute-start.55) | collective-permute-done | bytes 327712 | tf_op jit(solution)/shard_map/ppermute | solution.py:497
  260.5 15.3 %collective-permute-done.57.refs_7_.refs_31_ = bf16[80,2048]{1,0:T(8,128)(2,1)S(1)} collective-permute-done((bf16[80,2048]{1,0:T(8,128)(2,1)S(1)}, bf16[80,2048]{1,0:T(8,128)(2,1)S(1)}, u32[]{:S(2)}, u32[]{:S(2)}) %collective-permute-start.57) | collective-permute-done | bytes 327712 | tf_op jit(solution)/shard_map/ppermute | solution.py:497
  285.5 13.1 %shard_map.273 = (bf16[80,2176]{1,0:T(8,128)(2,1)S(1)}, bf16[80,2176]{1,0:T(8,128)(2,1)S(1)}, bf16[80,2176]{1,0:T(8,128)(2,1)S(1)}, bf16[80,2176]{1,0:T(8,128)(2...) custom-call(s32[1]{0:T(128)} %bitcast.35.me, ...), custom_call_target="tpu_custom_call" | custom-call | flops 12999999488 | bytes 26000000 | tf_op jit(solution)/shard_map/pallas_call | solution.py:789
  306.1 13.9 %shard_map.275 = (bf16[80,2176]{1,0:T(8,128)(2,1)S(1)}, bf16[80,2176]{1,0:T(8,128)(2,1)S(1)}, bf16[80,2176]{1,0:T(8,128)(2,1)}, bf16[80,2176]{1,0:T(8,128)(2,1)S...) custom-call(s32[1]{0:T(128)} %bitcast.35.me, bf16[80,2176]{1,0:T(8,128)(2,1)S(1)} %copy-done.73, ...), custom_call_target="tpu_custom_call" | custom-call | flops 12999999488 | bytes 26000000 | tf_op jit(solution)/shard_map/pallas_call | solution.py:789
  331.3 8.7 %collective-permute-done.72.refs_2_ = bf16[80,2176]{1,0:T(8,128)(2,1)S(1)} collective-permute-done((bf16[80,2176]{1,0:T(8,128)(2,1)}, bf16[80,2176]{1,0:T(8,128)(2,1)S(1)}, u32[]{:S(2)}, u32[]{:S(2)}) %collective-permute-start.72) | collective-permute-done | bytes 348192 | tf_op jit(solution)/shard_map/ppermute | solution.py:497
  346.0 8.2 %collective-permute-done.64.refs_2_.refs_10_ = bf16[80,2176]{1,0:T(8,128)(2,1)S(1)} collective-permute-done((bf16[80,2176]{1,0:T(8,128)(2,1)}, bf16[80,2176]{1,0:T(8,128)(2,1)S(1)}, u32[]{:S(2)}, u32[]{:S(2)}) %collective-permute-start.64) | collective-permute-done | bytes 348192 | tf_op jit(solution)/shard_map/ppermute | solution.py:497
  357.1 13.2 %shard_map.278 = (bf16[80,2176]{1,0:T(8,128)(2,1)S(1)}, bf16[80,2176]{1,0:T(8,128)(2,1)S(1)}, bf16[80,2176]{1,0:T(8,128)(2,1)S(1)}, bf16[80,2176]{1,0:T(8,128)(2...) custom-call(s32[1]{0:T(128)} %bitcast.35.me, ...), custom_call_target="tpu_custom_call" | custom-call | flops 12999999488 | bytes 26000000 | tf_op jit(solution)/shard_map/pallas_call | solution.py:789
  374.6 6.8 collective-permute-done.74.refs_1_
  389.9 6.5 collective-permute-done.68.refs_1_.refs_13_
  396.4 6.5 collective-permute-done.69.refs_2_.refs_14_
  406.0 13.2 %shard_map.277 = (bf16[80,2176]{1,0:T(8,128)(2,1)S(1)}, bf16[80,2176]{1,0:T(8,128)(2,1)S(1)}, bf16[80,2176]{1,0:T(8,128)(2,1)S(1)}, bf16[80,2176]{1,0:T(8,128)(2...) custom-call(s32[1]{0:T(128)} %bitcast.35.me, ...), custom_call_target="tpu_custom_call" | custom-call | flops 12999999488 | bytes 26000000 | tf_op jit(solution)/shard_map/pallas_call | solution.py:789
  422.9 7.6 %collective-permute-done.77.refs_1_ = bf16[80,2176]{1,0:T(8,128)(2,1)S(1)} collective-permute-done((bf16[80,2176]{1,0:T(8,128)(2,1)S(1)}, bf16[80,2176]{1,0:T(8,128)(2,1)S(1)}, u32[]{:S(2)}, u32[]{:S(2)}) %collective-permute-start.77) | collective-permute-done | bytes 348192 | tf_op jit(solution)/shard_map/ppermute | solution.py:497
  430.5 6.8 collective-permute-done.78.refs_2_
  443.1 7.5 %collective-permute-done.80.refs_1_ = bf16[80,2176]{1,0:T(8,128)(2,1)S(1)} collective-permute-done((bf16[80,2176]{1,0:T(8,128)(2,1)S(1)}, bf16[80,2176]{1,0:T(8,128)(2,1)S(1)}, u32[]{:S(2)}, u32[]{:S(2)}) %collective-permute-start.80) | collective-permute-done | bytes 348192 | tf_op jit(solution)/shard_map/ppermute | solution.py:497
  450.6 7.1 collective-permute-done.81.refs_2_
  500.2 21.0 %shard_map.284 = (f32[2048,768]{1,0:T(8,128)}, f32[2048,768]{1,0:T(8,128)}, f32[768,2048]{1,0:T(8,128)}) custom-call(bf16[80,2176]{1,0:T(8,128)(2,1)} %copy-done.68, bf16[80,2176]{1,0:T(8,128)(2,1)} %copy-done.69, bf16[80,2176]{1,0:T(8,128)(2,1)} %copy-done.70, bf16[80,2176]{1,0:T(8,128)(2,1)} %copy-done.71, bf16[80,2176]{1,0:T(8,128)(2,1)} %copy-done.72, ...), custom_call_target="tpu_custom_call" | custom-call | flops 17999998976 | bytes 36000000 | tf_op jit(solution)/shard_map/pallas_call | solution.py:871
  558.9 18.6 %shard_map.287 = (bf16[512,1280]{1,0:T(8,128)(2,1)S(1)}, f32[2,128]{1,0:T(2,128)S(1)}) custom-call(f32[512,1280]{1,0:T(8,128)S(1)} %shard_map.265.front, bf16[512,1024]{1,0:T(8,128)(2,1)S(1)} %copy-done.140, bf16[512,128]{1,0:T(8,128)(2,1)S(1)} %copy-done.142, bf16[512,128]{1,0:T(8,128)(2,1)S(1)} %copy-done.144, ...), custom_call_target="tpu_custom_call" | custom-call | flops 17999998976 | bytes 36000000 | tf_op jit(solution)/shard_map/pallas_call | solution.py:929
  613.9 10.0 %collective-permute-done.113.refs_0_ = bf16[128,2048]{1,0:T(8,128)(2,1)} collective-permute-done((bf16[128,2048]{1,0:T(8,128)(2,1)}, bf16[128,2048]{1,0:T(8,128)(2,1)}, u32[]{:S(2)}, u32[]{:S(2)}) %collective-permute-start.113) | collective-permute-done | bytes 524320 | tf_op jit(solution)/shard_map/ppermute | solution.py:497
  623.9 10.4 %collective-permute-done.114.refs_1_ = bf16[128,2048]{1,0:T(8,128)(2,1)} collective-permute-done((bf16[128,2048]{1,0:T(8,128)(2,1)}, bf16[128,2048]{1,0:T(8,128)(2,1)}, u32[]{:S(2)}, u32[]{:S(2)}) %collective-permute-start.114) | collective-permute-done | bytes 524320 | tf_op jit(solution)/shard_map/ppermute | solution.py:497
  655.3 7.1 collective-permute-done.123.refs_1_
  662.4 6.6 collective-permute-done.124.refs_2_
  683.1 10.5 %collective-permute-done.135 = bf16[128,2048]{1,0:T(8,128)(2,1)S(1)} collective-permute-done((bf16[128,2048]{1,0:T(8,128)(2,1)S(1)}, bf16[128,2048]{1,0:T(8,128)(2,1)S(1)}, u32[]{:S(2)}, u32[]{:S(2)}) %collective-permute-start.135) | collective-permute-done | bytes 524320 | tf_op jit(solution)/shard_map/ppermute | solution.py:502
  693.7 13.2 %collective-permute-done.134 = bf16[256,1280]{1,0:T(8,128)(2,1)S(1)} collective-permute-done((bf16[256,1280]{1,0:T(8,128)(2,1)S(1)}, bf16[256,1280]{1,0:T(8,128)(2,1)S(1)}, u32[]{:S(2)}, u32[]{:S(2)}) %collective-permute-start.134) | collective-permute-done | bytes 655392 | tf_op jit(solution)/shard_map/ppermute | solution.py:502
  (743 shorter events, 359.6 us)
Async XLA Ops:
  27.2 63.6 %collective-permute-start.17 = (bf16[128,2048]{1,0:T(8,128)(2,1)S(1)}, bf16[128,2048]{1,0:T(8,128)(2,1)S(1)}, u32[]{:S(2)}, u32[]{:S(2)}) collective-permute-start(bf16[128,2048]{1,0:T(8,128)(2,1)S(1)} %copy-done.5), channel_id=1, source_target_pairs={{0,2},{1,3},{2,0},{3,1},{4,6},{5,7},{6,4},{7,5},{8,10},{9,11},{10,... | collective-permute-start | bytes 1572872 | tf_op jit(solution)/shard_map/ppermute | solution.py:497
  28.8 30.3 %collective-permute-start.4 = (bf16[256,1280]{1,0:T(8,128)(2,1)S(1)}, bf16[256,1280]{1,0:T(8,128)(2,1)}, u32[]{:S(2)}, u32[]{:S(2)}) collective-permute-start(bf16[256,1280]{1,0:T(8,128)(2,1)S(1)} %pad_maximum_fusion.4.refs_0_), channel_id=1, source_target_pairs={{0,8},{1,9},{2,10},{3,11},{4,12},{5,13},{6,14},{7,15},{8,16},{9,17... | collective-permute-start | bytes 1966088 | tf_op jit(solution)/shard_map/ppermute | solution.py:502
  29.5 29.6 %collective-permute-start.5 = (bf16[128,2048]{1,0:T(8,128)(2,1)}, bf16[128,2048]{1,0:T(8,128)(2,1)}, u32[]{:S(2)}, u32[]{:S(2)}) collective-permute-start(bf16[128,2048]{1,0:T(8,128)(2,1)} %collective-permute-done.3), channel_id=1, source_target_pairs={{0,8},{1,9},{2,10},{3,11},{4,12},{5,13},{6,14},{7,15},{8,16},{9,17... | collective-permute-start | bytes 1572872 | tf_op jit(solution)/shard_map/ppermute | solution.py:502
  30.5 30.7 %collective-permute-start.23 = (bf16[128,2176]{1,0:T(8,128)(2,1)}, bf16[128,2176]{1,0:T(8,128)(2,1)S(1)}, u32[]{:S(2)}, u32[]{:S(2)}) collective-permute-start(bf16[128,2176]{1,0:T(8,128)(2,1)} %pad_maximum_fusion.6.own), channel_id=1, source_target_pairs={{0,1},{1,0},{2,3},{3,2},{4,5},{5,4},{6,7},{7,6},{8,9},{9,8},{10,11... | collective-permute-start | bytes 1671176 | tf_op jit(solution)/shard_map/ppermute | solution.py:492
  59.1 30.1 %collective-permute-start.7 = (bf16[256,1280]{1,0:T(8,128)(2,1)}, bf16[256,1280]{1,0:T(8,128)(2,1)}, u32[]{:S(2)}, u32[]{:S(2)}) collective-permute-start(bf16[256,1280]{1,0:T(8,128)(2,1)} %collective-permute-done.4.refs_1_), channel_id=1, source_target_pairs={{0,8},{1,9},{2,10},{3,11},{4,12},{5,13},{6,14},{7,15},{8,16},{9,17... | collective-permute-start | bytes 1966088 | tf_op jit(solution)/shard_map/ppermute | solution.py:502
  61.2 27.5 %collective-permute-start.8 = (bf16[128,2048]{1,0:T(8,128)(2,1)}, bf16[128,2048]{1,0:T(8,128)(2,1)S(1)}, u32[]{:S(2)}, u32[]{:S(2)}) collective-permute-start(bf16[128,2048]{1,0:T(8,128)(2,1)} %collective-permute-done.5), channel_id=1, source_target_pairs={{0,8},{1,9},{2,10},{3,11},{4,12},{5,13},{6,14},{7,15},{8,16},{9,17... | collective-permute-start | bytes 1572872 | tf_op jit(solution)/shard_map/ppermute | solution.py:502
  62.8 30.9 %collective-permute-start.18 = (bf16[128,2048]{1,0:T(8,128)(2,1)S(1)}, bf16[128,2048]{1,0:T(8,128)(2,1)S(1)}, u32[]{:S(2)}, u32[]{:S(2)}) collective-permute-start(bf16[128,2048]{1,0:T(8,128)(2,1)S(1)} %copy-done.5), channel_id=1, source_target_pairs={{0,4},{1,5},{2,6},{3,7},{4,0},{5,1},{6,2},{7,3},{8,12},{9,13},{10,... | collective-permute-start | bytes 1572872 | tf_op jit(solution)/shard_map/ppermute | solution.py:497
  69.0 25.0 %collective-permute-start.19 = (bf16[128,2048]{1,0:T(8,128)(2,1)S(1)}, bf16[128,2048]{1,0:T(8,128)(2,1)S(1)}, u32[]{:S(2)}, u32[]{:S(2)}) collective-permute-start(bf16[128,2048]{1,0:T(8,128)(2,1)S(1)} %copy-done.5), channel_id=1, source_target_pairs={{0,6},{1,7},{2,4},{3,5},{4,2},{5,3},{6,0},{7,1},{8,14},{9,15},{10,... | collective-permute-start | bytes 1572872 | tf_op jit(solution)/shard_map/ppermute | solution.py:497
  93.7 34.0 %collective-permute-start.12 = (bf16[256,1280]{1,0:T(8,128)(2,1)}, bf16[256,1280]{1,0:T(8,128)(2,1)}, u32[]{:S(2)}, u32[]{:S(2)}) collective-permute-start(bf16[256,1280]{1,0:T(8,128)(2,1)} %collective-permute-done.7.refs_2_), channel_id=1, source_target_pairs={{0,8},{1,9},{2,10},{3,11},{4,12},{5,13},{6,14},{7,15},{8,16},{9,17... | collective-permute-start | bytes 1966088 | tf_op jit(solution)/shard_map/ppermute | solution.py:502
  131.1 40.1 %collective-permute-start.31 = (bf16[512,2048]{1,0:T(8,128)(2,1)}, bf16[512,2048]{1,0:T(8,128)(2,1)}, u32[]{:S(2)}, u32[]{:S(2)}) collective-permute-start(bf16[512,2048]{1,0:T(8,128)(2,1)} %constant_dynamic-update-slice_fusion), channel_id=1, source_target_pairs={{0,1},{1,0},{2,3},{3,2},{4,5},{5,4},{6,7},{7,6},{8,9},{9,8},{10,11... | collective-permute-start | bytes 6291464 | tf_op jit(solution)/shard_map/ppermute | solution.py:492
  143.8 27.3 %collective-permute-start.32 = (bf16[128,2176]{1,0:T(8,128)(2,1)}, bf16[128,2176]{1,0:T(8,128)(2,1)S(1)}, u32[]{:S(2)}, u32[]{:S(2)}) collective-permute-start(bf16[128,2176]{1,0:T(8,128)(2,1)} %copy-done.29), channel_id=1, source_target_pairs={{0,8},{1,9},{2,10},{3,11},{4,12},{5,13},{6,14},{7,15},{8,16},{9,17... | collective-permute-start | bytes 1671176 | tf_op jit(solution)/shard_map/ppermute | solution.py:502
  177.0 32.1 %collective-permute-start.37 = (bf16[128,2048]{1,0:T(8,128)(2,1)S(1)}, bf16[128,2048]{1,0:T(8,128)(2,1)S(1)}, u32[]{:S(2)}, u32[]{:S(2)}) collective-permute-start(bf16[128,2048]{1,0:T(8,128)(2,1)S(1)} %get-tuple-element.735), channel_id=1, source_target_pairs={{0,4},{1,5},{2,6},{3,7},{4,0},{5,1},{6,2},{7,3},{8,12},{9,13},{10,... | collective-permute-start | bytes 1572872 | tf_op jit(solution)/shard_map/ppermute | solution.py:497
  181.3 31.9 %collective-permute-start.39 = (bf16[128,2176]{1,0:T(8,128)(2,1)S(1)}, bf16[128,2176]{1,0:T(8,128)(2,1)S(1)}, u32[]{:S(2)}, u32[]{:S(2)}) collective-permute-start(bf16[128,2176]{1,0:T(8,128)(2,1)S(1)} %collective-permute-done.32.own), channel_id=1, source_target_pairs={{0,8},{1,9},{2,10},{3,11},{4,12},{5,13},{6,14},{7,15},{8,16},{9,17... | collective-permute-start | bytes 1671176 | tf_op jit(solution)/shard_map/ppermute | solution.py:502
  181.6 31.5 %collective-permute-start.38 = (bf16[128,2048]{1,0:T(8,128)(2,1)S(1)}, bf16[128,2048]{1,0:T(8,128)(2,1)S(1)}, u32[]{:S(2)}, u32[]{:S(2)}) collective-permute-start(bf16[128,2048]{1,0:T(8,128)(2,1)S(1)} %get-tuple-element.734), channel_id=1, source_target_pairs={{0,6},{1,7},{2,4},{3,5},{4,2},{5,3},{6,0},{7,1},{8,14},{9,15},{10,... | collective-permute-start | bytes 1572872 | tf_op jit(solution)/shard_map/ppermute | solution.py:497
  245.8 36.7 %collective-permute-start.61 = (bf16[128,2176]{1,0:T(8,128)(2,1)S(1)}, bf16[128,2176]{1,0:T(8,128)(2,1)S(1)}, u32[]{:S(2)}, u32[]{:S(2)}) collective-permute-start(bf16[128,2176]{1,0:T(8,128)(2,1)S(1)} %collective-permute-done.52.own), channel_id=1, source_target_pairs={{0,8},{1,9},{2,10},{3,11},{4,12},{5,13},{6,14},{7,15},{8,16},{9,17... | collective-permute-start | bytes 1671176 | tf_op jit(solution)/shard_map/ppermute | solution.py:502
  246.4 30.1 %collective-permute-start.49 = (bf16[80,2176]{1,0:T(8,128)(2,1)S(1)}, bf16[80,2176]{1,0:T(8,128)(2,1)S(1)}, u32[]{:S(2)}, u32[]{:S(2)}) collective-permute-start(bf16[80,2176]{1,0:T(8,128)(2,1)S(1)} %get-tuple-element.426), channel_id=1, source_target_pairs={{0,2},{1,3},{2,0},{3,1},{4,6},{5,7},{6,4},{7,5},{8,10},{9,11},{10,... | collective-permute-start | bytes 1044488 | tf_op jit(solution)/shard_map/ppermute | solution.py:497
  340.8 41.2 %collective-permute-start.84 = (bf16[128,2176]{1,0:T(8,128)(2,1)S(1)}, bf16[128,2176]{1,0:T(8,128)(2,1)S(1)}, u32[]{:S(2)}, u32[]{:S(2)}) collective-permute-start(bf16[128,2176]{1,0:T(8,128)(2,1)S(1)} %get-tuple-element.556), channel_id=1, source_target_pairs={{0,1},{1,0},{2,3},{3,2},{4,5},{5,4},{6,7},{7,6},{8,9},{9,8},{10,11... | collective-permute-start | bytes 1671176 | tf_op jit(solution)/shard_map/ppermute | solution.py:492
  387.7 50.5 %collective-permute-start.85 = (bf16[128,2176]{1,0:T(8,128)(2,1)S(1)}, bf16[128,2176]{1,0:T(8,128)(2,1)S(1)}, u32[]{:S(2)}, u32[]{:S(2)}) collective-permute-start(bf16[128,2176]{1,0:T(8,128)(2,1)S(1)} %add_convert_fusion.5), channel_id=1, source_target_pairs={{0,8},{1,9},{2,10},{3,11},{4,12},{5,13},{6,14},{7,15},{8,16},{9,17... | collective-permute-start | bytes 1671176 | tf_op jit(solution)/shard_map/ppermute | solution.py:502
  389.8 48.4 %collective-permute-start.86 = (bf16[128,2176]{1,0:T(8,128)(2,1)S(1)}, bf16[128,2176]{1,0:T(8,128)(2,1)}, u32[]{:S(2)}, u32[]{:S(2)}) collective-permute-start(bf16[128,2176]{1,0:T(8,128)(2,1)S(1)} %get-tuple-element.559), channel_id=1, source_target_pairs={{0,1},{1,0},{2,3},{3,2},{4,5},{5,4},{6,7},{7,6},{8,9},{9,8},{10,11... | collective-permute-start | bytes 1671176 | tf_op jit(solution)/shard_map/ppermute | solution.py:492
  475.9 47.1 %collective-permute-start.97 = (bf16[80,2048]{1,0:T(8,128)(2,1)}, bf16[80,2048]{1,0:T(8,128)(2,1)}, u32[]{:S(2)}, u32[]{:S(2)}) collective-permute-start(bf16[80,2048]{1,0:T(8,128)(2,1)} %get-tuple-element.634), channel_id=1, source_target_pairs={{0,4},{1,5},{2,6},{3,7},{4,0},{5,1},{6,2},{7,3},{8,12},{9,13},{10,... | collective-permute-start | bytes 983048 | tf_op jit(solution)/shard_map/ppermute | solution.py:497
  480.0 43.1 %collective-permute-start.98 = (bf16[80,2048]{1,0:T(8,128)(2,1)}, bf16[80,2048]{1,0:T(8,128)(2,1)S(1)}, u32[]{:S(2)}, u32[]{:S(2)}) collective-permute-start(bf16[80,2048]{1,0:T(8,128)(2,1)} %get-tuple-element.635), channel_id=1, source_target_pairs={{0,6},{1,7},{2,4},{3,5},{4,2},{5,3},{6,0},{7,1},{8,14},{9,15},{10,... | collective-permute-start | bytes 983048 | tf_op jit(solution)/shard_map/ppermute | solution.py:497
  482.4 40.6 %collective-permute-start.90 = (bf16[128,2048]{1,0:T(8,128)(2,1)S(1)}, bf16[128,2048]{1,0:T(8,128)(2,1)}, u32[]{:S(2)}, u32[]{:S(2)}) collective-permute-start(bf16[128,2048]{1,0:T(8,128)(2,1)S(1)} %get-tuple-element.636), channel_id=1, source_target_pairs={{0,2},{1,3},{2,0},{3,1},{4,6},{5,7},{6,4},{7,5},{8,10},{9,11},{10,... | collective-permute-start | bytes 1572872 | tf_op jit(solution)/shard_map/ppermute | solution.py:497
  483.5 39.5 %collective-permute-start.91 = (bf16[128,2048]{1,0:T(8,128)(2,1)S(1)}, bf16[128,2048]{1,0:T(8,128)(2,1)}, u32[]{:S(2)}, u32[]{:S(2)}) collective-permute-start(bf16[128,2048]{1,0:T(8,128)(2,1)S(1)} %get-tuple-element.636), channel_id=1, source_target_pairs={{0,4},{1,5},{2,6},{3,7},{4,0},{5,1},{6,2},{7,3},{8,12},{9,13},{10,... | collective-permute-start | bytes 1572872 | tf_op jit(solution)/shard_map/ppermute | solution.py:497
  487.1 35.9 %collective-permute-start.92 = (bf16[128,2048]{1,0:T(8,128)(2,1)S(1)}, bf16[128,2048]{1,0:T(8,128)(2,1)}, u32[]{:S(2)}, u32[]{:S(2)}) collective-permute-start(bf16[128,2048]{1,0:T(8,128)(2,1)S(1)} %get-tuple-element.636), channel_id=1, source_target_pairs={{0,6},{1,7},{2,4},{3,5},{4,2},{5,3},{6,0},{7,1},{8,14},{9,15},{10,... | collective-permute-start | bytes 1572872 | tf_op jit(solution)/shard_map/ppermute | solution.py:497
  544.2 33.4 %collective-permute-start.105 = (bf16[80,2048]{1,0:T(8,128)(2,1)S(1)}, bf16[80,2048]{1,0:T(8,128)(2,1)S(1)}, u32[]{:S(2)}, u32[]{:S(2)}) collective-permute-start(bf16[80,2048]{1,0:T(8,128)(2,1)S(1)} %get-tuple-element.646), channel_id=1, source_target_pairs={{0,6},{1,7},{2,4},{3,5},{4,2},{5,3},{6,0},{7,1},{8,14},{9,15},{10,... | collective-permute-start | bytes 983048 | tf_op jit(solution)/shard_map/ppermute | solution.py:497
  545.9 31.6 %collective-permute-start.109 = (bf16[128,2048]{1,0:T(8,128)(2,1)S(1)}, bf16[128,2048]{1,0:T(8,128)(2,1)S(1)}, u32[]{:S(2)}, u32[]{:S(2)}) collective-permute-start(bf16[128,2048]{1,0:T(8,128)(2,1)S(1)} %add_convert_fusion.8), channel_id=1, source_target_pairs={{0,8},{1,9},{2,10},{3,11},{4,12},{5,13},{6,14},{7,15},{8,16},{9,17... | collective-permute-start | bytes 1572872 | tf_op jit(solution)/shard_map/ppermute | solution.py:502
  550.0 27.6 %collective-permute-start.100 = (bf16[128,2048]{1,0:T(8,128)(2,1)S(1)}, bf16[128,2048]{1,0:T(8,128)(2,1)S(1)}, u32[]{:S(2)}, u32[]{:S(2)}) collective-permute-start(bf16[128,2048]{1,0:T(8,128)(2,1)S(1)} %get-tuple-element.728), channel_id=1, source_target_pairs={{0,2},{1,3},{2,0},{3,1},{4,6},{5,7},{6,4},{7,5},{8,10},{9,11},{10,... | collective-permute-start | bytes 1572872 | tf_op jit(solution)/shard_map/ppermute | solution.py:497
  552.3 25.3 %collective-permute-start.101 = (bf16[128,2048]{1,0:T(8,128)(2,1)S(1)}, bf16[128,2048]{1,0:T(8,128)(2,1)S(1)}, u32[]{:S(2)}, u32[]{:S(2)}) collective-permute-start(bf16[128,2048]{1,0:T(8,128)(2,1)S(1)} %get-tuple-element.727), channel_id=1, source_target_pairs={{0,4},{1,5},{2,6},{3,7},{4,0},{5,1},{6,2},{7,3},{8,12},{9,13},{10,... | collective-permute-start | bytes 1572872 | tf_op jit(solution)/shard_map/ppermute | solution.py:497
  600.6 36.7 %collective-permute-start.111 = (bf16[256,1280]{1,0:T(8,128)(2,1)}, bf16[256,1280]{1,0:T(8,128)(2,1)}, u32[]{:S(2)}, u32[]{:S(2)}) collective-permute-start(bf16[256,1280]{1,0:T(8,128)(2,1)} %slice_bitcast_fusion), channel_id=1, source_target_pairs={{0,8},{1,9},{2,10},{3,11},{4,12},{5,13},{6,14},{7,15},{8,16},{9,17... | collective-permute-start | bytes 1966088 | tf_op jit(solution)/shard_map/ppermute | solution.py:502
  640.2 29.4 %collective-permute-start.121 = (bf16[256,1280]{1,0:T(8,128)(2,1)}, bf16[256,1280]{1,0:T(8,128)(2,1)}, u32[]{:S(2)}, u32[]{:S(2)}) collective-permute-start(bf16[256,1280]{1,0:T(8,128)(2,1)} %fusion.3), channel_id=1, source_target_pairs={{0,8},{1,9},{2,10},{3,11},{4,12},{5,13},{6,14},{7,15},{8,16},{9,17... | collective-permute-start | bytes 1966088 | tf_op jit(solution)/shard_map/ppermute | solution.py:502
  642.4 27.3 %collective-permute-start.122 = (bf16[128,2048]{1,0:T(8,128)(2,1)}, bf16[128,2048]{1,0:T(8,128)(2,1)}, u32[]{:S(2)}, u32[]{:S(2)}) collective-permute-start(bf16[128,2048]{1,0:T(8,128)(2,1)} %fusion.5), channel_id=1, source_target_pairs={{0,8},{1,9},{2,10},{3,11},{4,12},{5,13},{6,14},{7,15},{8,16},{9,17... | collective-permute-start | bytes 1572872 | tf_op jit(solution)/shard_map/ppermute | solution.py:502
  677.8 29.1 %collective-permute-start.134 = (bf16[256,1280]{1,0:T(8,128)(2,1)S(1)}, bf16[256,1280]{1,0:T(8,128)(2,1)S(1)}, u32[]{:S(2)}, u32[]{:S(2)}) collective-permute-start(bf16[256,1280]{1,0:T(8,128)(2,1)S(1)} %fusion.2), channel_id=1, source_target_pairs={{0,8},{1,9},{2,10},{3,11},{4,12},{5,13},{6,14},{7,15},{8,16},{9,17... | collective-permute-start | bytes 1966088 | tf_op jit(solution)/shard_map/ppermute | solution.py:502
  (280 other events, 4350.2 us)

commit v3 on v2

--- a/solution.py
+++ b/solution.py
@@ -12,10 +12,9 @@
 NEGATIVE = -1e30
 CORES = 2
 LANES = 128
+MEBIBYTE = 1024 * 1024
 FLOPS_A_MICRO = 1_000_000_000
 BYTES_A_MICRO = 2_000_000
-VMEM_BYTES = 32 * 1024 * 1024
-MORE_BYTES = 50 * 1024 * 1024
 CONTRACT_ROWS = (((0,), (0,)), ((), ()))
 CONTRACT_LAST = (((1,), (1,)), ((), ()))
 
@@ -49,7 +48,7 @@
     return (jnp.cos(angle), jnp.sin(angle))
 
 
-def call(kernel, outs, vmem=VMEM_BYTES, micros=0, **specs):
+def call(kernel, outs, mebibytes=32, micros=0, **specs):
     if micros:
         specs["cost_estimate"] = pl.CostEstimate(
             flops=micros * FLOPS_A_MICRO, bytes_accessed=micros * BYTES_A_MICRO, transcendentals=0
@@ -57,7 +56,7 @@
     return pl.pallas_call(
         kernel,
         out_shape=outs,
-        compiler_params=pltpu.CompilerParams(vmem_limit_bytes=vmem),
+        compiler_params=pltpu.CompilerParams(vmem_limit_bytes=mebibytes * MEBIBYTE),
         **specs,
     )
 
@@ -111,22 +110,52 @@
     out[...] = total
 
 
-def project_back_kernel(my_outer, grad, own, other, order, out):
+def project_back_kernel(outer, my_outer, grad, *refs):
+    *pieces, order, out = refs
     f32, bf16 = jnp.float32, jnp.bfloat16
-    block = jnp.concatenate(
-        [
-            lax.dot_general(grad[...], part[0], CONTRACT_LAST, preferred_element_type=f32)
-            for part in (own, other)
-        ],
-        axis=1,
-    ).astype(bf16)
-    out[...] = lax.dot_general(
-        block, order[...], CONTRACT_LAST, preferred_element_type=f32
-    ).astype(bf16)
+    for s in range(outer):
+
+        @pl.when(pl.program_id(0) == s)
+        def _(s=s):
+            block = jnp.concatenate(
+                [
+                    lax.dot_general(
+                        grad[...], part[...], CONTRACT_LAST, preferred_element_type=f32
+                    )
+                    for part in pieces[s::outer]
+                ],
+                axis=1,
+            ).astype(bf16)
+            out[...] = lax.dot_general(
+                block, order[...], CONTRACT_LAST, preferred_element_type=f32
+            ).astype(bf16)
+
+
+def router_order_kernel(outer, experts, my_outer, *refs):
+    *pieces, order, out = refs
+    span = order.shape[0]
+    column = lax.broadcasted_iota(jnp.int32, (span, out.shape[1]), 1)
+    for s in range(outer):
+        block = jnp.concatenate([part[...] for part in pieces[s::outer]], axis=0)
+        block = jnp.dot(order[...], block, preferred_element_type=jnp.float32)
+        start = pl.multiple_of(lax.rem(my_outer[0] + (outer - s), outer) * span, LANES)
+        out[pl.ds(start, span), :] = jnp.where(column < experts, block, 0.0).astype(jnp.bfloat16)
+
+
+def gain_back_kernel(grad, *refs):
+    *parts, gain_grad = refs
+    count = parts[0].shape[0]
+    total = jnp.zeros(gain_grad.shape, jnp.float32)
+    for b, part in enumerate(parts):
+        value = part[...].astype(jnp.float32)
+        root = lax.rsqrt(jnp.mean(value * value, axis=-1, keepdims=True) + EPS)
+        rows = grad[b * count : (b + 1) * count, :].astype(jnp.float32)
+        total += jnp.sum(rows * value * root, axis=0, keepdims=True)
+    gain_grad[...] = total
 
 
 def tokens_back_kernel(tokens, own, *refs):
-    *others, hidden_grad, gain, tokens_grad, gain_grad = refs
+    *others, hidden_grad, gain, tokens_grad = refs
     f32 = jnp.float32
     grad = own[...].astype(f32)
     for other in others:
@@ -134,7 +163,6 @@
     value = tokens[...].astype(f32)
     root = lax.rsqrt(jnp.mean(value * value, axis=-1, keepdims=True) + EPS)
     normal = value * root
-    gain_grad[...] = jnp.sum(grad * normal, axis=0, keepdims=True)
     grad = grad * gain[...]
     tokens_grad[...] = hidden_grad[...] + root * (
         grad - normal * jnp.mean(normal * grad, axis=-1, keepdims=True)
@@ -511,12 +539,6 @@
     def spread(parts):
         return [swap_chip(part, r) for r, part in enumerate(parts)]
 
-    def ring_reduce(part):
-        total = part(1)
-        for s in range(2, outer):
-            total = shift_outer(total.astype(bf16)).astype(f32) + part(s)
-        return part(0), shift_outer(total.astype(bf16))
-
     def scatter_outer(take):
         total = take(my_outer)
         for s in range(1, outer):
@@ -534,6 +556,81 @@
     half_columns = group_columns // CORES
     columns = group_columns + 2 * width
     rows_out = out_weight.shape[0]
+
+    lanes = round_up(experts, LANES)
+    pair_width = round_up(2 * experts, LANES)
+    part_rows = round_up(CORES * capacity, 16)
+    slots = chips * part_rows
+
+    def dispatch_first(piece, partner):
+        *parts, picks = call(
+            functools.partial(pick_kernel, capacity),
+            [shape((part_rows, model), bf16)] * chips + [shape((slots, CORES * count), bf16)],
+            mebibytes=16,
+        )(piece, partner, near, earlier)
+        return parts, picks
+
+    def dispatch(picks, piece, partner):
+        outs = [shape((part_rows, piece.shape[1]), bf16)] * chips
+        return call(send_kernel, outs, mebibytes=16)(picks, piece, partner)
+
+    def settle(picks, parts):
+        columns_of = parts[0].shape[1]
+        return call(
+            settle_kernel,
+            (shape((count, columns_of), f32), shape((count, columns_of), bf16)),
+            mebibytes=16,
+        )(picks, *parts)
+
+    together = chips * count
+    first_gain_row, second_gain_row = first_gain[None, :], second_gain[None, :]
+    query_gain_row, key_gain_row = query_norm_gain[None, :], key_gain[None, :]
+
+    def norm(token_parts):
+        return call(
+            functools.partial(norm_kernel, outer),
+            shape((together, model), bf16),
+            in_specs=[smem] + [vmem] * (chips + 2),
+            scratch_shapes=[pltpu.VMEM((together, model), bf16)],
+        )(outer_scalar, *token_parts, first_gain_row, front_order)
+
+    def positions(length_parts):
+        layouts = [sequence_layout(part[0], count) for part in length_parts]
+        segment = jnp.stack([layout[0] for layout in layouts])
+        position = jnp.concatenate([layout[1] for layout in layouts])
+        cosine_table, sine_table = rotary_tables(position, width)
+        sine_table = turned_sine(sine_table)
+        places = jnp.arange(count, dtype=i32)
+        allowed = (segment[:, :, None] == segment[:, None, :]) & (
+            places[None, None, :] <= places[None, :, None]
+        )
+        return cosine_table, sine_table, allowed.astype(f32).reshape(together, count)
+
+    sequences = lengths.shape[1]
+    side_width = round_up(experts + sequences, LANES)
+    side = jnp.pad(router_weight, ((0, 0), (0, side_width - experts))) + jnp.pad(
+        lengths.astype(bf16), ((0, depth - 1), (experts, side_width - experts - sequences))
+    )
+    cut = []
+    for r in range(chips):
+        target = my_chip ^ r
+        part = [
+            lax.dynamic_slice_in_dim(query_weight, target * group_columns, group_columns, 1),
+            lax.dynamic_slice_in_dim(key_matrix, target * width, width, 1),
+            lax.dynamic_slice_in_dim(value_matrix, target * width, width, 1),
+            side,
+        ]
+        cut.append(swap_chip(jnp.concatenate(part, axis=1), r))
+    out_pieces = [out_weight, shift_outer(out_weight)]
+    front_pieces, front_others = [], []
+    state = fence((cut, out_pieces, routes, tokens, cotangent))
+    cut, out_pieces, routes, tokens, cotangent = state
+    length_parts = [
+        part[:1, columns + experts : columns + experts + sequences].astype(i32) for part in cut
+    ]
+    cut = jnp.concatenate(cut, axis=0)
+    me = after(me, cut)
+    my_core, my_chip, my_outer = me % CORES, (me // CORES) % chips, me // plane
 
     def arrival_order(length, block, inner):
         place = jnp.arange(length, dtype=i32)
@@ -550,8 +647,6 @@
     front_order = arrival_order(plane * depth, depth, 1)
     out_order = arrival_order(group_columns, rows_out, span)
 
-    lanes = round_up(experts, LANES)
-    pair_width = round_up(2 * experts, LANES)
     mask = jnp.sum(
         (routes[:, :, None] == jnp.arange(lanes, dtype=i32)[None, None, :]).astype(f32), axis=1
     )
@@ -561,142 +656,60 @@
     )
     near = (near[:, None] == jnp.arange(lanes, dtype=i32)[None, :]).astype(bf16)
     earlier = jnp.triu(jnp.ones((count, count), bf16), 1)
-    part_rows = round_up(CORES * capacity, 16)
-    slots = chips * part_rows
-
-    def dispatch_first(piece, partner):
-        *parts, picks = call(
-            functools.partial(pick_kernel, capacity),
-            [shape((part_rows, model), bf16)] * chips + [shape((slots, CORES * count), bf16)],
-        )(piece, partner, near, earlier)
-        return parts, picks
-
-    def dispatch(picks, piece, partner):
-        return call(send_kernel, [shape((part_rows, piece.shape[1]), bf16)] * chips)(
-            picks, piece, partner
-        )
-
-    def settle(picks, parts):
-        columns_of = parts[0].shape[1]
-        return call(
-            settle_kernel, (shape((count, columns_of), f32), shape((count, columns_of), bf16))
-        )(picks, *parts)
-
-    cut = []
-    for r in range(chips):
-        target = my_chip ^ r
-        part = [
-            lax.dynamic_slice_in_dim(query_weight, target * group_columns, group_columns, 1),
-            lax.dynamic_slice_in_dim(key_matrix, target * width, width, 1),
-            lax.dynamic_slice_in_dim(value_matrix, target * width, width, 1),
-        ]
-        cut.append(swap_chip(jnp.concatenate(part, axis=1), r))
-    cut = jnp.concatenate(cut, axis=0)
-    front_pieces, front_others = [cut], []
-    out_pieces = [out_weight, shift_outer(out_weight)]
     cotangent_wide = jnp.concatenate([cotangent, mask.astype(bf16)], axis=1)
     cotangent_pieces, cotangent_parts, picks = [cotangent_wide], [], []
-
-    def send_cotangent(piece, partner):
-        parts, pick = dispatch_first(piece, partner)
+    cotangent_partners = []
+
+    def send_cotangent(s):
+        parts, pick = dispatch_first(cotangent_pieces[s], cotangent_partners[s])
         cotangent_parts.append(spread(parts))
         picks.append(pick)
 
-    router_parts = router_weight.reshape(1, depth * experts)
+    front_pieces.append(cut)
     for t in range(2, outer + 1):
-        (
-            front_pieces[-1],
-            out_pieces[-1],
-            tokens,
-            lengths,
-            router_parts,
-            cotangent_pieces[0],
-        ) = fence(
-            (
-                front_pieces[-1],
-                out_pieces[-1],
-                tokens,
-                lengths,
-                router_parts,
-                cotangent_pieces[0],
-            )
-        )
         front_pieces.append(shift_outer(front_pieces[-1]))
-        front_others.append(swap_core(front_pieces[-2]))
         if t < outer:
             out_pieces.append(shift_outer(out_pieces[-1]))
+        front_others.append(swap_core(front_pieces[-2]))
         if t == 2:
             token_parts = gather_chips(tokens)
-            length_parts = gather_chips(lengths)
-            router_parts = jnp.concatenate([router_parts, swap_core(router_parts)], axis=0)
-            cotangent_partner = swap_core(cotangent_pieces[0])
-        if t == 3:
-            router_parts = jnp.concatenate(gather_chips(router_parts), axis=0)
-            send_cotangent(cotangent_pieces[0], cotangent_partner)
-    cotangent_pieces.append(shift_outer(cotangent_pieces[0]))
-    stacked = jnp.stack(out_pieces)
-    out_own = []
-    for r in range(chips):
-        part = [
-            lax.dynamic_index_in_dim(
-                stacked,
-                (my_outer + outer - ((my_chip ^ r) * span + u)) % outer,
-                0,
-                keepdims=False,
-            )
-            for u in range(span)
-        ]
-        out_own.append(swap_chip(jnp.concatenate(part, axis=0), r))
-
-    together = chips * count
-    first_gain_row, second_gain_row = first_gain[None, :], second_gain[None, :]
-    query_gain_row, key_gain_row = query_norm_gain[None, :], key_gain[None, :]
-    normed_low = call(
-        functools.partial(norm_kernel, outer),
-        shape((together, model), bf16),
-        in_specs=[smem] + [vmem] * (chips + 2),
-        scratch_shapes=[pltpu.VMEM((together, model), bf16)],
-    )(outer_scalar, *token_parts, first_gain_row, front_order)
-    layouts = [sequence_layout(part[0], count) for part in length_parts]
-    segment = jnp.stack([layout[0] for layout in layouts])
-    position = jnp.concatenate([layout[1] for layout in layouts])
-    cosine_table, sine_table = rotary_tables(position, width)
-    sine_table = turned_sine(sine_table)
-    places = jnp.arange(count, dtype=i32)
-    allowed = (segment[:, :, None] == segment[:, None, :]) & (
-        places[None, None, :] <= places[None, :, None]
-    )
-    allowed = allowed.astype(f32).reshape(together, count)
-    (
-        front_pieces[-1],
-        cotangent_pieces[-1],
-        router_parts,
-        out_own,
-        normed_low,
-        cosine_table,
-        sine_table,
-        allowed,
-        out_order,
-        cotangent_parts[0],
-    ) = fence(
-        (
-            front_pieces[-1],
-            cotangent_pieces[-1],
-            router_parts,
-            out_own,
-            normed_low,
-            cosine_table,
-            sine_table,
-            allowed,
-            out_order,
-            cotangent_parts[0],
-        )
-    )
+            cotangent_partners.append(swap_core(cotangent_pieces[0]))
+            state = (token_parts, cotangent_partners, positions(length_parts))
+            state = fence((state, front_pieces, front_others, out_pieces))
+            (token_parts, cotangent_partners, tables), *state = state
+            cosine_table, sine_table, allowed = tables
+        elif t == 3:
+            send_cotangent(0)
+            normed_low = norm(token_parts)
+            state = (cotangent_parts, picks, normed_low)
+            state = fence((state, front_pieces, front_others, out_pieces))
+            (cotangent_parts, picks, normed_low), *state = state
+        elif t < outer:
+            state = fence((front_pieces, front_others, out_pieces))
+        else:
+            cotangent_pieces.append(shift_outer(cotangent_pieces[0]))
+            stacked = jnp.stack(out_pieces)
+            out_own = []
+            for r in range(chips):
+                part = [
+                    lax.dynamic_index_in_dim(
+                        stacked,
+                        (my_outer + outer - ((my_chip ^ r) * span + u)) % outer,
+                        0,
+                        keepdims=False,
+                    )
+                    for u in range(span)
+                ]
+                out_own.append(swap_chip(jnp.concatenate(part, axis=0), r))
+            state = fence((front_pieces, front_others, out_pieces))
+        front_pieces, front_others, out_pieces = state
+    cotangent_pieces, out_own = fence((cotangent_pieces, out_own))
+
     front_others.append(swap_core(front_pieces[-1]))
-    router_parts = jnp.concatenate([shift_outer(router_parts, s) for s in range(outer)], axis=0)
+    cotangent_partners.append(swap_core(cotangent_pieces[1]))
     out_own = jnp.concatenate(out_own, axis=0)
+    front_others, cotangent_partners, out_own = fence((front_others, cotangent_partners, out_own))
     out_other = swap_core(out_own)
-    cotangent_partner = swap_core(cotangent_pieces[1])
     for s in range(2, outer - 1):
         cotangent_pieces.append(shift_outer(cotangent_pieces[-1]))
     tile = 2 * width
@@ -709,6 +722,9 @@
         out_specs=pl.BlockSpec((together, tile), lambda n: (0, n)),
     )(normed_low, *front_pieces, *front_others)
 
+    cotangent_pieces[1] = after(cotangent_pieces[1], projected)
+    send_cotangent(1)
+
     def blocks(columns_of):
         return pl.BlockSpec((count, columns_of), lambda b: (b, 0))
 
@@ -722,7 +738,6 @@
             shape((together, width), bf16),
             shape((together, group_columns), bf16),
         ),
-        micros=13,
         grid=(chips,),
         in_specs=[
             blocks(columns),
@@ -736,22 +751,10 @@
         out_specs=[blocks(group_columns), blocks(width), blocks(width), blocks(group_columns)],
         scratch_shapes=[pltpu.VMEM((count, group_columns), bf16)],
     )(projected, cosine_table, sine_table, allowed, query_gain_row, key_gain_row, out_order)
-    send_cotangent(after(cotangent_pieces[1], context_low), cotangent_partner)
-    device = jnp.arange(shards, dtype=i32)
-    came_from = ((my_outer - device // plane) % outer) * plane + (
-        (device % plane) ^ (me % plane)
-    )
-    full_router = jnp.dot(
-        (came_from[:, None] == device[None, :]).astype(bf16),
-        router_parts,
-        preferred_element_type=f32,
-    )
-    full_router = full_router.astype(bf16).reshape(model, experts)
-    router_wide = jnp.pad(full_router, ((0, 0), (0, lanes - experts)))
-
-    context_low, out_own, out_other, cotangent_pieces[-1], router_wide = fence(
-        (context_low, out_own, out_other, cotangent_pieces[-1], router_wide)
-    )
+    state = (context_low, out_other, cotangent_pieces, cotangent_parts, picks)
+    state = fence((state, query_low, key_low, value_low, projected))
+    (context_low, out_other, cotangent_pieces, cotangent_parts, picks), *state = state
+    query_low, key_low, value_low, projected = state
     context_own, context_other = context_low[:, :half_columns], context_low[:, half_columns:]
 
     def attended(first, last):
@@ -763,12 +766,19 @@
     arrived = [swap_chip(away[(r - 1) * count : r * count], r) for r in range(1, chips)]
     home = attended(0, count)
     cotangent_pieces.append(shift_outer(cotangent_pieces[-1]))
-    for s in range(2, outer - 1):
-        send_cotangent(after(cotangent_pieces[s], away), swap_core(cotangent_pieces[s]))
-    arrived, home, cotangent_pieces[-1], cotangent_parts = fence(
-        (arrived, home, cotangent_pieces[-1], cotangent_parts)
-    )
-    send_cotangent(cotangent_pieces[-1], swap_core(cotangent_pieces[-1]))
+    cotangent_partners.append(swap_core(cotangent_pieces[2]))
+    router_block = pl.BlockSpec((chips * depth, lanes), lambda n: (0, columns // lanes))
+    order_block = pl.BlockSpec((plane * depth, plane * depth), lambda n: (0, 0))
+    router_wide = call(
+        functools.partial(router_order_kernel, outer, experts),
+        shape((model, lanes), bf16),
+        grid=(1,),
+        in_specs=[smem, *[router_block] * (CORES * outer), order_block],
+        out_specs=pl.BlockSpec((model, lanes), lambda n: (0, 0)),
+    )(outer_scalar, *front_pieces, *front_others, after(front_order, away))
+    arrived, home, cotangent_pieces, cotangent_partners, router_wide = fence(
+        (arrived, home, cotangent_pieces, cotangent_partners, router_wide)
+    )
     hidden, second_wide, prob, gates = call(
         functools.partial(router_kernel, experts),
         (
@@ -790,8 +800,7 @@
             functools.partial(expert_kernel, chips, experts),
             [shape((part_rows, model + pair_width), bf16)] * chips
             + [shape((slots, hidden_units), bf16)] * 3,
-            vmem=MORE_BYTES,
-            micros=13,
+            micros=11,
             grid=(hidden_units // unit_tile,),
             in_specs=[smem]
             + [part] * chips
@@ -809,40 +818,52 @@
         )(me_scalar, *came, *given, gate_weight, up_weight, down_weight)
         return outs[:chips], (came, given, *outs[chips:])
 
-    second_pieces = [second_wide]
-    for s in range(1, outer):
-        second_pieces.append(shift_outer(second_pieces[-1]))
-    backs, kept = [], []
-    sent = dispatch(picks[0], second_pieces[0], swap_core(second_pieces[0]))
-    for s in range(outer):
-        came = spread(sent)
-        if s + 1 < outer:
-            piece = second_pieces[s + 1]
-            partner = swap_core(piece)
-            if s:
-                piece = after(piece, *backs[s - 1])
-            sent = dispatch(picks[s + 1], piece, partner)
-            came, sent, cotangent_parts = fence((came, sent, cotangent_parts))
-        back, keep = expert(came, cotangent_parts[s])
-        backs.append(back)
-        kept.append(keep)
-
-    returned, latest = {}, ()
-    for s in [*range(1, outer), 0]:
-        parts = spread(fence((backs[s], latest))[0])
-        latest = tuple(parts[1:])
-        own, partner = settle(picks[s], parts)
-        returned[s] = (own, swap_core(partner))
-    grad_own, grad_came = ring_reduce(
-        lambda s: returned[s][0] + returned[s][1].astype(f32) if s else returned[0]
-    )
-
-    def move(s, *others):
-        return call(move_kernel, [shape((part_rows, model), bf16)] * chips)(
-            after(kept[s][2], *others), down_weight
+    def move(s):
+        return call(move_kernel, [shape((part_rows, model), bf16)] * chips, mebibytes=16)(
+            kept[s][2], down_weight
         )
 
-    moved = {s: spread(move(s, *latest)) for s in range(1, outer - 1)}
+    second_pieces, second_partners = [second_wide], []
+    came, backs, kept, returned, settled_own, settled_partner = {}, {}, {}, {}, {}, {}
+    moved, moving, moved_own, moved_partner = {}, [], {}, {}
+    grad_step = None
+    for t in range(outer + 5):
+        if 0 <= t - 1 < outer:
+            sent = dispatch(picks[t - 1], second_pieces[t - 1], second_partners[t - 1])
+            came[t - 1] = spread(sent)
+        if 2 <= t + 2 < outer:
+            send_cotangent(t + 2)
+        if t + 3 < outer:
+            cotangent_partners.append(swap_core(cotangent_pieces[t + 3]))
+        if t + 1 < outer:
+            second_pieces.append(shift_outer(second_pieces[t]))
+        if t < outer:
+            second_partners.append(swap_core(second_pieces[t]))
+        if t - 5 >= 1:
+            total = settled_own[t - 5] + settled_partner[t - 5].astype(f32)
+            if grad_step is not None:
+                total = total + grad_step.astype(f32)
+            grad_step = shift_outer(total.astype(bf16))
+        if 0 <= t - 4 < outer:
+            settled_own[t - 4], partner = settle(picks[t - 4], returned[t - 4])
+            settled_partner[t - 4] = swap_core(partner)
+        if 0 <= t - 3 < outer:
+            returned[t - 3] = spread(backs[t - 3])
+        if t == outer + 2:
+            moving = [move(i) for i in range(outer)]
+        if t >= outer + 3:
+            moved[t - outer - 2] = spread(moving[t - outer - 2])
+        if t == outer + 4:
+            moved_own[1], partner = settle(picks[1], moved[1])
+            moved_partner[1] = swap_core(partner)
+        if 0 <= t - 2 < outer:
+            backs[t - 2], kept[t - 2] = expert(came[t - 2], cotangent_parts[t - 2])
+        state = (second_pieces, second_partners, cotangent_partners, cotangent_parts, picks)
+        state = (state, came, backs, returned, settled_own, settled_partner)
+        state = fence((state, moved, moving, moved_own, moved_partner, grad_step, kept))
+        state, moved, moving, moved_own, moved_partner, grad_step, kept = state
+        state, came, backs, returned, settled_own, settled_partner = state
+        second_pieces, second_partners, cotangent_partners, cotangent_parts, picks = state
 
     grad_hidden, grad_hidden_low, grad_logits_low, second_gain_term = call(
         functools.partial(router_back_kernel, experts),
@@ -852,9 +873,11 @@
             shape((count, lanes), bf16),
             shape((1, model), f32),
         ),
+        mebibytes=60,
     )(
-        *grad_own,
-        grad_came,
+        settled_own[0],
+        settled_partner[0],
+        grad_step,
         cotangent,
         hidden,
         second_gain_row,
@@ -863,8 +886,11 @@
         prob,
         gates,
     )
-    grad_attn_parts = gather_chips(grad_hidden_low)
-    kept_late = [fence((keep, grad_hidden_low))[0] for keep in kept]
+    grad_attn_low = jnp.concatenate(gather_chips(grad_hidden_low), axis=0)
+    moved_step = shift_outer((moved_own[1] + moved_partner[1].astype(f32)).astype(bf16))
+    moved_own[2], partner = settle(picks[2], moved[2])
+    moved_partner[2] = swap_core(partner)
+    kept_late = [fence((kept[s], grad_hidden_low))[0] for s in range(outer)]
     total_slots = outer * slots
     row_tile = pl.BlockSpec((part_rows, unit_tile), lambda i: (0, i))
     unit_once = pl.BlockSpec((slots, hidden_units), lambda i: (0, 0))
@@ -875,8 +901,8 @@
             shape((model, hidden_units), f32),
             shape((hidden_units, model), f32),
         ),
-        vmem=MORE_BYTES,
-        micros=18,
+        mebibytes=50,
+        micros=20,
         grid=(model // unit_tile,),
         in_specs=[row_tile] * (2 * outer * chips) + [unit_once] * (3 * outer),
         out_specs=[
@@ -892,20 +918,25 @@
     )
 
 
-    def settled(s, parts):
-        own, partner = settle(picks[s], parts)
-        return own + swap_core(partner).astype(f32)
-
-    moved_step = shift_outer(settled(1, after(moved[1], gate_grad)).astype(bf16))
-    (
-        grad_attn_parts,
-        gate_grad,
-        up_grad,
-        down_grad,
-        moved,
-    ) = fence((grad_attn_parts, gate_grad, up_grad, down_grad, moved))
-
-    grad_attn_low = jnp.concatenate(grad_attn_parts, axis=0)
+    router_part = lax.dot_general(
+        grad_logits_low[:, :experts],
+        second_wide[:, :model],
+        CONTRACT_ROWS,
+        preferred_element_type=f32,
+    )
+    router_part = scatter_outer(
+        lambda o: lax.dynamic_slice_in_dim(router_part, o * (plane * depth), plane * depth, 1)
+    )
+    state = (grad_attn_low, gate_grad, up_grad, down_grad, moved_step, moved_own, moved_partner)
+    state, router_part = fence((state, router_part))
+    grad_attn_low, gate_grad, up_grad, down_grad, moved_step, moved_own, moved_partner = state
+
+    def next_step(step, *parts):
+        total = step.astype(f32)
+        for part in parts:
+            total = total + part.astype(f32)
+        return shift_outer(total.astype(bf16))
+
     out_send, out_keep = (
         lax.dot_general(
             context, grad_attn_low, CONTRACT_ROWS, preferred_element_type=f32
@@ -919,13 +950,13 @@
         ).astype(bf16)
         for weight in (out_own, out_other)
     )
+    out_keep, out_swapped, grad_context_own, grad_context_other = fence(
+        (out_keep, out_swapped, grad_context_own, grad_context_other)
+    )
     out_half = (out_keep.astype(f32) + out_swapped.astype(f32)).astype(bf16)
     out_half = out_half.reshape(chips, span * rows_out, model)
     out_came = [swap_chip(out_half[r], r) for r in range(chips)]
-    grad_context_own = after(grad_context_own, out_half)
-    for s in range(2, outer - 1):
-        moved_step = shift_outer((moved_step.astype(f32) + settled(s, moved[s])).astype(bf16))
-    moved_last = spread(move(outer - 1, grad_context_other))
+    moved_step = next_step(moved_step, moved_own[2], moved_partner[2])
     grad_front_low, gain_terms = call(
         functools.partial(attend_back_kernel, scale),
         (shape((together, columns), bf16), shape((2, width), f32)),
@@ -962,8 +993,8 @@
         out_order,
     )
 
-    grad_front_low, gain_terms, out_came, moved_last, moved_step = fence(
-        (grad_front_low, gain_terms, out_came, moved_last, moved_step)
+    grad_front_low, gain_terms, out_came, moved_step, router_part = fence(
+        (grad_front_low, gain_terms, out_came, moved_step, router_part)
     )
 
     half_model = model // CORES
@@ -976,100 +1007,99 @@
         ).astype(bf16)
         for k in (1, 0)
     )
-    front_half = (front_keep.astype(f32) + swap_core(front_send).astype(f32)).astype(bf16)
-    front_half = front_half.reshape(outer, chips * depth, columns)
-    moved_step = shift_outer(
-        (moved_step.astype(f32) + settled(outer - 1, moved_last)).astype(bf16)
-    )
-    out_whole = jnp.stack(out_came).reshape(outer, rows_out, model)
-    router_part = lax.dot_general(
-        after(grad_logits_low, front_send)[:, :experts],
-        second_wide[:, :model],
-        CONTRACT_ROWS,
-        preferred_element_type=f32,
-    )
-    router_part = scatter_outer(
-        lambda o: lax.dynamic_slice_in_dim(router_part, o * (plane * depth), plane * depth, 1)
-    )
+    front_swapped = swap_core(front_send)
+    out_parts = [
+        part[u * rows_out : (u + 1) * rows_out] for part in out_came for u in range(span)
+    ]
 
     def out_slice(s):
         target = (my_outer - s) % outer
-        return lax.dynamic_index_in_dim(
-            out_whole, ((target // span) ^ my_chip) * span + target % span, 0, keepdims=False
-        )
-
-    def next_step(step, part):
-        return shift_outer((step.astype(f32) + part.astype(f32)).astype(bf16))
-
-    out_first = out_slice(1)
-    front_half, grad_front_late, out_first = fence((front_half, grad_front_low, out_first))
-    front_step, out_step = shift_outer(front_half[1]), shift_outer(out_first)
-    piece_block = pl.BlockSpec((1, chips * depth, columns), lambda s, o: (s, 0, 0))
+        place = ((target // span) ^ my_chip) * span + target % span
+        chosen = out_parts[0]
+        for i in range(1, outer):
+            chosen = jnp.where(place == i, out_parts[i], chosen)
+        return chosen
+
+    out_step = shift_outer(out_slice(1))
+    for s in range(3, outer):
+        moved[s] = spread(moving[s])
+    state = (front_keep, front_swapped, out_step, moved, router_part)
+    front_keep, front_swapped, out_step, moved, router_part = fence(state)
+    front_half = (front_keep.astype(f32) + front_swapped.astype(f32)).astype(bf16)
+    front_half = front_half.reshape(outer, chips * depth, columns)
+    front_step = shift_outer(front_half[1])
+    out_step = next_step(out_step, out_slice(2))
+    piece_block = pl.BlockSpec((chips * depth, columns), lambda s, o: (0, 0))
     grad_normed = pl.pallas_call(
-        project_back_kernel,
+        functools.partial(project_back_kernel, outer),
         out_shape=shape((together, model), bf16),
         grid_spec=pltpu.PrefetchScalarGridSpec(
             num_scalar_prefetch=1,
             grid=(outer,),
             in_specs=[
                 pl.BlockSpec((together, columns), lambda s, o: (0, 0)),
-                piece_block,
-                piece_block,
+                *[piece_block] * (CORES * outer),
                 pl.BlockSpec((plane * depth, plane * depth), lambda s, o: (0, 0)),
             ],
             out_specs=pl.BlockSpec(
                 (together, plane * depth), lambda s, o: (0, lax.rem(o[0] + outer - s, outer))
             ),
         ),
-        compiler_params=pltpu.CompilerParams(vmem_limit_bytes=VMEM_BYTES),
+        compiler_params=pltpu.CompilerParams(vmem_limit_bytes=32 * MEBIBYTE),
     )(
         outer_scalar,
-        grad_front_late,
-        jnp.stack(front_pieces),
-        jnp.stack(front_others),
+        after(grad_front_low, front_half),
+        *front_pieces,
+        *front_others,
         front_order,
     )
-    came = [swap_chip(grad_normed[r * count : (r + 1) * count], r) for r in range(1, chips)]
-    grad_home = grad_normed[:count]
-    front_step, out_step, came, grad_home, moved_step, router_part = fence(
-        (front_step, out_step, came, grad_home, moved_step, router_part)
-    )
-    for s in range(2, outer):
+    for s in range(3, outer):
+        moved_own[s], partner = settle(picks[s], moved[s])
+        moved_partner[s] = swap_core(partner)
+    router_part = sum(
+        [
+            swap_chip(
+                lax.dynamic_slice_in_dim(
+                    router_part, (my_chip ^ r) * (CORES * depth), CORES * depth, 1
+                ),
+                r,
+            )
+            for r in range(chips)
+        ]
+    )
+    state = (front_half, front_step, out_step, grad_normed, moved_own, moved_partner)
+    state, router_part = fence((state, router_part))
+    front_half, front_step, out_step, grad_normed, moved_own, moved_partner = state
+    front_step = next_step(front_step, front_half[2])
+    for s in range(3, outer):
+        out_step = next_step(out_step, out_slice(s))
+    arrived = [swap_chip(grad_normed[r * count : (r + 1) * count], r) for r in range(1, chips)]
+    first_gain_term = call(gain_back_kernel, shape((1, model), f32))(grad_normed, *token_parts)
+    gain_sums = jnp.concatenate(
+        [first_gain_term.reshape(-1), second_gain_term.reshape(-1), gain_terms.reshape(-1)]
+    ).reshape(-1, LANES)
+    gain_sums = gain_sums + swap_core(gain_sums)
+    router_grad = (
+        lax.dynamic_slice_in_dim(router_part, my_core * depth, depth, 1)
+        + swap_core(lax.dynamic_slice_in_dim(router_part, (1 - my_core) * depth, depth, 1))
+    ).T
+    state = (front_step, out_step, arrived, gain_sums, router_grad)
+    front_step, out_step, arrived, gain_sums, router_grad = fence(state)
+    for s in range(3, outer):
         front_step = next_step(front_step, front_half[s])
-        out_step = next_step(out_step, out_slice(s))
-        if s == 2:
-            moved_home = spread(move(0, moved_step))
-            tokens_grad, first_gain_term = call(
-                tokens_back_kernel,
-                (shape((count, model), f32), shape((1, model), f32)),
-            )(tokens, grad_home, *came, grad_hidden, first_gain_row)
-            gain_sums = jnp.concatenate(
-                [first_gain_term.reshape(-1), second_gain_term.reshape(-1), gain_terms.reshape(-1)]
-            ).reshape(-1, LANES)
-            gain_sums = gain_sums + swap_core(gain_sums)
-            router_part = sum(
-                [
-                    swap_chip(
-                        lax.dynamic_slice_in_dim(
-                            router_part, (my_chip ^ r) * (CORES * depth), CORES * depth, 1
-                        ),
-                        r,
-                    )
-                    for r in range(chips)
-                ]
-            )
-            front_step, out_step, moved_home, gain_sums, tokens_grad, router_part = fence(
-                (front_step, out_step, moved_home, gain_sums, tokens_grad, router_part)
-            )
-            router_grad = (
-                lax.dynamic_slice_in_dim(router_part, my_core * depth, depth, 1)
-                + swap_core(lax.dynamic_slice_in_dim(router_part, (1 - my_core) * depth, depth, 1))
-            ).T
-            gain_sums = sum([swap_chip(gain_sums, r) for r in range(1, chips)], gain_sums)
-            output = (hidden + settled(0, moved_home) + moved_step.astype(f32)).astype(bf16)
-        else:
-            front_step, out_step = fence((front_step, out_step))
-    gain_sums, output, front_step, out_step = fence((gain_sums, output, front_step, out_step))
+        moved_step = next_step(moved_step, moved_own[s], moved_partner[s])
+    moved[0] = spread(moving[0])
+    tokens_grad = call(tokens_back_kernel, shape((count, model), f32))(
+        tokens, grad_normed[:count], *arrived, grad_hidden, first_gain_row
+    )
+    gain_sums = sum([swap_chip(gain_sums, r) for r in range(1, chips)], gain_sums)
+    out_grad = out_step.astype(f32) + out_slice(0).astype(f32)
+    state = (front_step, moved_step, moved, gain_sums, tokens_grad, out_grad)
+    front_step, moved_step, moved, gain_sums, tokens_grad, out_grad = fence(state)
+    moved_own[0], partner = settle(picks[0], moved[0])
+    moved_partner[0] = swap_core(partner)
+    output = hidden + moved_own[0] + moved_partner[0].astype(f32) + moved_step.astype(f32)
+    output = output.astype(bf16)
     gain_sums = sum([shift_outer(gain_sums, s) for s in range(1, outer)], gain_sums).reshape(-1)
     front = (front_step.astype(f32) + front_half[0].astype(f32)).astype(bf16)
     front = front.reshape(chips, depth, columns)

time: 733 us -> 642 us (0.88)
  waiting for transfers between devices: 311 us -> 266 us
  local copies, waits for them, and re-layouts: 67.1 us -> 36.5 us
  matrix products: 24.2 us -> 15.1 us
    ppermute x33 -> x30, waiting for transfers between devices: 107 us -> 73.5 us  [shift_outer(): lax.ppermute(value, 'fsdp', [(i, (i // plane + s) % outer * plane + i % p...]
    unnamed x346 -> x356, local copies, waits for them, and re-layouts: 53.3 us -> 30 us
    ppermute x84 -> x78, waiting for transfers between devices: 204 us -> 191 us  [swap_chip(): lax.ppermute(value, 'fsdp', [(i, i ^ r * CORES) for i in range(shards)])]
    ppermute x84 -> x78, starting transfers between devices: 104 us -> 93.3 us  [swap_chip(): lax.ppermute(value, 'fsdp', [(i, i ^ r * CORES) for i in range(shards)])]
    pallas_call x4, Pallas kernels: 53.4 us -> 45.3 us  [expert(): call(functools.partial(expert_kernel, chips, experts), [shape((part_rows,...]
    ppermute x33 -> x30, starting transfers between devices: 30.6 us -> 38.3 us  [shift_outer(): lax.ppermute(value, 'fsdp', [(i, (i // plane + s) % outer * plane + i % p...]
    pallas_call x11 -> x13, Pallas kernels: 20.5 us -> 23.2 us  [the longest x1 6.26 us: body(): pl.pallas_call(functools.partial(project_back_kernel, outer), out_shape=s...]
    convert_element_type x13 -> x15, other arithmetic: 14.2 us -> 15.4 us  [the longest x6 6.66 us: next_step(): return shift_outer(total.astype(bf16))]
  transfers between devices with their start and end apart: 143 -> 133, of which waited for: 52 -> 55; matrix products, arithmetic and copies ran while one was open for 9% -> 8% of each run, Pallas kernels for 20% -> 21%
where the time goes in v3:
time: 642 us; the launch traced here: 635 us
  waiting for transfers between devices  266 us (41%)
  Pallas kernels  146 us (23%)
  starting transfers between devices  133 us (21%)
  local copies, waits for them, and re-layouts  36.5 us (6%)
  other arithmetic  34.6 us (5%)
  matrix products  15.1 us (2%)
    ppermute x78, waiting for transfers between devices, swap_chip(): lax.ppermute(value, 'fsdp', [(i, i ^ r * CORES) for i in range(shards)])  191 us
    ppermute x78, starting transfers between devices, swap_chip(): lax.ppermute(value, 'fsdp', [(i, i ^ r * CORES) for i in range(shards)])  93.3 us
    ppermute x30, waiting for transfers between devices, shift_outer(): lax.ppermute(value, 'fsdp', [(i, (i // plane + s) % outer * plane + i % p...  73.5 us
    pallas_call x4, Pallas kernels, expert(): call(functools.partial(expert_kernel, chips, experts), [shape((part_rows,...  45.3 us
    ppermute x30, starting transfers between devices, shift_outer(): lax.ppermute(value, 'fsdp', [(i, (i // plane + s) % outer * plane + i % p...  38.3 us
    unnamed x356, local copies, waits for them, and re-layouts  30 us
    pallas_call x1, Pallas kernels, body(): call(functools.partial(expert_grad_kernel, outer, chips), (shape((model,...  21.1 us
    pallas_call x1, Pallas kernels, body(): call(functools.partial(attend_back_kernel, scale), (shape((together, colu...  18.6 us
  transfers between devices with their start and end apart: 133, of which 55 were waited for; matrix products, arithmetic and copies ran while one was open for 8% of the time, Pallas kernels for 21%

profile of v3, /device:TPU:0, one launch (start us, length us, event | category | flops | bytes accessed | tf_op | source)
XLA Modules:
  0.0 635.0 jit_solution(5147204822340617473)
XLA Ops:
  31.4 18.3 %collective-permute-done.10 = bf16[128,2048]{1,0:T(8,128)(2,1)} collective-permute-done((bf16[128,2048]{1,0:T(8,128)(2,1)}, bf16[128,2048]{1,0:T(8,128)(2,1)}, u32[]{:S(2)}, u32[]{:S(2)}) %collective-permute-start.10) | collective-permute-done | bytes 524320 | tf_op jit(solution)/shard_map/ppermute | solution.py:530
  56.0 5.9 collective-permute-done.6.refs_3_
  69.9 7.2 %collective-permute-done.11.refs_5_.refs_17_ = bf16[80,2048]{1,0:T(8,128)(2,1)} collective-permute-done((bf16[80,2048]{1,0:T(8,128)(2,1)}, bf16[80,2048]{1,0:T(8,128)(2,1)}, u32[]{:S(2)}, u32[]{:S(2)}) %collective-permute-start.11) | collective-permute-done | bytes 327712 | tf_op jit(solution)/shard_map/ppermute | solution.py:525
  95.6 15.9 %collective-permute-done.17.refs_3_ = bf16[256,1408]{1,0:T(8,128)(2,1)S(1)} collective-permute-done((bf16[256,1408]{1,0:T(8,128)(2,1)S(1)}, bf16[256,1408]{1,0:T(8,128)(2,1)S(1)}, u32[]{:S(2)}, u32[]{:S(2)}) %collective-permute-start.17) | collective-permute-done | bytes 720928 | tf_op jit(solution)/shard_map/ppermute | solution.py:530
  113.6 5.7 collective-permute-done.20.own
  127.2 5.6 shard_map.265.front
  138.8 13.5 %shard_map.266 = (bf16[512,1024]{1,0:T(8,128)(2,1)S(1)}, bf16[512,128]{1,0:T(8,128)(2,1)S(1)}, bf16[512,128]{1,0:T(8,128)(2,1)S(1)}, bf16[512,1024]{1,0:T(8,128)(2,1)S(1)}) custom-call(f32[512,1280]{1,0:T(8,128)S(1)} %shard_map.265.front, f32[512,128]{1,0:T(8,128)S(1)} %copy-done.50, f32[512,128]{1,0:T(8,128)S(1)} %copy-done.52, f32[512,128]{1,0:T(8,128)S(1)} %copy-done.54, ...), custom_call_target="tpu_custom_call" | custom-call | tf_op jit(solution)/shard_map/pallas_call | solution.py:733
  163.5 10.3 %collective-permute-done.30.refs_2_ = bf16[128,2048]{1,0:T(8,128)(2,1)S(1)} collective-permute-done((bf16[128,2048]{1,0:T(8,128)(2,1)S(1)}, bf16[128,2048]{1,0:T(8,128)(2,1)S(1)}, u32[]{:S(2)}, u32[]{:S(2)}) %collective-permute-start.30) | collective-permute-done | bytes 524320 | tf_op jit(solution)/shard_map/ppermute | solution.py:525
  173.7 11.5 %collective-permute-done.31.refs_3_ = bf16[128,2048]{1,0:T(8,128)(2,1)S(1)} collective-permute-done((bf16[128,2048]{1,0:T(8,128)(2,1)S(1)}, bf16[128,2048]{1,0:T(8,128)(2,1)S(1)}, u32[]{:S(2)}, u32[]{:S(2)}) %collective-permute-start.31) | collective-permute-done | bytes 524320 | tf_op jit(solution)/shard_map/ppermute | solution.py:525
  196.6 10.7 %collective-permute-done.39.refs_6_.refs_26_ = bf16[80,2048]{1,0:T(8,128)(2,1)S(1)} collective-permute-done((bf16[80,2048]{1,0:T(8,128)(2,1)S(1)}, bf16[80,2048]{1,0:T(8,128)(2,1)S(1)}, u32[]{:S(2)}, u32[]{:S(2)}) %collective-permute-start.39) | collective-permute-done | bytes 327712 | tf_op jit(solution)/shard_map/ppermute | solution.py:525
  233.3 6.3 collective-permute-done.47.refs_2_
  246.3 11.9 %shard_map.274 = (bf16[80,2176]{1,0:T(8,128)(2,1)S(1)}, bf16[80,2176]{1,0:T(8,128)(2,1)S(1)}, bf16[80,2176]{1,0:T(8,128)(2,1)S(1)}, bf16[80,2176]{1,0:T(8,128)(2...) custom-call(s32[1]{0:T(128)} %bitcast.36.me, ...), custom_call_target="tpu_custom_call" | custom-call | flops 11000000512 | bytes 22000000 | tf_op jit(solution)/shard_map/pallas_call | solution.py:799
  266.7 6.5 %collective-permute-done.55.refs_1_.refs_9_ = bf16[80,2176]{1,0:T(8,128)(2,1)S(1)} collective-permute-done((bf16[80,2176]{1,0:T(8,128)(2,1)S(1)}, bf16[80,2176]{1,0:T(8,128)(2,1)S(1)}, u32[]{:S(2)}, u32[]{:S(2)}) %collective-permute-start.55) | collective-permute-done | bytes 348192 | tf_op jit(solution)/shard_map/ppermute | solution.py:525
  274.1 5.5 collective-permute-done.56.refs_2_.refs_10_
  281.7 11.0 %shard_map.276 = (bf16[80,2176]{1,0:T(8,128)(2,1)S(1)}, bf16[80,2176]{1,0:T(8,128)(2,1)S(1)}, bf16[80,2176]{1,0:T(8,128)(2,1)S(1)}, bf16[80,2176]{1,0:T(8,128)(2...) custom-call(s32[1]{0:T(128)} %bitcast.36.me, ...), custom_call_target="tpu_custom_call" | custom-call | flops 11000000512 | bytes 22000000 | tf_op jit(solution)/shard_map/pallas_call | solution.py:799
  305.6 7.4 %collective-permute-done.62.refs_2_.refs_14_ = bf16[80,2176]{1,0:T(8,128)(2,1)S(1)} collective-permute-done((bf16[80,2176]{1,0:T(8,128)(2,1)S(1)}, bf16[80,2176]{1,0:T(8,128)(2,1)S(1)}, u32[]{:S(2)}, u32[]{:S(2)}) %collective-permute-start.62) | collective-permute-done | bytes 348192 | tf_op jit(solution)/shard_map/ppermute | solution.py:525
  313.3 11.4 %shard_map.278 = (bf16[80,2176]{1,0:T(8,128)(2,1)S(1)}, bf16[80,2176]{1,0:T(8,128)(2,1)S(1)}, bf16[80,2176]{1,0:T(8,128)(2,1)S(1)}, bf16[80,2176]{1,0:T(8,128)(2...) custom-call(s32[1]{0:T(128)} %bitcast.36.me, ...), custom_call_target="tpu_custom_call" | custom-call | flops 11000000512 | bytes 22000000 | tf_op jit(solution)/shard_map/pallas_call | solution.py:799
  331.6 11.0 %shard_map.280 = (bf16[80,2176]{1,0:T(8,128)(2,1)S(1)}, bf16[80,2176]{1,0:T(8,128)(2,1)S(1)}, bf16[80,2176]{1,0:T(8,128)(2,1)S(1)}, bf16[80,2176]{1,0:T(8,128)(2...) custom-call(s32[1]{0:T(128)} %bitcast.36.me, ...), custom_call_target="tpu_custom_call" | custom-call | flops 11000000512 | bytes 22000000 | tf_op jit(solution)/shard_map/pallas_call | solution.py:799
  374.3 7.0 %collective-permute-done.78.refs_1_ = bf16[80,2048]{1,0:T(8,128)(2,1)S(1)} collective-permute-done((bf16[80,2048]{1,0:T(8,128)(2,1)S(1)}, bf16[80,2048]{1,0:T(8,128)(2,1)S(1)}, u32[]{:S(2)}, u32[]{:S(2)}) %collective-permute-start.78) | collective-permute-done | bytes 327712 | tf_op jit(solution)/shard_map/ppermute | solution.py:525
  381.3 6.2 collective-permute-done.79.refs_2_
  395.8 7.3 %collective-permute-done.82.refs_1_ = bf16[80,2048]{1,0:T(8,128)(2,1)} collective-permute-done((bf16[80,2048]{1,0:T(8,128)(2,1)}, bf16[80,2048]{1,0:T(8,128)(2,1)}, u32[]{:S(2)}, u32[]{:S(2)}) %collective-permute-start.82) | collective-permute-done | bytes 327712 | tf_op jit(solution)/shard_map/ppermute | solution.py:525
  403.1 6.2 collective-permute-done.83.refs_2_
  429.5 21.1 %shard_map.290 = (f32[2048,768]{1,0:T(8,128)}, f32[2048,768]{1,0:T(8,128)}, f32[768,2048]{1,0:T(8,128)}) custom-call(bf16[80,2176]{1,0:T(8,128)(2,1)} %copy-done.80, bf16[80,2176]{1,0:T(8,128)(2,1)} %copy-done.81, bf16[80,2176]{1,0:T(8,128)(2,1)} %copy-done.82, bf16[80,2176]{1,0:T(8,128)(2,1)} %copy-done.83, bf16[80,2176]{1,0:T(8,128)(2,1)} %copy-done.84, ...), custom_call_target="tpu_custom_call" | custom-call | flops 20000000000 | bytes 40000000 | tf_op jit(solution)/shard_map/pallas_call | solution.py:897
  463.7 18.6 %shard_map.292 = (bf16[512,1280]{1,0:T(8,128)(2,1)S(1)}, f32[2,128]{1,0:T(2,128)S(1)}) custom-call(f32[512,1280]{1,0:T(8,128)S(1)} %shard_map.265.front, bf16[512,1024]{1,0:T(8,128)(2,1)S(1)} %copy-done.79, bf16[512,128]{1,0:T(8,128)(2,1)S(1)} %copy-done.138, bf16[512,128]{1,0:T(8,128)(2,1)S(1)} %copy-done.140, ...), custom_call_target="tpu_custom_call" | custom-call | flops 17999998976 | bytes 36000000 | tf_op jit(solution)/shard_map/pallas_call | solution.py:960
  503.9 5.9 collective-permute-done.103.refs_2_
  534.2 6.3 shard_map.293.grad
  540.6 5.8 collective-permute-done.106
  565.8 8.7 %collective-permute-done.114.refs_1_ = bf16[128,2048]{1,0:T(8,128)(2,1)S(1)} collective-permute-done((bf16[128,2048]{1,0:T(8,128)(2,1)S(1)}, bf16[128,2048]{1,0:T(8,128)(2,1)S(1)}, u32[]{:S(2)}, u32[]{:S(2)}) %collective-permute-start.114) | collective-permute-done | bytes 524320 | tf_op jit(solution)/shard_map/ppermute | solution.py:525
  577.4 7.7 %collective-permute-done.111 = bf16[256,1280]{1,0:T(8,128)(2,1)S(1)} collective-permute-done((bf16[256,1280]{1,0:T(8,128)(2,1)S(1)}, bf16[256,1280]{1,0:T(8,128)(2,1)S(1)}, u32[]{:S(2)}, u32[]{:S(2)}) %collective-permute-start.111) | collective-permute-done | bytes 655392 | tf_op jit(solution)/shard_map/ppermute | solution.py:530
  590.6 6.7 %collective-permute-done.124 = f32[34,128]{1,0:T(8,128)S(1)} collective-permute-done((f32[34,128]{1,0:T(8,128)S(1)}, f32[34,128]{1,0:T(8,128)S(1)}, u32[]{:S(2)}, u32[]{:S(2)}) %collective-permute-start.124) | collective-permute-done | bytes 17440 | tf_op jit(solution)/shard_map/ppermute | solution.py:525
  600.4 10.0 %collective-permute-done.119 = bf16[128,2048]{1,0:T(8,128)(2,1)S(1)} collective-permute-done((bf16[128,2048]{1,0:T(8,128)(2,1)S(1)}, bf16[128,2048]{1,0:T(8,128)(2,1)S(1)}, u32[]{:S(2)}, u32[]{:S(2)}) %collective-permute-start.119) | collective-permute-done | bytes 524320 | tf_op jit(solution)/shard_map/ppermute | solution.py:530
  610.4 7.8 %collective-permute-done.118 = bf16[256,1280]{1,0:T(8,128)(2,1)S(1)} collective-permute-done((bf16[256,1280]{1,0:T(8,128)(2,1)S(1)}, bf16[256,1280]{1,0:T(8,128)(2,1)S(1)}, u32[]{:S(2)}, u32[]{:S(2)}) %collective-permute-start.118) | collective-permute-done | bytes 655392 | tf_op jit(solution)/shard_map/ppermute | solution.py:530
  (731 shorter events, 330.8 us)
Async XLA Ops:
  20.1 42.6 %collective-permute-start.8 = (bf16[256,1408]{1,0:T(8,128)(2,1)S(1)}, bf16[256,1408]{1,0:T(8,128)(2,1)S(1)}, u32[]{:S(2)}, u32[]{:S(2)}) collective-permute-start(bf16[256,1408]{1,0:T(8,128)(2,1)S(1)} %constant_dynamic-update-slice_fusion.refs_0_), channel_id=1, source_target_pairs={{0,8},{1,9},{2,10},{3,11},{4,12},{5,13},{6,14},{7,15},{8,16},{9,17... | collective-permute-start | bytes 2162696 | tf_op jit(solution)/shard_map/ppermute | solution.py:530
  21.7 41.0 %collective-permute-start.9 = (bf16[256,1408]{1,0:T(8,128)(2,1)S(1)}, bf16[256,1408]{1,0:T(8,128)(2,1)S(1)}, u32[]{:S(2)}, u32[]{:S(2)}) collective-permute-start(bf16[256,1408]{1,0:T(8,128)(2,1)S(1)} %constant_dynamic-update-slice_fusion.refs_0_), channel_id=1, source_target_pairs={{0,1},{1,0},{2,3},{3,2},{4,5},{5,4},{6,7},{7,6},{8,9},{9,8},{10,11... | collective-permute-start | bytes 2162696 | tf_op jit(solution)/shard_map/ppermute | solution.py:520
  22.0 29.4 %collective-permute-start.4 = (bf16[128,2048]{1,0:T(8,128)(2,1)S(1)}, bf16[128,2048]{1,0:T(8,128)(2,1)}, u32[]{:S(2)}, u32[]{:S(2)}) collective-permute-start(bf16[128,2048]{1,0:T(8,128)(2,1)S(1)} %copy-done.7), channel_id=1, source_target_pairs={{0,2},{1,3},{2,0},{3,1},{4,6},{5,7},{6,4},{7,5},{8,10},{9,11},{10,... | collective-permute-start | bytes 1572872 | tf_op jit(solution)/shard_map/ppermute | solution.py:525
  23.3 32.7 %collective-permute-start.5 = (bf16[128,2048]{1,0:T(8,128)(2,1)S(1)}, bf16[128,2048]{1,0:T(8,128)(2,1)}, u32[]{:S(2)}, u32[]{:S(2)}) collective-permute-start(bf16[128,2048]{1,0:T(8,128)(2,1)S(1)} %copy-done.7), channel_id=1, source_target_pairs={{0,4},{1,5},{2,6},{3,7},{4,0},{5,1},{6,2},{7,3},{8,12},{9,13},{10,... | collective-permute-start | bytes 1572872 | tf_op jit(solution)/shard_map/ppermute | solution.py:525
  62.8 27.8 %collective-permute-start.14 = (bf16[256,1408]{1,0:T(8,128)(2,1)S(1)}, bf16[256,1408]{1,0:T(8,128)(2,1)S(1)}, u32[]{:S(2)}, u32[]{:S(2)}) collective-permute-start(bf16[256,1408]{1,0:T(8,128)(2,1)S(1)} %collective-permute-done.8.refs_1_), channel_id=1, source_target_pairs={{0,8},{1,9},{2,10},{3,11},{4,12},{5,13},{6,14},{7,15},{8,16},{9,17... | collective-permute-start | bytes 2162696 | tf_op jit(solution)/shard_map/ppermute | solution.py:530
  62.9 27.7 %collective-permute-start.15 = (bf16[256,1408]{1,0:T(8,128)(2,1)S(1)}, bf16[256,1408]{1,0:T(8,128)(2,1)}, u32[]{:S(2)}, u32[]{:S(2)}) collective-permute-start(bf16[256,1408]{1,0:T(8,128)(2,1)S(1)} %collective-permute-done.8.refs_1_), channel_id=1, source_target_pairs={{0,1},{1,0},{2,3},{3,2},{4,5},{5,4},{6,7},{7,6},{8,9},{9,8},{10,11... | collective-permute-start | bytes 2162696 | tf_op jit(solution)/shard_map/ppermute | solution.py:520
  90.7 28.6 %collective-permute-start.20 = (bf16[128,2176]{1,0:T(8,128)(2,1)S(1)}, bf16[128,2176]{1,0:T(8,128)(2,1)}, u32[]{:S(2)}, u32[]{:S(2)}) collective-permute-start(bf16[128,2176]{1,0:T(8,128)(2,1)S(1)} %pad_maximum_fusion.4.own), channel_id=1, source_target_pairs={{0,8},{1,9},{2,10},{3,11},{4,12},{5,13},{6,14},{7,15},{8,16},{9,17... | collective-permute-start | bytes 1671176 | tf_op jit(solution)/shard_map/ppermute | solution.py:530
  93.6 25.7 %collective-permute-start.21 = (bf16[128,2048]{1,0:T(8,128)(2,1)S(1)}, bf16[128,2048]{1,0:T(8,128)(2,1)S(1)}, u32[]{:S(2)}, u32[]{:S(2)}) collective-permute-start(bf16[128,2048]{1,0:T(8,128)(2,1)S(1)} %get-tuple-element.1522), channel_id=1, source_target_pairs={{0,2},{1,3},{2,0},{3,1},{4,6},{5,7},{6,4},{7,5},{8,10},{9,11},{10,... | collective-permute-start | bytes 1572872 | tf_op jit(solution)/shard_map/ppermute | solution.py:525
  123.8 29.0 %collective-permute-start.25 = (bf16[512,2048]{1,0:T(8,128)(2,1)S(1)}, bf16[512,2048]{1,0:T(8,128)(2,1)S(1)}, u32[]{:S(2)}, u32[]{:S(2)}) collective-permute-start(bf16[512,2048]{1,0:T(8,128)(2,1)S(1)} %pad_maximum_fusion.1), channel_id=1, source_target_pairs={{0,1},{1,0},{2,3},{3,2},{4,5},{5,4},{6,7},{7,6},{8,9},{9,8},{10,11... | collective-permute-start | bytes 6291464 | tf_op jit(solution)/shard_map/ppermute | solution.py:520
  123.9 28.4 %collective-permute-start.26 = (bf16[128,2176]{1,0:T(8,128)(2,1)}, bf16[128,2176]{1,0:T(8,128)(2,1)S(1)}, u32[]{:S(2)}, u32[]{:S(2)}) collective-permute-start(bf16[128,2176]{1,0:T(8,128)(2,1)} %collective-permute-done.20.own), channel_id=1, source_target_pairs={{0,8},{1,9},{2,10},{3,11},{4,12},{5,13},{6,14},{7,15},{8,16},{9,17... | collective-permute-start | bytes 1671176 | tf_op jit(solution)/shard_map/ppermute | solution.py:530
  155.0 30.2 %collective-permute-start.33 = (bf16[128,2176]{1,0:T(8,128)(2,1)S(1)}, bf16[128,2176]{1,0:T(8,128)(2,1)S(1)}, u32[]{:S(2)}, u32[]{:S(2)}) collective-permute-start(bf16[128,2176]{1,0:T(8,128)(2,1)S(1)} %collective-permute-done.26.own), channel_id=1, source_target_pairs={{0,8},{1,9},{2,10},{3,11},{4,12},{5,13},{6,14},{7,15},{8,16},{9,17... | collective-permute-start | bytes 1671176 | tf_op jit(solution)/shard_map/ppermute | solution.py:530
  157.3 27.9 %collective-permute-start.34 = (bf16[128,2176]{1,0:T(8,128)(2,1)S(1)}, bf16[128,2176]{1,0:T(8,128)(2,1)S(1)}, u32[]{:S(2)}, u32[]{:S(2)}) collective-permute-start(bf16[128,2176]{1,0:T(8,128)(2,1)S(1)} %collective-permute-done.26.own), channel_id=1, source_target_pairs={{0,1},{1,0},{2,3},{3,2},{4,5},{5,4},{6,7},{7,6},{8,9},{9,8},{10,11... | collective-permute-start | bytes 1671176 | tf_op jit(solution)/shard_map/ppermute | solution.py:520
  159.9 25.3 %collective-permute-start.31 = (bf16[128,2048]{1,0:T(8,128)(2,1)S(1)}, bf16[128,2048]{1,0:T(8,128)(2,1)S(1)}, u32[]{:S(2)}, u32[]{:S(2)}) collective-permute-start(bf16[128,2048]{1,0:T(8,128)(2,1)S(1)} %get-tuple-element.1525), channel_id=1, source_target_pairs={{0,4},{1,5},{2,6},{3,7},{4,0},{5,1},{6,2},{7,3},{8,12},{9,13},{10,... | collective-permute-start | bytes 1572872 | tf_op jit(solution)/shard_map/ppermute | solution.py:525
  160.7 24.5 %collective-permute-start.32 = (bf16[128,2048]{1,0:T(8,128)(2,1)S(1)}, bf16[128,2048]{1,0:T(8,128)(2,1)S(1)}, u32[]{:S(2)}, u32[]{:S(2)}) collective-permute-start(bf16[128,2048]{1,0:T(8,128)(2,1)S(1)} %get-tuple-element.1524), channel_id=1, source_target_pairs={{0,6},{1,7},{2,4},{3,5},{4,2},{5,3},{6,0},{7,1},{8,14},{9,15},{10,... | collective-permute-start | bytes 1572872 | tf_op jit(solution)/shard_map/ppermute | solution.py:525
  211.6 28.0 %collective-permute-start.41 = (bf16[128,2176]{1,0:T(8,128)(2,1)S(1)}, bf16[128,2176]{1,0:T(8,128)(2,1)S(1)}, u32[]{:S(2)}, u32[]{:S(2)}) collective-permute-start(bf16[128,2176]{1,0:T(8,128)(2,1)S(1)} %collective-permute-done.35.own), channel_id=1, source_target_pairs={{0,8},{1,9},{2,10},{3,11},{4,12},{5,13},{6,14},{7,15},{8,16},{9,17... | collective-permute-start | bytes 1671176 | tf_op jit(solution)/shard_map/ppermute | solution.py:530
  213.8 25.8 %collective-permute-start.42 = (bf16[128,2176]{1,0:T(8,128)(2,1)S(1)}, bf16[128,2176]{1,0:T(8,128)(2,1)S(1)}, u32[]{:S(2)}, u32[]{:S(2)}) collective-permute-start(bf16[128,2176]{1,0:T(8,128)(2,1)S(1)} %collective-permute-done.35.own), channel_id=1, source_target_pairs={{0,1},{1,0},{2,3},{3,2},{4,5},{5,4},{6,7},{7,6},{8,9},{9,8},{10,11... | collective-permute-start | bytes 1671176 | tf_op jit(solution)/shard_map/ppermute | solution.py:520
  263.9 28.9 %collective-permute-start.57 = (bf16[80,2176]{1,0:T(8,128)(2,1)S(1)}, bf16[80,2176]{1,0:T(8,128)(2,1)S(1)}, u32[]{:S(2)}, u32[]{:S(2)}) collective-permute-start(bf16[80,2176]{1,0:T(8,128)(2,1)S(1)} %get-tuple-element.952), channel_id=1, source_target_pairs={{0,6},{1,7},{2,4},{3,5},{4,2},{5,3},{6,0},{7,1},{8,14},{9,15},{10,... | collective-permute-start | bytes 1044488 | tf_op jit(solution)/shard_map/ppermute | solution.py:525
  265.6 29.0 %collective-permute-start.54 = (bf16[128,2176]{1,0:T(8,128)(2,1)S(1)}, bf16[128,2176]{1,0:T(8,128)(2,1)S(1)}, u32[]{:S(2)}, u32[]{:S(2)}) collective-permute-start(bf16[128,2176]{1,0:T(8,128)(2,1)S(1)} %collective-permute-done.49.own), channel_id=1, source_target_pairs={{0,1},{1,0},{2,3},{3,2},{4,5},{5,4},{6,7},{7,6},{8,9},{9,8},{10,11... | collective-permute-start | bytes 1671176 | tf_op jit(solution)/shard_map/ppermute | solution.py:520
  265.6 27.2 %collective-permute-start.58 = (bf16[80,2176]{1,0:T(8,128)(2,1)S(1)}, bf16[80,2176]{1,0:T(8,128)(2,1)S(1)}, u32[]{:S(2)}, u32[]{:S(2)}) collective-permute-start(bf16[80,2176]{1,0:T(8,128)(2,1)S(1)} %get-tuple-element.953), channel_id=1, source_target_pairs={{0,2},{1,3},{2,0},{3,1},{4,6},{5,7},{6,4},{7,5},{8,10},{9,11},{10,... | collective-permute-start | bytes 1044488 | tf_op jit(solution)/shard_map/ppermute | solution.py:525
  299.3 27.8 %collective-permute-start.67 = (bf16[128,2176]{1,0:T(8,128)(2,1)S(1)}, bf16[128,2176]{1,0:T(8,128)(2,1)S(1)}, u32[]{:S(2)}, u32[]{:S(2)}) collective-permute-start(bf16[128,2176]{1,0:T(8,128)(2,1)S(1)} %get-tuple-element.1010), channel_id=1, source_target_pairs={{0,1},{1,0},{2,3},{3,2},{4,5},{5,4},{6,7},{7,6},{8,9},{9,8},{10,11... | collective-permute-start | bytes 1671176 | tf_op jit(solution)/shard_map/ppermute | solution.py:520
  299.3 27.0 %collective-permute-start.63 = (bf16[80,2176]{1,0:T(8,128)(2,1)S(1)}, bf16[80,2176]{1,0:T(8,128)(2,1)S(1)}, u32[]{:S(2)}, u32[]{:S(2)}) collective-permute-start(bf16[80,2176]{1,0:T(8,128)(2,1)S(1)} %get-tuple-element.996), channel_id=1, source_target_pairs={{0,6},{1,7},{2,4},{3,5},{4,2},{5,3},{6,0},{7,1},{8,14},{9,15},{10,... | collective-permute-start | bytes 1044488 | tf_op jit(solution)/shard_map/ppermute | solution.py:525
  300.6 25.7 %collective-permute-start.64 = (bf16[80,2176]{1,0:T(8,128)(2,1)S(1)}, bf16[80,2176]{1,0:T(8,128)(2,1)S(1)}, u32[]{:S(2)}, u32[]{:S(2)}) collective-permute-start(bf16[80,2176]{1,0:T(8,128)(2,1)S(1)} %get-tuple-element.997), channel_id=1, source_target_pairs={{0,2},{1,3},{2,0},{3,1},{4,6},{5,7},{6,4},{7,5},{8,10},{9,11},{10,... | collective-permute-start | bytes 1044488 | tf_op jit(solution)/shard_map/ppermute | solution.py:525
  414.7 35.9 %collective-permute-start.87 = (bf16[128,2048]{1,0:T(8,128)(2,1)}, bf16[128,2048]{1,0:T(8,128)(2,1)S(1)}, u32[]{:S(2)}, u32[]{:S(2)}) collective-permute-start(bf16[128,2048]{1,0:T(8,128)(2,1)} %get-tuple-element.1334), channel_id=1, source_target_pairs={{0,2},{1,3},{2,0},{3,1},{4,6},{5,7},{6,4},{7,5},{8,10},{9,11},{10,... | collective-permute-start | bytes 1572872 | tf_op jit(solution)/shard_map/ppermute | solution.py:525
  415.9 34.8 %collective-permute-start.88 = (bf16[128,2048]{1,0:T(8,128)(2,1)}, bf16[128,2048]{1,0:T(8,128)(2,1)S(1)}, u32[]{:S(2)}, u32[]{:S(2)}) collective-permute-start(bf16[128,2048]{1,0:T(8,128)(2,1)} %get-tuple-element.1334), channel_id=1, source_target_pairs={{0,4},{1,5},{2,6},{3,7},{4,0},{5,1},{6,2},{7,3},{8,12},{9,13},{10,... | collective-permute-start | bytes 1572872 | tf_op jit(solution)/shard_map/ppermute | solution.py:525
  453.6 28.7 %collective-permute-start.99 = (bf16[128,2048]{1,0:T(8,128)(2,1)S(1)}, bf16[128,2048]{1,0:T(8,128)(2,1)S(1)}, u32[]{:S(2)}, u32[]{:S(2)}) collective-permute-start(bf16[128,2048]{1,0:T(8,128)(2,1)S(1)} %add_convert_fusion.10), channel_id=1, source_target_pairs={{0,8},{1,9},{2,10},{3,11},{4,12},{5,13},{6,14},{7,15},{8,16},{9,17... | collective-permute-start | bytes 1572872 | tf_op jit(solution)/shard_map/ppermute | solution.py:530
  512.3 28.2 %collective-permute-start.107 = (bf16[128,2048]{1,0:T(8,128)(2,1)S(1)}, bf16[128,2048]{1,0:T(8,128)(2,1)}, u32[]{:S(2)}, u32[]{:S(2)}) collective-permute-start(bf16[128,2048]{1,0:T(8,128)(2,1)S(1)} %get-tuple-element.1467), channel_id=1, source_target_pairs={{0,1},{1,0},{2,3},{3,2},{4,5},{5,4},{6,7},{7,6},{8,9},{9,8},{10,11... | collective-permute-start | bytes 1572872 | tf_op jit(solution)/shard_map/ppermute | solution.py:520
  516.0 30.4 %collective-permute-start.105 = (bf16[256,1280]{1,0:T(8,128)(2,1)}, bf16[256,1280]{1,0:T(8,128)(2,1)}, u32[]{:S(2)}, u32[]{:S(2)}) collective-permute-start(bf16[256,1280]{1,0:T(8,128)(2,1)} %slice.245), channel_id=1, source_target_pairs={{0,8},{1,9},{2,10},{3,11},{4,12},{5,13},{6,14},{7,15},{8,16},{9,17... | collective-permute-start | bytes 1966088 | tf_op jit(solution)/shard_map/ppermute | solution.py:530
  520.5 25.9 %collective-permute-start.106 = (bf16[128,2048]{1,0:T(8,128)(2,1)}, bf16[128,2048]{1,0:T(8,128)(2,1)}, u32[]{:S(2)}, u32[]{:S(2)}) collective-permute-start(bf16[128,2048]{1,0:T(8,128)(2,1)} %add_convert_fusion.9), channel_id=1, source_target_pairs={{0,8},{1,9},{2,10},{3,11},{4,12},{5,13},{6,14},{7,15},{8,16},{9,17... | collective-permute-start | bytes 1572872 | tf_op jit(solution)/shard_map/ppermute | solution.py:530
  552.1 25.3 %collective-permute-start.115 = (bf16[128,2048]{1,0:T(8,128)(2,1)S(1)}, bf16[128,2048]{1,0:T(8,128)(2,1)S(1)}, u32[]{:S(2)}, u32[]{:S(2)}) collective-permute-start(bf16[128,2048]{1,0:T(8,128)(2,1)S(1)} %get-tuple-element.1513), channel_id=1, source_target_pairs={{0,6},{1,7},{2,4},{3,5},{4,2},{5,3},{6,0},{7,1},{8,14},{9,15},{10,... | collective-permute-start | bytes 1572872 | tf_op jit(solution)/shard_map/ppermute | solution.py:525
  556.5 28.6 %collective-permute-start.111 = (bf16[256,1280]{1,0:T(8,128)(2,1)S(1)}, bf16[256,1280]{1,0:T(8,128)(2,1)S(1)}, u32[]{:S(2)}, u32[]{:S(2)}) collective-permute-start(bf16[256,1280]{1,0:T(8,128)(2,1)S(1)} %fusion.3), channel_id=1, source_target_pairs={{0,8},{1,9},{2,10},{3,11},{4,12},{5,13},{6,14},{7,15},{8,16},{9,17... | collective-permute-start | bytes 1966088 | tf_op jit(solution)/shard_map/ppermute | solution.py:530
  564.5 35.9 %collective-permute-start.120 = (bf16[80,2048]{1,0:T(8,128)(2,1)S(1)}, bf16[80,2048]{1,0:T(8,128)(2,1)S(1)}, u32[]{:S(2)}, u32[]{:S(2)}) collective-permute-start(bf16[80,2048]{1,0:T(8,128)(2,1)S(1)} %copy-done.110), channel_id=1, source_target_pairs={{0,2},{1,3},{2,0},{3,1},{4,6},{5,7},{6,4},{7,5},{8,10},{9,11},{10,... | collective-permute-start | bytes 983048 | tf_op jit(solution)/shard_map/ppermute | solution.py:525
  574.5 25.9 %collective-permute-start.121 = (bf16[80,2048]{1,0:T(8,128)(2,1)S(1)}, bf16[80,2048]{1,0:T(8,128)(2,1)S(1)}, u32[]{:S(2)}, u32[]{:S(2)}) collective-permute-start(bf16[80,2048]{1,0:T(8,128)(2,1)S(1)} %copy-done.108), channel_id=1, source_target_pairs={{0,4},{1,5},{2,6},{3,7},{4,0},{5,1},{6,2},{7,3},{8,12},{9,13},{10,... | collective-permute-start | bytes 983048 | tf_op jit(solution)/shard_map/ppermute | solution.py:525
  (277 other events, 5730.6 us)

commit v4 on v3

--- a/solution.py
+++ b/solution.py
@@ -110,9 +110,30 @@
     out[...] = total
 
 
-def project_back_kernel(outer, my_outer, grad, *refs):
-    *pieces, order, out = refs
+def add_kernel(first, second, *outs):
+    rows = outs[0].shape[0]
+    for i, out in enumerate(outs):
+        part = slice(i * rows, (i + 1) * rows)
+        total = first[part, :].astype(jnp.float32) + second[part, :].astype(jnp.float32)
+        out[...] = total.astype(out.dtype)
+
+
+def choose_kernel(places, *refs):
+    half = len(refs) // 2
+    parts, outs = refs[:half], refs[half:]
+    for i, out in enumerate(outs):
+        for j, part in enumerate(parts):
+
+            @pl.when(places[i] == j)
+            def _(part=part, out=out):
+                out[...] = part[...]
+
+
+def project_back_kernel(outer, chips, my_outer, grad, *refs):
+    *pieces, order = refs[:-chips]
+    outs = refs[-chips:]
     f32, bf16 = jnp.float32, jnp.bfloat16
+    count = outs[0].shape[0]
     for s in range(outer):
 
         @pl.when(pl.program_id(0) == s)
@@ -126,9 +147,11 @@
                 ],
                 axis=1,
             ).astype(bf16)
-            out[...] = lax.dot_general(
+            block = lax.dot_general(
                 block, order[...], CONTRACT_LAST, preferred_element_type=f32
             ).astype(bf16)
+            for r, out in enumerate(outs):
+                out[...] = block[r * count : (r + 1) * count, :]
 
 
 def router_order_kernel(outer, experts, my_outer, *refs):
@@ -142,15 +165,14 @@
         out[pl.ds(start, span), :] = jnp.where(column < experts, block, 0.0).astype(jnp.bfloat16)
 
 
-def gain_back_kernel(grad, *refs):
+def gain_back_kernel(*refs):
     *parts, gain_grad = refs
-    count = parts[0].shape[0]
+    half = len(parts) // 2
     total = jnp.zeros(gain_grad.shape, jnp.float32)
-    for b, part in enumerate(parts):
+    for grad, part in zip(parts[:half], parts[half:]):
         value = part[...].astype(jnp.float32)
         root = lax.rsqrt(jnp.mean(value * value, axis=-1, keepdims=True) + EPS)
-        rows = grad[b * count : (b + 1) * count, :].astype(jnp.float32)
-        total += jnp.sum(rows * value * root, axis=0, keepdims=True)
+        total += jnp.sum(grad[...].astype(jnp.float32) * value * root, axis=0, keepdims=True)
     gain_grad[...] = total
 
 
@@ -672,22 +694,23 @@
             out_pieces.append(shift_outer(out_pieces[-1]))
         front_others.append(swap_core(front_pieces[-2]))
         if t == 2:
-            token_parts = gather_chips(tokens)
+            token_parts = [swap_chip(tokens, r) for r in range(chips - 1)]
             cotangent_partners.append(swap_core(cotangent_pieces[0]))
             state = (token_parts, cotangent_partners, positions(length_parts))
             state = fence((state, front_pieces, front_others, out_pieces))
             (token_parts, cotangent_partners, tables), *state = state
             cosine_table, sine_table, allowed = tables
         elif t == 3:
+            token_parts.append(swap_chip(tokens, chips - 1))
             send_cotangent(0)
-            normed_low = norm(token_parts)
-            state = (cotangent_parts, picks, normed_low)
+            state = (cotangent_parts, picks, token_parts)
             state = fence((state, front_pieces, front_others, out_pieces))
-            (cotangent_parts, picks, normed_low), *state = state
+            (cotangent_parts, picks, token_parts), *state = state
         elif t < outer:
             state = fence((front_pieces, front_others, out_pieces))
         else:
             cotangent_pieces.append(shift_outer(cotangent_pieces[0]))
+            normed_low = norm(token_parts)
             stacked = jnp.stack(out_pieces)
             out_own = []
             for r in range(chips):
@@ -703,7 +726,7 @@
                 out_own.append(swap_chip(jnp.concatenate(part, axis=0), r))
             state = fence((front_pieces, front_others, out_pieces))
         front_pieces, front_others, out_pieces = state
-    cotangent_pieces, out_own = fence((cotangent_pieces, out_own))
+    cotangent_pieces, out_own, normed_low = fence((cotangent_pieces, out_own, normed_low))
 
     front_others.append(swap_core(front_pieces[-1]))
     cotangent_partners.append(swap_core(cotangent_pieces[1]))
@@ -888,8 +911,6 @@
     )
     grad_attn_low = jnp.concatenate(gather_chips(grad_hidden_low), axis=0)
     moved_step = shift_outer((moved_own[1] + moved_partner[1].astype(f32)).astype(bf16))
-    moved_own[2], partner = settle(picks[2], moved[2])
-    moved_partner[2] = swap_core(partner)
     kept_late = [fence((kept[s], grad_hidden_low))[0] for s in range(outer)]
     total_slots = outer * slots
     row_tile = pl.BlockSpec((part_rows, unit_tile), lambda i: (0, i))
@@ -901,7 +922,7 @@
             shape((model, hidden_units), f32),
             shape((hidden_units, model), f32),
         ),
-        mebibytes=50,
+        mebibytes=60,
         micros=20,
         grid=(model // unit_tile,),
         in_specs=[row_tile] * (2 * outer * chips) + [unit_once] * (3 * outer),
@@ -918,18 +939,8 @@
     )
 
 
-    router_part = lax.dot_general(
-        grad_logits_low[:, :experts],
-        second_wide[:, :model],
-        CONTRACT_ROWS,
-        preferred_element_type=f32,
-    )
-    router_part = scatter_outer(
-        lambda o: lax.dynamic_slice_in_dim(router_part, o * (plane * depth), plane * depth, 1)
-    )
-    state = (grad_attn_low, gate_grad, up_grad, down_grad, moved_step, moved_own, moved_partner)
-    state, router_part = fence((state, router_part))
-    grad_attn_low, gate_grad, up_grad, down_grad, moved_step, moved_own, moved_partner = state
+    state = (grad_attn_low, gate_grad, up_grad, down_grad, moved_step, grad_logits_low)
+    grad_attn_low, gate_grad, up_grad, down_grad, moved_step, grad_logits_low = fence(state)
 
     def next_step(step, *parts):
         total = step.astype(f32)
@@ -950,9 +961,11 @@
         ).astype(bf16)
         for weight in (out_own, out_other)
     )
-    out_keep, out_swapped, grad_context_own, grad_context_other = fence(
-        (out_keep, out_swapped, grad_context_own, grad_context_other)
-    )
+    moved_own[2], partner = settle(picks[2], after(moved[2], out_send))
+    moved_partner[2] = swap_core(partner)
+    state = (out_keep, out_swapped, grad_context_own, grad_context_other)
+    state, moved_own, moved_partner = fence((state, moved_own, moved_partner))
+    out_keep, out_swapped, grad_context_own, grad_context_other = state
     out_half = (out_keep.astype(f32) + out_swapped.astype(f32)).astype(bf16)
     out_half = out_half.reshape(chips, span * rows_out, model)
     out_came = [swap_chip(out_half[r], r) for r in range(chips)]
@@ -993,8 +1006,8 @@
         out_order,
     )
 
-    grad_front_low, gain_terms, out_came, moved_step, router_part = fence(
-        (grad_front_low, gain_terms, out_came, moved_step, router_part)
+    grad_front_low, gain_terms, out_came, moved_step, grad_logits_low = fence(
+        (grad_front_low, gain_terms, out_came, moved_step, grad_logits_low)
     )
 
     half_model = model // CORES
@@ -1009,30 +1022,35 @@
     )
     front_swapped = swap_core(front_send)
     out_parts = [
-        part[u * rows_out : (u + 1) * rows_out] for part in out_came for u in range(span)
+        part[u * rows_out : (u + 1) * rows_out]
+        for part in after(out_came, front_send)
+        for u in range(span)
     ]
-
-    def out_slice(s):
-        target = (my_outer - s) % outer
-        place = ((target // span) ^ my_chip) * span + target % span
-        chosen = out_parts[0]
-        for i in range(1, outer):
-            chosen = jnp.where(place == i, out_parts[i], chosen)
-        return chosen
-
-    out_step = shift_outer(out_slice(1))
+    target = (my_outer - jnp.arange(outer, dtype=i32)) % outer
+    out_places = ((target // span) ^ my_chip) * span + target % span
+    out_home, *out_away = call(
+        choose_kernel,
+        [shape((rows_out, model), bf16)] * outer,
+        in_specs=[smem] + [vmem] * outer,
+    )(out_places, *out_parts)
+    out_step = shift_outer(out_away[0])
     for s in range(3, outer):
         moved[s] = spread(moving[s])
-    state = (front_keep, front_swapped, out_step, moved, router_part)
-    front_keep, front_swapped, out_step, moved, router_part = fence(state)
-    front_half = (front_keep.astype(f32) + front_swapped.astype(f32)).astype(bf16)
-    front_half = front_half.reshape(outer, chips * depth, columns)
+    state = (front_keep, front_swapped, moved, out_step, out_home, out_away)
+    front_keep, front_swapped, moved, out_step, out_home, out_away = fence(state)
+    front_half = call(add_kernel, [shape((chips * depth, columns), bf16)] * outer)(
+        front_keep, front_swapped
+    )
+
+    def next_sum(step, part):
+        return shift_outer(call(add_kernel, [shape(part.shape, bf16)])(step, part)[0])
+
     front_step = shift_outer(front_half[1])
-    out_step = next_step(out_step, out_slice(2))
+    out_step = next_sum(out_step, out_away[1])
     piece_block = pl.BlockSpec((chips * depth, columns), lambda s, o: (0, 0))
     grad_normed = pl.pallas_call(
-        functools.partial(project_back_kernel, outer),
-        out_shape=shape((together, model), bf16),
+        functools.partial(project_back_kernel, outer, chips),
+        out_shape=[shape((count, model), bf16)] * chips,
         grid_spec=pltpu.PrefetchScalarGridSpec(
             num_scalar_prefetch=1,
             grid=(outer,),
@@ -1041,21 +1059,55 @@
                 *[piece_block] * (CORES * outer),
                 pl.BlockSpec((plane * depth, plane * depth), lambda s, o: (0, 0)),
             ],
-            out_specs=pl.BlockSpec(
-                (together, plane * depth), lambda s, o: (0, lax.rem(o[0] + outer - s, outer))
-            ),
+            out_specs=[
+                pl.BlockSpec(
+                    (count, plane * depth), lambda s, o: (0, lax.rem(o[0] + outer - s, outer))
+                )
+            ]
+            * chips,
         ),
         compiler_params=pltpu.CompilerParams(vmem_limit_bytes=32 * MEBIBYTE),
     )(
         outer_scalar,
-        after(grad_front_low, front_half),
+        after(grad_front_low, *front_half),
         *front_pieces,
         *front_others,
         front_order,
     )
+    first_gain_term = call(gain_back_kernel, shape((1, model), f32))(*grad_normed, *token_parts)
+    gain_sums = jnp.concatenate(
+        [first_gain_term.reshape(-1), second_gain_term.reshape(-1), gain_terms.reshape(-1)]
+    ).reshape(-1, LANES)
+    gain_sums = gain_sums + swap_core(gain_sums)
     for s in range(3, outer):
         moved_own[s], partner = settle(picks[s], moved[s])
         moved_partner[s] = swap_core(partner)
+    state = (front_half, front_step, out_step, grad_normed, moved_own, moved_partner)
+    state, gain_sums = fence((state, gain_sums))
+    front_half, front_step, out_step, grad_normed, moved_own, moved_partner = state
+    front_step = next_sum(front_step, front_half[2])
+    for s in range(3, outer):
+        out_step = next_sum(out_step, out_away[s - 1])
+    arrived = [swap_chip(grad_normed[r], r) for r in range(1, chips)]
+    router_part = lax.dot_general(
+        after(grad_logits_low, *grad_normed)[:, :experts],
+        second_wide[:, :model],
+        CONTRACT_ROWS,
+        preferred_element_type=f32,
+    )
+    router_part = scatter_outer(
+        lambda o: lax.dynamic_slice_in_dim(router_part, o * (plane * depth), plane * depth, 1)
+    )
+    state = (front_step, out_step, arrived, router_part)
+    front_step, out_step, arrived, router_part = fence(state)
+    for s in range(3, outer):
+        front_step = next_sum(front_step, front_half[s])
+        moved_step = next_step(moved_step, moved_own[s], moved_partner[s])
+    moved[0] = spread(moving[0])
+    tokens_grad = call(tokens_back_kernel, shape((count, model), f32))(
+        tokens, grad_normed[0], *arrived, grad_hidden, first_gain_row
+    )
+    gain_sums = sum([swap_chip(gain_sums, r) for r in range(1, chips)], gain_sums)
     router_part = sum(
         [
             swap_chip(
@@ -1067,44 +1119,23 @@
             for r in range(chips)
         ]
     )
-    state = (front_half, front_step, out_step, grad_normed, moved_own, moved_partner)
-    state, router_part = fence((state, router_part))
-    front_half, front_step, out_step, grad_normed, moved_own, moved_partner = state
-    front_step = next_step(front_step, front_half[2])
-    for s in range(3, outer):
-        out_step = next_step(out_step, out_slice(s))
-    arrived = [swap_chip(grad_normed[r * count : (r + 1) * count], r) for r in range(1, chips)]
-    first_gain_term = call(gain_back_kernel, shape((1, model), f32))(grad_normed, *token_parts)
-    gain_sums = jnp.concatenate(
-        [first_gain_term.reshape(-1), second_gain_term.reshape(-1), gain_terms.reshape(-1)]
-    ).reshape(-1, LANES)
-    gain_sums = gain_sums + swap_core(gain_sums)
+    out_grad = out_step.astype(f32) + out_home.astype(f32)
+    state = (front_step, moved_step, moved, gain_sums, router_part, tokens_grad, out_grad)
+    front_step, moved_step, moved, gain_sums, router_part, tokens_grad, out_grad = fence(state)
+    moved_own[0], partner = settle(picks[0], moved[0])
+    moved_partner[0] = swap_core(partner)
+    output = hidden + moved_own[0] + moved_partner[0].astype(f32) + moved_step.astype(f32)
+    output = output.astype(bf16)
+    front = (front_step.astype(f32) + front_half[0].astype(f32)).astype(bf16)
+    front = front.reshape(chips, depth, columns)
+    front = [swap_chip(front[r], r) for r in range(chips)]
+    front, gain_sums, router_part = fence((front, gain_sums, router_part))
+    gain_sums = sum([shift_outer(gain_sums, s) for s in range(1, outer)], gain_sums).reshape(-1)
     router_grad = (
         lax.dynamic_slice_in_dim(router_part, my_core * depth, depth, 1)
         + swap_core(lax.dynamic_slice_in_dim(router_part, (1 - my_core) * depth, depth, 1))
     ).T
-    state = (front_step, out_step, arrived, gain_sums, router_grad)
-    front_step, out_step, arrived, gain_sums, router_grad = fence(state)
-    for s in range(3, outer):
-        front_step = next_step(front_step, front_half[s])
-        moved_step = next_step(moved_step, moved_own[s], moved_partner[s])
-    moved[0] = spread(moving[0])
-    tokens_grad = call(tokens_back_kernel, shape((count, model), f32))(
-        tokens, grad_normed[:count], *arrived, grad_hidden, first_gain_row
-    )
-    gain_sums = sum([swap_chip(gain_sums, r) for r in range(1, chips)], gain_sums)
-    out_grad = out_step.astype(f32) + out_slice(0).astype(f32)
-    state = (front_step, moved_step, moved, gain_sums, tokens_grad, out_grad)
-    front_step, moved_step, moved, gain_sums, tokens_grad, out_grad = fence(state)
-    moved_own[0], partner = settle(picks[0], moved[0])
-    moved_partner[0] = swap_core(partner)
-    output = hidden + moved_own[0] + moved_partner[0].astype(f32) + moved_step.astype(f32)
-    output = output.astype(bf16)
-    gain_sums = sum([shift_outer(gain_sums, s) for s in range(1, outer)], gain_sums).reshape(-1)
-    front = (front_step.astype(f32) + front_half[0].astype(f32)).astype(bf16)
-    front = front.reshape(chips, depth, columns)
-    front = by_chip([swap_chip(front[r], r) for r in range(chips)])
-    out_grad = out_step.astype(f32) + out_slice(0).astype(f32)
+    front = by_chip(front)
 
     def lay_out(first, last):
         return jnp.concatenate([part[:, first:last] for part in front], axis=1).astype(f32)

time: 642 us -> 631 us (0.983)
  local copies, waits for them, and re-layouts: 36.5 us -> 29.1 us
    ppermute x30, waiting for transfers between devices: 73.5 us -> 86.5 us  [shift_outer(): lax.ppermute(value, 'fsdp', [(i, (i // plane + s) % outer * plane + i % p...]
    ppermute x78, waiting for transfers between devices: 191 us -> 180 us  [swap_chip(): lax.ppermute(value, 'fsdp', [(i, i ^ r * CORES) for i in range(shards)])]
    unnamed x356 -> x338, local copies, waits for them, and re-layouts: 30 us -> 22.5 us
    pallas_call x2 -> x8, Pallas kernels: 8.85 us -> 15.5 us  [the longest x1 6.58 us: body(): pl.pallas_call(functools.partial(project_back_kernel, outer, chips), out_...]
  transfers between devices with their start and end apart: 133 -> 133, of which waited for: 55 -> 56; matrix products, arithmetic and copies ran while one was open for 8% -> 6% of each run, Pallas kernels for 21% -> 22%
where the time goes in v4:
time: 631 us; the launch traced here: 624 us
  waiting for transfers between devices  268 us (42%)
  Pallas kernels  148 us (23%)
  starting transfers between devices  134 us (21%)
  local copies, waits for them, and re-layouts  29.1 us (5%)
  other arithmetic  28.9 us (5%)
  matrix products  11.5 us (2%)
    ppermute x78, waiting for transfers between devices, swap_chip(): lax.ppermute(value, 'fsdp', [(i, i ^ r * CORES) for i in range(shards)])  180 us
    ppermute x78, starting transfers between devices, swap_chip(): lax.ppermute(value, 'fsdp', [(i, i ^ r * CORES) for i in range(shards)])  94.4 us
    ppermute x30, waiting for transfers between devices, shift_outer(): lax.ppermute(value, 'fsdp', [(i, (i // plane + s) % outer * plane + i % p...  86.5 us
    pallas_call x4, Pallas kernels, expert(): call(functools.partial(expert_kernel, chips, experts), [shape((part_rows,...  44.5 us
    ppermute x30, starting transfers between devices, shift_outer(): lax.ppermute(value, 'fsdp', [(i, (i // plane + s) % outer * plane + i % p...  37.7 us
    unnamed x338, local copies, waits for them, and re-layouts  22.5 us
    pallas_call x1, Pallas kernels, body(): call(functools.partial(expert_grad_kernel, outer, chips), (shape((model,...  20.7 us
    pallas_call x1, Pallas kernels, body(): call(functools.partial(attend_back_kernel, scale), (shape((together, colu...  18.7 us
  transfers between devices with their start and end apart: 133, of which 56 were waited for; matrix products, arithmetic and copies ran while one was open for 6% of the time, Pallas kernels for 22%

profile of v4, /device:TPU:0, one launch (start us, length us, event | category | flops | bytes accessed | tf_op | source)
XLA Modules:
  0.0 624.0 jit_solution(12261944370124017029)
XLA Ops:
  29.2 19.9 %collective-permute-done.10 = bf16[128,2048]{1,0:T(8,128)(2,1)} collective-permute-done((bf16[128,2048]{1,0:T(8,128)(2,1)}, bf16[128,2048]{1,0:T(8,128)(2,1)}, u32[]{:S(2)}, u32[]{:S(2)}) %collective-permute-start.10) | collective-permute-done | bytes 524320 | tf_op jit(solution)/shard_map/ppermute | solution.py:552
  59.1 10.2 %collective-permute-done.14.refs_3_.refs_7_ = bf16[128,2048]{1,0:T(8,128)(2,1)S(1)} collective-permute-done((bf16[128,2048]{1,0:T(8,128)(2,1)S(1)}, bf16[128,2048]{1,0:T(8,128)(2,1)S(1)}, u32[]{:S(2)}, u32[]{:S(2)}) %collective-permute-start.14) | collective-permute-done | bytes 524320 | tf_op jit(solution)/shard_map/ppermute | solution.py:547
  79.8 6.5 %collective-permute-done.13.refs_7_.refs_19_ = bf16[80,2048]{1,0:T(8,128)(2,1)S(1)} collective-permute-done((bf16[80,2048]{1,0:T(8,128)(2,1)S(1)}, bf16[80,2048]{1,0:T(8,128)(2,1)S(1)}, u32[]{:S(2)}, u32[]{:S(2)}) %collective-permute-start.13) | collective-permute-done | bytes 327712 | tf_op jit(solution)/shard_map/ppermute | solution.py:547
  95.1 13.8 %collective-permute-done.21.refs_3_ = bf16[256,1408]{1,0:T(8,128)(2,1)} collective-permute-done((bf16[256,1408]{1,0:T(8,128)(2,1)S(1)}, bf16[256,1408]{1,0:T(8,128)(2,1)}, u32[]{:S(2)}, u32[]{:S(2)}) %collective-permute-start.21) | collective-permute-done | bytes 720928 | tf_op jit(solution)/shard_map/ppermute | solution.py:552
  123.3 5.7 shard_map.265.front
  134.9 13.5 %shard_map.266 = (bf16[512,1024]{1,0:T(8,128)(2,1)S(1)}, bf16[512,128]{1,0:T(8,128)(2,1)S(1)}, bf16[512,128]{1,0:T(8,128)(2,1)S(1)}, bf16[512,1024]{1,0:T(8,128)(2,1)S(1)}) custom-call(f32[512,1280]{1,0:T(8,128)S(1)} %shard_map.265.front, f32[512,128]{1,0:T(8,128)S(1)} %copy-done.37, f32[512,128]{1,0:T(8,128)S(1)} %copy-done.39, f32[512,128]{1,0:T(8,128)S(1)} %copy-done.41, ...), custom_call_target="tpu_custom_call" | custom-call | tf_op jit(solution)/shard_map/pallas_call | solution.py:756
  159.6 10.2 %collective-permute-done.30.refs_2_ = bf16[128,2048]{1,0:T(8,128)(2,1)S(1)} collective-permute-done((bf16[128,2048]{1,0:T(8,128)(2,1)S(1)}, bf16[128,2048]{1,0:T(8,128)(2,1)S(1)}, u32[]{:S(2)}, u32[]{:S(2)}) %collective-permute-start.30) | collective-permute-done | bytes 524320 | tf_op jit(solution)/shard_map/ppermute | solution.py:547
  169.8 10.2 %collective-permute-done.31.refs_3_ = bf16[128,2048]{1,0:T(8,128)(2,1)S(1)} collective-permute-done((bf16[128,2048]{1,0:T(8,128)(2,1)S(1)}, bf16[128,2048]{1,0:T(8,128)(2,1)S(1)}, u32[]{:S(2)}, u32[]{:S(2)}) %collective-permute-start.31) | collective-permute-done | bytes 524320 | tf_op jit(solution)/shard_map/ppermute | solution.py:547
  192.7 10.7 %collective-permute-done.39.refs_6_.refs_26_ = bf16[80,2048]{1,0:T(8,128)(2,1)S(1)} collective-permute-done((bf16[80,2048]{1,0:T(8,128)(2,1)S(1)}, bf16[80,2048]{1,0:T(8,128)(2,1)S(1)}, u32[]{:S(2)}, u32[]{:S(2)}) %collective-permute-start.39) | collective-permute-done | bytes 327712 | tf_op jit(solution)/shard_map/ppermute | solution.py:547
  223.9 5.6 collective-permute-done.46.refs_1_
  242.2 11.0 %shard_map.274 = (bf16[80,2176]{1,0:T(8,128)(2,1)S(1)}, bf16[80,2176]{1,0:T(8,128)(2,1)S(1)}, bf16[80,2176]{1,0:T(8,128)(2,1)S(1)}, bf16[80,2176]{1,0:T(8,128)(2...) custom-call(s32[1]{0:T(128)} %bitcast.36.me, ...), custom_call_target="tpu_custom_call" | custom-call | flops 11000000512 | bytes 22000000 | tf_op jit(solution)/shard_map/pallas_call | solution.py:822
  262.5 6.6 %collective-permute-done.55.refs_1_.refs_9_ = bf16[80,2176]{1,0:T(8,128)(2,1)S(1)} collective-permute-done((bf16[80,2176]{1,0:T(8,128)(2,1)S(1)}, bf16[80,2176]{1,0:T(8,128)(2,1)S(1)}, u32[]{:S(2)}, u32[]{:S(2)}) %collective-permute-start.55) | collective-permute-done | bytes 348192 | tf_op jit(solution)/shard_map/ppermute | solution.py:547
  270.4 5.9 collective-permute-done.56.refs_2_.refs_10_
  276.8 11.0 %shard_map.276 = (bf16[80,2176]{1,0:T(8,128)(2,1)S(1)}, bf16[80,2176]{1,0:T(8,128)(2,1)S(1)}, bf16[80,2176]{1,0:T(8,128)(2,1)S(1)}, bf16[80,2176]{1,0:T(8,128)(2...) custom-call(s32[1]{0:T(128)} %bitcast.36.me, ...), custom_call_target="tpu_custom_call" | custom-call | flops 11000000512 | bytes 22000000 | tf_op jit(solution)/shard_map/pallas_call | solution.py:822
  302.1 5.8 collective-permute-done.62.refs_2_.refs_14_
  310.3 11.4 %shard_map.278 = (bf16[80,2176]{1,0:T(8,128)(2,1)S(1)}, bf16[80,2176]{1,0:T(8,128)(2,1)S(1)}, bf16[80,2176]{1,0:T(8,128)(2,1)S(1)}, bf16[80,2176]{1,0:T(8,128)(2...) custom-call(s32[1]{0:T(128)} %bitcast.36.me, ...), custom_call_target="tpu_custom_call" | custom-call | flops 11000000512 | bytes 22000000 | tf_op jit(solution)/shard_map/pallas_call | solution.py:822
  328.1 11.0 %shard_map.280 = (bf16[80,2176]{1,0:T(8,128)(2,1)S(1)}, bf16[80,2176]{1,0:T(8,128)(2,1)S(1)}, bf16[80,2176]{1,0:T(8,128)(2,1)S(1)}, bf16[80,2176]{1,0:T(8,128)(2...) custom-call(s32[1]{0:T(128)} %bitcast.36.me, ...), custom_call_target="tpu_custom_call" | custom-call | flops 11000000512 | bytes 22000000 | tf_op jit(solution)/shard_map/pallas_call | solution.py:822
  356.0 6.5 %collective-permute-done.73.refs_2_ = bf16[80,2176]{1,0:T(8,128)(2,1)S(1)} collective-permute-done((bf16[80,2176]{1,0:T(8,128)(2,1)S(1)}, bf16[80,2176]{1,0:T(8,128)(2,1)S(1)}, u32[]{:S(2)}, u32[]{:S(2)}) %collective-permute-start.73) | collective-permute-done | bytes 348192 | tf_op jit(solution)/shard_map/ppermute | solution.py:547
  370.7 7.0 %collective-permute-done.78.refs_1_ = bf16[80,2048]{1,0:T(8,128)(2,1)S(1)} collective-permute-done((bf16[80,2048]{1,0:T(8,128)(2,1)S(1)}, bf16[80,2048]{1,0:T(8,128)(2,1)S(1)}, u32[]{:S(2)}, u32[]{:S(2)}) %collective-permute-start.78) | collective-permute-done | bytes 327712 | tf_op jit(solution)/shard_map/ppermute | solution.py:547
  377.8 6.1 collective-permute-done.79.refs_2_
  390.9 7.0 %collective-permute-done.82.refs_1_ = bf16[80,2048]{1,0:T(8,128)(2,1)S(1)} collective-permute-done((bf16[80,2048]{1,0:T(8,128)(2,1)S(1)}, bf16[80,2048]{1,0:T(8,128)(2,1)S(1)}, u32[]{:S(2)}, u32[]{:S(2)}) %collective-permute-start.82) | collective-permute-done | bytes 327712 | tf_op jit(solution)/shard_map/ppermute | solution.py:547
  398.7 5.5 collective-permute-done.83.refs_2_
  419.1 20.7 %shard_map.290 = (f32[2048,768]{1,0:T(8,128)}, f32[2048,768]{1,0:T(8,128)}, f32[768,2048]{1,0:T(8,128)}) custom-call(bf16[80,2176]{1,0:T(8,128)(2,1)} %copy-done.91, bf16[80,2176]{1,0:T(8,128)(2,1)} %copy-done.92, bf16[80,2176]{1,0:T(8,128)(2,1)} %copy-done.93, bf16[80,2176]{1,0:T(8,128)(2,1)} %copy-done.94, bf16[80,2176]{1,0:T(8,128)(2,1)} %copy-done.95, ...), custom_call_target="tpu_custom_call" | custom-call | flops 20000000000 | bytes 40000000 | tf_op jit(solution)/shard_map/pallas_call | solution.py:918
  455.2 18.7 %shard_map.292 = (bf16[512,1280]{1,0:T(8,128)(2,1)S(1)}, f32[2,128]{1,0:T(2,128)S(1)}) custom-call(f32[512,1280]{1,0:T(8,128)S(1)} %shard_map.265.front, bf16[512,1024]{1,0:T(8,128)(2,1)S(1)} %copy-done.90, bf16[512,128]{1,0:T(8,128)(2,1)S(1)} %copy-done.140, bf16[512,128]{1,0:T(8,128)(2,1)S(1)} %copy-done.142, ...), custom_call_target="tpu_custom_call" | custom-call | flops 17999998976 | bytes 36000000 | tf_op jit(solution)/shard_map/pallas_call | solution.py:973
  488.1 6.4 %collective-permute-done.100.refs_3_ = bf16[80,2048]{1,0:T(8,128)(2,1)S(1)} collective-permute-done((bf16[80,2048]{1,0:T(8,128)(2,1)S(1)}, bf16[80,2048]{1,0:T(8,128)(2,1)S(1)}, u32[]{:S(2)}, u32[]{:S(2)}) %collective-permute-start.100) | collective-permute-done | bytes 327712 | tf_op jit(solution)/shard_map/ppermute | solution.py:547
  494.5 5.9 collective-permute-done.98.refs_1_
  509.1 6.6 %shard_map.296 = (bf16[128,2048]{1,0:T(8,128)(2,1)S(1)}, bf16[128,2048]{1,0:T(8,128)(2,1)S(1)}, bf16[128,2048]{1,0:T(8,128)(2,1)S(1)}, bf16[128,2048]{1,0:T(8,128)(2,1)S(1)}) custom-call(s32[1]{0:T(128)} %bitcast.31.my_outer, bf16[512,1280]{1,0:T(8,128)(2,1)S(1)} %get-tuple-element.1517.grad, bf16[256,1408]{1,0:T(8,128)(2,1)S(1)} %copy-done.8, ...), custom_call_target="tpu_custom_call" | custom-call | tf_op jit(solution)/shard_map/pallas_call | solution.py:1051
  520.2 12.9 %collective-permute-done.103.first = bf16[128,2048]{1,0:T(8,128)(2,1)} collective-permute-done((bf16[128,2048]{1,0:T(8,128)(2,1)}, bf16[128,2048]{1,0:T(8,128)(2,1)}, u32[]{:S(2)}, u32[]{:S(2)}) %collective-permute-start.103) | collective-permute-done | bytes 524320 | tf_op jit(solution)/shard_map/ppermute | solution.py:552
  550.2 11.6 %collective-permute-done.107 = bf16[128,2048]{1,0:T(8,128)(2,1)S(1)} collective-permute-done((bf16[128,2048]{1,0:T(8,128)(2,1)S(1)}, bf16[128,2048]{1,0:T(8,128)(2,1)S(1)}, u32[]{:S(2)}, u32[]{:S(2)}) %collective-permute-start.107) | collective-permute-done | bytes 524320 | tf_op jit(solution)/shard_map/ppermute | solution.py:552
  565.8 6.7 %collective-permute-done.106.first = bf16[256,1280]{1,0:T(8,128)(2,1)S(1)} collective-permute-done((bf16[256,1280]{1,0:T(8,128)(2,1)S(1)}, bf16[256,1280]{1,0:T(8,128)(2,1)S(1)}, u32[]{:S(2)}, u32[]{:S(2)}) %collective-permute-start.106) | collective-permute-done | bytes 655392 | tf_op jit(solution)/shard_map/ppermute | solution.py:552
  587.2 11.0 %collective-permute-done.115 = bf16[128,2048]{1,0:T(8,128)(2,1)S(1)} collective-permute-done((bf16[128,2048]{1,0:T(8,128)(2,1)S(1)}, bf16[128,2048]{1,0:T(8,128)(2,1)S(1)}, u32[]{:S(2)}, u32[]{:S(2)}) %collective-permute-start.115) | collective-permute-done | bytes 524320 | tf_op jit(solution)/shard_map/ppermute | solution.py:552
  598.2 7.0 %collective-permute-done.114 = bf16[256,1280]{1,0:T(8,128)(2,1)S(1)} collective-permute-done((bf16[256,1280]{1,0:T(8,128)(2,1)S(1)}, bf16[256,1280]{1,0:T(8,128)(2,1)S(1)}, u32[]{:S(2)}, u32[]{:S(2)}) %collective-permute-start.114) | collective-permute-done | bytes 655392 | tf_op jit(solution)/shard_map/ppermute | solution.py:552
  (712 shorter events, 311.6 us)
Async XLA Ops:
  19.3 36.1 %collective-permute-start.8 = (bf16[256,1408]{1,0:T(8,128)(2,1)S(1)}, bf16[256,1408]{1,0:T(8,128)(2,1)S(1)}, u32[]{:S(2)}, u32[]{:S(2)}) collective-permute-start(bf16[256,1408]{1,0:T(8,128)(2,1)S(1)} %constant_dynamic-update-slice_fusion.refs_0_), channel_id=1, source_target_pairs={{0,8},{1,9},{2,10},{3,11},{4,12},{5,13},{6,14},{7,15},{8,16},{9,17... | collective-permute-start | bytes 2162696 | tf_op jit(solution)/shard_map/ppermute | solution.py:552
  21.0 34.5 %collective-permute-start.9 = (bf16[256,1408]{1,0:T(8,128)(2,1)S(1)}, bf16[256,1408]{1,0:T(8,128)(2,1)S(1)}, u32[]{:S(2)}, u32[]{:S(2)}) collective-permute-start(bf16[256,1408]{1,0:T(8,128)(2,1)S(1)} %constant_dynamic-update-slice_fusion.refs_0_), channel_id=1, source_target_pairs={{0,1},{1,0},{2,3},{3,2},{4,5},{5,4},{6,7},{7,6},{8,9},{9,8},{10,11... | collective-permute-start | bytes 2162696 | tf_op jit(solution)/shard_map/ppermute | solution.py:542
  21.3 32.4 %collective-permute-start.5 = (bf16[128,2048]{1,0:T(8,128)(2,1)S(1)}, bf16[128,2048]{1,0:T(8,128)(2,1)}, u32[]{:S(2)}, u32[]{:S(2)}) collective-permute-start(bf16[128,2048]{1,0:T(8,128)(2,1)S(1)} %copy-done.5), channel_id=1, source_target_pairs={{0,2},{1,3},{2,0},{3,1},{4,6},{5,7},{6,4},{7,5},{8,10},{9,11},{10,... | collective-permute-start | bytes 1572872 | tf_op jit(solution)/shard_map/ppermute | solution.py:547
  22.5 32.9 %collective-permute-start.6 = (bf16[128,2048]{1,0:T(8,128)(2,1)S(1)}, bf16[128,2048]{1,0:T(8,128)(2,1)}, u32[]{:S(2)}, u32[]{:S(2)}) collective-permute-start(bf16[128,2048]{1,0:T(8,128)(2,1)S(1)} %copy-done.5), channel_id=1, source_target_pairs={{0,4},{1,5},{2,6},{3,7},{4,0},{5,1},{6,2},{7,3},{8,12},{9,13},{10,... | collective-permute-start | bytes 1572872 | tf_op jit(solution)/shard_map/ppermute | solution.py:547
  24.9 24.1 %collective-permute-start.10 = (bf16[128,2048]{1,0:T(8,128)(2,1)}, bf16[128,2048]{1,0:T(8,128)(2,1)}, u32[]{:S(2)}, u32[]{:S(2)}) collective-permute-start(bf16[128,2048]{1,0:T(8,128)(2,1)} %collective-permute-done.3), channel_id=1, source_target_pairs={{0,8},{1,9},{2,10},{3,11},{4,12},{5,13},{6,14},{7,15},{8,16},{9,17... | collective-permute-start | bytes 1572872 | tf_op jit(solution)/shard_map/ppermute | solution.py:552
  55.4 31.5 %collective-permute-start.15 = (bf16[256,1408]{1,0:T(8,128)(2,1)S(1)}, bf16[256,1408]{1,0:T(8,128)(2,1)S(1)}, u32[]{:S(2)}, u32[]{:S(2)}) collective-permute-start(bf16[256,1408]{1,0:T(8,128)(2,1)S(1)} %collective-permute-done.8.refs_1_), channel_id=1, source_target_pairs={{0,8},{1,9},{2,10},{3,11},{4,12},{5,13},{6,14},{7,15},{8,16},{9,17... | collective-permute-start | bytes 2162696 | tf_op jit(solution)/shard_map/ppermute | solution.py:552
  55.5 31.5 %collective-permute-start.16 = (bf16[256,1408]{1,0:T(8,128)(2,1)S(1)}, bf16[256,1408]{1,0:T(8,128)(2,1)S(1)}, u32[]{:S(2)}, u32[]{:S(2)}) collective-permute-start(bf16[256,1408]{1,0:T(8,128)(2,1)S(1)} %collective-permute-done.8.refs_1_), channel_id=1, source_target_pairs={{0,1},{1,0},{2,3},{3,2},{4,5},{5,4},{6,7},{7,6},{8,9},{9,8},{10,11... | collective-permute-start | bytes 2162696 | tf_op jit(solution)/shard_map/ppermute | solution.py:542
  58.5 28.5 %collective-permute-start.17 = (bf16[128,2048]{1,0:T(8,128)(2,1)}, bf16[128,2048]{1,0:T(8,128)(2,1)S(1)}, u32[]{:S(2)}, u32[]{:S(2)}) collective-permute-start(bf16[128,2048]{1,0:T(8,128)(2,1)} %collective-permute-done.10), channel_id=1, source_target_pairs={{0,8},{1,9},{2,10},{3,11},{4,12},{5,13},{6,14},{7,15},{8,16},{9,17... | collective-permute-start | bytes 1572872 | tf_op jit(solution)/shard_map/ppermute | solution.py:552
  88.3 30.9 %collective-permute-start.4 = (bf16[128,2176]{1,0:T(8,128)(2,1)S(1)}, bf16[128,2176]{1,0:T(8,128)(2,1)}, u32[]{:S(2)}, u32[]{:S(2)}) collective-permute-start(bf16[128,2176]{1,0:T(8,128)(2,1)S(1)} %pad_maximum_fusion.4.own), channel_id=1, source_target_pairs={{0,8},{1,9},{2,10},{3,11},{4,12},{5,13},{6,14},{7,15},{8,16},{9,17... | collective-permute-start | bytes 1671176 | tf_op jit(solution)/shard_map/ppermute | solution.py:552
  93.0 26.1 %collective-permute-start.18 = (bf16[128,2048]{1,0:T(8,128)(2,1)}, bf16[128,2048]{1,0:T(8,128)(2,1)S(1)}, u32[]{:S(2)}, u32[]{:S(2)}) collective-permute-start(bf16[128,2048]{1,0:T(8,128)(2,1)} %get-tuple-element.1594), channel_id=1, source_target_pairs={{0,2},{1,3},{2,0},{3,1},{4,6},{5,7},{6,4},{7,5},{8,10},{9,11},{10,... | collective-permute-start | bytes 1572872 | tf_op jit(solution)/shard_map/ppermute | solution.py:547
  94.5 24.6 %collective-permute-start.19 = (bf16[128,2048]{1,0:T(8,128)(2,1)}, bf16[128,2048]{1,0:T(8,128)(2,1)}, u32[]{:S(2)}, u32[]{:S(2)}) collective-permute-start(bf16[128,2048]{1,0:T(8,128)(2,1)} %get-tuple-element.1593), channel_id=1, source_target_pairs={{0,4},{1,5},{2,6},{3,7},{4,0},{5,1},{6,2},{7,3},{8,12},{9,13},{10,... | collective-permute-start | bytes 1572872 | tf_op jit(solution)/shard_map/ppermute | solution.py:547
  122.8 25.7 %collective-permute-start.25 = (bf16[512,2048]{1,0:T(8,128)(2,1)S(1)}, bf16[512,2048]{1,0:T(8,128)(2,1)S(1)}, u32[]{:S(2)}, u32[]{:S(2)}) collective-permute-start(bf16[512,2048]{1,0:T(8,128)(2,1)S(1)} %pad_maximum_fusion.1), channel_id=1, source_target_pairs={{0,1},{1,0},{2,3},{3,2},{4,5},{5,4},{6,7},{7,6},{8,9},{9,8},{10,11... | collective-permute-start | bytes 6291464 | tf_op jit(solution)/shard_map/ppermute | solution.py:542
  123.0 25.5 %collective-permute-start.26 = (bf16[128,2176]{1,0:T(8,128)(2,1)}, bf16[128,2176]{1,0:T(8,128)(2,1)S(1)}, u32[]{:S(2)}, u32[]{:S(2)}) collective-permute-start(bf16[128,2176]{1,0:T(8,128)(2,1)} %collective-permute-done.4.own), channel_id=1, source_target_pairs={{0,8},{1,9},{2,10},{3,11},{4,12},{5,13},{6,14},{7,15},{8,16},{9,17... | collective-permute-start | bytes 1671176 | tf_op jit(solution)/shard_map/ppermute | solution.py:552
  150.7 30.6 %collective-permute-start.33 = (bf16[128,2176]{1,0:T(8,128)(2,1)S(1)}, bf16[128,2176]{1,0:T(8,128)(2,1)S(1)}, u32[]{:S(2)}, u32[]{:S(2)}) collective-permute-start(bf16[128,2176]{1,0:T(8,128)(2,1)S(1)} %collective-permute-done.26.own), channel_id=1, source_target_pairs={{0,8},{1,9},{2,10},{3,11},{4,12},{5,13},{6,14},{7,15},{8,16},{9,17... | collective-permute-start | bytes 1671176 | tf_op jit(solution)/shard_map/ppermute | solution.py:552
  153.4 27.9 %collective-permute-start.34 = (bf16[128,2176]{1,0:T(8,128)(2,1)S(1)}, bf16[128,2176]{1,0:T(8,128)(2,1)S(1)}, u32[]{:S(2)}, u32[]{:S(2)}) collective-permute-start(bf16[128,2176]{1,0:T(8,128)(2,1)S(1)} %collective-permute-done.26.own), channel_id=1, source_target_pairs={{0,1},{1,0},{2,3},{3,2},{4,5},{5,4},{6,7},{7,6},{8,9},{9,8},{10,11... | collective-permute-start | bytes 1671176 | tf_op jit(solution)/shard_map/ppermute | solution.py:542
  207.8 27.9 %collective-permute-start.41 = (bf16[128,2176]{1,0:T(8,128)(2,1)S(1)}, bf16[128,2176]{1,0:T(8,128)(2,1)S(1)}, u32[]{:S(2)}, u32[]{:S(2)}) collective-permute-start(bf16[128,2176]{1,0:T(8,128)(2,1)S(1)} %collective-permute-done.35.own), channel_id=1, source_target_pairs={{0,8},{1,9},{2,10},{3,11},{4,12},{5,13},{6,14},{7,15},{8,16},{9,17... | collective-permute-start | bytes 1671176 | tf_op jit(solution)/shard_map/ppermute | solution.py:552
  209.8 25.9 %collective-permute-start.42 = (bf16[128,2176]{1,0:T(8,128)(2,1)S(1)}, bf16[128,2176]{1,0:T(8,128)(2,1)S(1)}, u32[]{:S(2)}, u32[]{:S(2)}) collective-permute-start(bf16[128,2176]{1,0:T(8,128)(2,1)S(1)} %collective-permute-done.35.own), channel_id=1, source_target_pairs={{0,1},{1,0},{2,3},{3,2},{4,5},{5,4},{6,7},{7,6},{8,9},{9,8},{10,11... | collective-permute-start | bytes 1671176 | tf_op jit(solution)/shard_map/ppermute | solution.py:542
  260.2 27.7 %collective-permute-start.57 = (bf16[80,2176]{1,0:T(8,128)(2,1)S(1)}, bf16[80,2176]{1,0:T(8,128)(2,1)S(1)}, u32[]{:S(2)}, u32[]{:S(2)}) collective-permute-start(bf16[80,2176]{1,0:T(8,128)(2,1)S(1)} %get-tuple-element.993), channel_id=1, source_target_pairs={{0,6},{1,7},{2,4},{3,5},{4,2},{5,3},{6,0},{7,1},{8,14},{9,15},{10,... | collective-permute-start | bytes 1044488 | tf_op jit(solution)/shard_map/ppermute | solution.py:547
  261.6 29.3 %collective-permute-start.54 = (bf16[128,2176]{1,0:T(8,128)(2,1)S(1)}, bf16[128,2176]{1,0:T(8,128)(2,1)S(1)}, u32[]{:S(2)}, u32[]{:S(2)}) collective-permute-start(bf16[128,2176]{1,0:T(8,128)(2,1)S(1)} %collective-permute-done.49.own), channel_id=1, source_target_pairs={{0,1},{1,0},{2,3},{3,2},{4,5},{5,4},{6,7},{7,6},{8,9},{9,8},{10,11... | collective-permute-start | bytes 1671176 | tf_op jit(solution)/shard_map/ppermute | solution.py:542
  261.6 26.4 %collective-permute-start.58 = (bf16[80,2176]{1,0:T(8,128)(2,1)S(1)}, bf16[80,2176]{1,0:T(8,128)(2,1)S(1)}, u32[]{:S(2)}, u32[]{:S(2)}) collective-permute-start(bf16[80,2176]{1,0:T(8,128)(2,1)S(1)} %get-tuple-element.994), channel_id=1, source_target_pairs={{0,2},{1,3},{2,0},{3,1},{4,6},{5,7},{6,4},{7,5},{8,10},{9,11},{10,... | collective-permute-start | bytes 1044488 | tf_op jit(solution)/shard_map/ppermute | solution.py:547
  295.2 27.7 %collective-permute-start.67 = (bf16[128,2176]{1,0:T(8,128)(2,1)S(1)}, bf16[128,2176]{1,0:T(8,128)(2,1)S(1)}, u32[]{:S(2)}, u32[]{:S(2)}) collective-permute-start(bf16[128,2176]{1,0:T(8,128)(2,1)S(1)} %get-tuple-element.1051), channel_id=1, source_target_pairs={{0,1},{1,0},{2,3},{3,2},{4,5},{5,4},{6,7},{7,6},{8,9},{9,8},{10,11... | collective-permute-start | bytes 1671176 | tf_op jit(solution)/shard_map/ppermute | solution.py:542
  295.2 26.7 %collective-permute-start.63 = (bf16[80,2176]{1,0:T(8,128)(2,1)S(1)}, bf16[80,2176]{1,0:T(8,128)(2,1)S(1)}, u32[]{:S(2)}, u32[]{:S(2)}) collective-permute-start(bf16[80,2176]{1,0:T(8,128)(2,1)S(1)} %get-tuple-element.1037), channel_id=1, source_target_pairs={{0,6},{1,7},{2,4},{3,5},{4,2},{5,3},{6,0},{7,1},{8,14},{9,15},{10,... | collective-permute-start | bytes 1044488 | tf_op jit(solution)/shard_map/ppermute | solution.py:547
  296.8 25.0 %collective-permute-start.64 = (bf16[80,2176]{1,0:T(8,128)(2,1)S(1)}, bf16[80,2176]{1,0:T(8,128)(2,1)S(1)}, u32[]{:S(2)}, u32[]{:S(2)}) collective-permute-start(bf16[80,2176]{1,0:T(8,128)(2,1)S(1)} %get-tuple-element.1038), channel_id=1, source_target_pairs={{0,2},{1,3},{2,0},{3,1},{4,6},{5,7},{6,4},{7,5},{8,10},{9,11},{10,... | collective-permute-start | bytes 1044488 | tf_op jit(solution)/shard_map/ppermute | solution.py:547
  411.1 28.6 %collective-permute-start.87 = (bf16[128,2048]{1,0:T(8,128)(2,1)}, bf16[128,2048]{1,0:T(8,128)(2,1)}, u32[]{:S(2)}, u32[]{:S(2)}) collective-permute-start(bf16[128,2048]{1,0:T(8,128)(2,1)} %get-tuple-element.1375), channel_id=1, source_target_pairs={{0,2},{1,3},{2,0},{3,1},{4,6},{5,7},{6,4},{7,5},{8,10},{9,11},{10,... | collective-permute-start | bytes 1572872 | tf_op jit(solution)/shard_map/ppermute | solution.py:547
  412.1 27.6 %collective-permute-start.88 = (bf16[128,2048]{1,0:T(8,128)(2,1)}, bf16[128,2048]{1,0:T(8,128)(2,1)}, u32[]{:S(2)}, u32[]{:S(2)}) collective-permute-start(bf16[128,2048]{1,0:T(8,128)(2,1)} %get-tuple-element.1375), channel_id=1, source_target_pairs={{0,4},{1,5},{2,6},{3,7},{4,0},{5,1},{6,2},{7,3},{8,12},{9,13},{10,... | collective-permute-start | bytes 1572872 | tf_op jit(solution)/shard_map/ppermute | solution.py:547
  414.1 25.6 %collective-permute-start.89 = (bf16[128,2048]{1,0:T(8,128)(2,1)}, bf16[128,2048]{1,0:T(8,128)(2,1)}, u32[]{:S(2)}, u32[]{:S(2)}) collective-permute-start(bf16[128,2048]{1,0:T(8,128)(2,1)} %get-tuple-element.1375), channel_id=1, source_target_pairs={{0,6},{1,7},{2,4},{3,5},{4,2},{5,3},{6,0},{7,1},{8,14},{9,15},{10,... | collective-permute-start | bytes 1572872 | tf_op jit(solution)/shard_map/ppermute | solution.py:547
  416.9 24.8 %collective-permute-start.90 = (bf16[128,2048]{1,0:T(8,128)(2,1)}, bf16[128,2048]{1,0:T(8,128)(2,1)}, u32[]{:S(2)}, u32[]{:S(2)}) collective-permute-start(bf16[128,2048]{1,0:T(8,128)(2,1)} %add_convert_fusion.9), channel_id=1, source_target_pairs={{0,8},{1,9},{2,10},{3,11},{4,12},{5,13},{6,14},{7,15},{8,16},{9,17... | collective-permute-start | bytes 1572872 | tf_op jit(solution)/shard_map/ppermute | solution.py:552
  503.1 30.1 %collective-permute-start.102 = (bf16[256,1280]{1,0:T(8,128)(2,1)}, bf16[256,1280]{1,0:T(8,128)(2,1)}, u32[]{:S(2)}, u32[]{:S(2)}) collective-permute-start(bf16[256,1280]{1,0:T(8,128)(2,1)} %get-tuple-element.1512), channel_id=1, source_target_pairs={{0,8},{1,9},{2,10},{3,11},{4,12},{5,13},{6,14},{7,15},{8,16},{9,17... | collective-permute-start | bytes 1966088 | tf_op jit(solution)/shard_map/ppermute | solution.py:552
  506.9 26.2 %collective-permute-start.103 = (bf16[128,2048]{1,0:T(8,128)(2,1)}, bf16[128,2048]{1,0:T(8,128)(2,1)}, u32[]{:S(2)}, u32[]{:S(2)}) collective-permute-start(bf16[128,2048]{1,0:T(8,128)(2,1)} %shard_map.295), channel_id=1, source_target_pairs={{0,8},{1,9},{2,10},{3,11},{4,12},{5,13},{6,14},{7,15},{8,16},{9,17... | collective-permute-start | bytes 1572872 | tf_op jit(solution)/shard_map/ppermute | solution.py:552
  537.9 24.7 %collective-permute-start.108 = (bf16[128,2048]{1,0:T(8,128)(2,1)}, bf16[128,2048]{1,0:T(8,128)(2,1)S(1)}, u32[]{:S(2)}, u32[]{:S(2)}) collective-permute-start(bf16[128,2048]{1,0:T(8,128)(2,1)} %copy-done.57), channel_id=1, source_target_pairs={{0,2},{1,3},{2,0},{3,1},{4,6},{5,7},{6,4},{7,5},{8,10},{9,11},{10,... | collective-permute-start | bytes 1572872 | tf_op jit(solution)/shard_map/ppermute | solution.py:547
  538.7 25.4 %collective-permute-start.109 = (bf16[128,2048]{1,0:T(8,128)(2,1)}, bf16[128,2048]{1,0:T(8,128)(2,1)S(1)}, u32[]{:S(2)}, u32[]{:S(2)}) collective-permute-start(bf16[128,2048]{1,0:T(8,128)(2,1)} %copy-done.56), channel_id=1, source_target_pairs={{0,4},{1,5},{2,6},{3,7},{4,0},{5,1},{6,2},{7,3},{8,12},{9,13},{10,... | collective-permute-start | bytes 1572872 | tf_op jit(solution)/shard_map/ppermute | solution.py:547
  545.7 26.9 %collective-permute-start.106 = (bf16[256,1280]{1,0:T(8,128)(2,1)S(1)}, bf16[256,1280]{1,0:T(8,128)(2,1)S(1)}, u32[]{:S(2)}, u32[]{:S(2)}) collective-permute-start(bf16[256,1280]{1,0:T(8,128)(2,1)S(1)} %shard_map.299), channel_id=1, source_target_pairs={{0,8},{1,9},{2,10},{3,11},{4,12},{5,13},{6,14},{7,15},{8,16},{9,17... | collective-permute-start | bytes 1966088 | tf_op jit(solution)/shard_map/ppermute | solution.py:552
  (268 other events, 5477.4 us)

commit v5 on v4

--- a/solution.py
+++ b/solution.py
@@ -77,7 +77,13 @@
     scores = lax.dot_general(query, key, CONTRACT_LAST, preferred_element_type=jnp.float32)
     scores = jnp.where(allowed, scores * scale, NEGATIVE)
     exponent = jnp.exp(scores - jnp.max(scores, axis=-1, keepdims=True))
-    return exponent / jnp.sum(exponent, axis=-1, keepdims=True)
+    return exponent * (1.0 / jnp.sum(exponent, axis=-1, keepdims=True))
+
+
+def stacked(source, heads, width):
+    return jnp.concatenate(
+        [source[:, h * width : (h + 1) * width] for h in range(heads)], axis=0
+    )
 
 
 def norm_kernel(outer, my_outer, *refs):
@@ -197,21 +203,23 @@
     heads = query_out.shape[1] // width
     bf16 = jnp.bfloat16
     cos, sin = cosine[...], sine[...]
-    open_places = allowed[...] > 0.0
     key = head_rotated(
         front[:, heads * width : (heads + 1) * width], key_gain[...], cos, sin
     ).astype(bf16)
     value = front[:, (heads + 1) * width :].astype(bf16)
     key_out[...] = key
     value_out[...] = value
+    count = cos.shape[0]
+    all_cos, all_sin = (jnp.concatenate([table] * heads, axis=0) for table in (cos, sin))
+    all_places = jnp.concatenate([allowed[...]] * heads, axis=0) > 0.0
+    query = head_rotated(stacked(front, heads, width), query_gain[...], all_cos, all_sin)
+    query = query.astype(bf16)
+    shares = head_shares(query, key, all_places, scale).astype(bf16)
+    mixed = jnp.dot(shares, value, preferred_element_type=jnp.float32).astype(bf16)
     for h in range(heads):
-        part = slice(h * width, (h + 1) * width)
-        query = head_rotated(front[:, part], query_gain[...], cos, sin).astype(bf16)
-        query_out[:, part] = query
-        shares = head_shares(query, key, open_places, scale).astype(bf16)
-        context[:, part] = jnp.dot(
-            shares, value, preferred_element_type=jnp.float32
-        ).astype(bf16)
+        part, rows = slice(h * width, (h + 1) * width), slice(h * count, (h + 1) * count)
+        query_out[:, part] = query[rows, :]
+        context[:, part] = mixed[rows, :]
     context_out[...] = jnp.dot(
         context[...], order[...], preferred_element_type=jnp.float32
     ).astype(bf16)
@@ -244,29 +252,27 @@
     heads = query_in.shape[1] // width
     f32, bf16 = jnp.float32, jnp.bfloat16
     cos, sin = cosine[...], sine[...]
-    open_places = allowed[...] > 0.0
+    count = cos.shape[0]
+    all_cos, all_sin = (jnp.concatenate([table] * heads, axis=0) for table in (cos, sin))
+    all_places = jnp.concatenate([allowed[...]] * heads, axis=0) > 0.0
     key, value = key_in[...], value_in[...]
-    key_total = jnp.zeros(key.shape, f32)
-    value_total = jnp.zeros(key.shape, f32)
-    gain_total = jnp.zeros((1, width), f32)
+    query, grad = stacked(query_in, heads, width), stacked(context_grad, heads, width)
+    shares = head_shares(query, key, all_places, scale)
+    grad_shares = lax.dot_general(grad, value, CONTRACT_LAST, preferred_element_type=f32)
+    grad_scores = (
+        shares * (grad_shares - jnp.sum(shares * grad_shares, axis=-1, keepdims=True))
+    ).astype(bf16)
+    value_total = lax.dot_general(
+        shares.astype(bf16), grad, CONTRACT_ROWS, preferred_element_type=f32
+    )
+    key_total = lax.dot_general(grad_scores, query, CONTRACT_ROWS, preferred_element_type=f32)
+    grad_query = jnp.dot(grad_scores, key, preferred_element_type=f32) * scale
+    grad_query, gain_total = head_back(
+        grad_query, stacked(front, heads, width), query_gain[...], all_cos, all_sin
+    )
+    grad_query = grad_query.astype(bf16)
     for h in range(heads):
-        part = slice(h * width, (h + 1) * width)
-        query, grad = query_in[:, part], context_grad[:, part]
-        shares = head_shares(query, key, open_places, scale)
-        grad_shares = lax.dot_general(grad, value, CONTRACT_LAST, preferred_element_type=f32)
-        grad_scores = (
-            shares * (grad_shares - jnp.sum(shares * grad_shares, axis=-1, keepdims=True))
-        ).astype(bf16)
-        value_total += lax.dot_general(
-            shares.astype(bf16), grad, CONTRACT_ROWS, preferred_element_type=f32
-        )
-        key_total += lax.dot_general(
-            grad_scores, query, CONTRACT_ROWS, preferred_element_type=f32
-        )
-        grad_query = jnp.dot(grad_scores, key, preferred_element_type=f32) * scale
-        grad_query, gain_grad = head_back(grad_query, front[:, part], query_gain[...], cos, sin)
-        front_grad[:, part] = grad_query.astype(bf16)
-        gain_total += gain_grad
+        front_grad[:, h * width : (h + 1) * width] = grad_query[h * count : (h + 1) * count, :]
     part = slice(heads * width, (heads + 1) * width)
     grad_key, key_gain_grad = head_back(
         key_total * scale, front[:, part], key_gain[...], cos, sin

time: 631 us -> 630 us (level)
  Pallas kernels: 148 us -> 134 us
  starting transfers between devices: 134 us -> 143 us
    pallas_call x1, Pallas kernels: 18.7 us -> 9.93 us  [body(): call(functools.partial(attend_back_kernel, scale), (shape((together, colu...]
    ppermute x78, starting transfers between devices: 94.4 us -> 103 us  [swap_chip(): lax.ppermute(value, 'fsdp', [(i, i ^ r * CORES) for i in range(shards)])]
  transfers between devices with their start and end apart: 133 -> 133, of which waited for: 56 -> 50; matrix products, arithmetic and copies ran while one was open for 6% -> 6% of each run, Pallas kernels for 22% -> 20%
where the time goes in v5:
time: 630 us; the launch traced here: 624 us
  waiting for transfers between devices  273 us (43%)
  starting transfers between devices  143 us (23%)
  Pallas kernels  134 us (21%)
  local copies, waits for them, and re-layouts  29.2 us (5%)
  other arithmetic  28.9 us (5%)
  matrix products  11.5 us (2%)
    ppermute x78, waiting for transfers between devices, swap_chip(): lax.ppermute(value, 'fsdp', [(i, i ^ r * CORES) for i in range(shards)])  184 us
    ppermute x78, starting transfers between devices, swap_chip(): lax.ppermute(value, 'fsdp', [(i, i ^ r * CORES) for i in range(shards)])  103 us
    ppermute x30, waiting for transfers between devices, shift_outer(): lax.ppermute(value, 'fsdp', [(i, (i // plane + s) % outer * plane + i % p...  87.7 us
    pallas_call x4, Pallas kernels, expert(): call(functools.partial(expert_kernel, chips, experts), [shape((part_rows,...  44.5 us
    ppermute x30, starting transfers between devices, shift_outer(): lax.ppermute(value, 'fsdp', [(i, (i // plane + s) % outer * plane + i % p...  37.4 us
    unnamed x338, local copies, waits for them, and re-layouts  22.6 us
    pallas_call x1, Pallas kernels, body(): call(functools.partial(expert_grad_kernel, outer, chips), (shape((model,...  20.7 us
  transfers between devices with their start and end apart: 133, of which 50 were waited for; matrix products, arithmetic and copies ran while one was open for 6% of the time, Pallas kernels for 20%

profile of v5, /device:TPU:0, one launch (start us, length us, event | category | flops | bytes accessed | tf_op | source)
XLA Modules:
  0.0 623.7 jit_solution(1354410056421443541)
XLA Ops:
  29.2 19.9 %collective-permute-done.10 = bf16[128,2048]{1,0:T(8,128)(2,1)} collective-permute-done((bf16[128,2048]{1,0:T(8,128)(2,1)}, bf16[128,2048]{1,0:T(8,128)(2,1)}, u32[]{:S(2)}, u32[]{:S(2)}) %collective-permute-start.10) | collective-permute-done | bytes 524320 | tf_op jit(solution)/shard_map/ppermute | solution.py:558
  59.1 10.2 %collective-permute-done.14.refs_3_.refs_7_ = bf16[128,2048]{1,0:T(8,128)(2,1)S(1)} collective-permute-done((bf16[128,2048]{1,0:T(8,128)(2,1)S(1)}, bf16[128,2048]{1,0:T(8,128)(2,1)S(1)}, u32[]{:S(2)}, u32[]{:S(2)}) %collective-permute-start.14) | collective-permute-done | bytes 524320 | tf_op jit(solution)/shard_map/ppermute | solution.py:553
  79.8 6.5 %collective-permute-done.13.refs_7_.refs_19_ = bf16[80,2048]{1,0:T(8,128)(2,1)S(1)} collective-permute-done((bf16[80,2048]{1,0:T(8,128)(2,1)S(1)}, bf16[80,2048]{1,0:T(8,128)(2,1)S(1)}, u32[]{:S(2)}, u32[]{:S(2)}) %collective-permute-start.13) | collective-permute-done | bytes 327712 | tf_op jit(solution)/shard_map/ppermute | solution.py:553
  95.1 13.8 %collective-permute-done.21.refs_3_ = bf16[256,1408]{1,0:T(8,128)(2,1)} collective-permute-done((bf16[256,1408]{1,0:T(8,128)(2,1)S(1)}, bf16[256,1408]{1,0:T(8,128)(2,1)}, u32[]{:S(2)}, u32[]{:S(2)}) %collective-permute-start.21) | collective-permute-done | bytes 720928 | tf_op jit(solution)/shard_map/ppermute | solution.py:558
  123.3 5.7 shard_map.265.front
  134.9 8.0 %shard_map.266 = (bf16[512,1024]{1,0:T(8,128)(2,1)S(1)}, bf16[512,128]{1,0:T(8,128)(2,1)S(1)}, bf16[512,128]{1,0:T(8,128)(2,1)S(1)}, bf16[512,1024]{1,0:T(8,128)(2,1)S(1)}) custom-call(f32[512,1280]{1,0:T(8,128)S(1)} %shard_map.265.front, f32[512,128]{1,0:T(8,128)S(1)} %copy-done.37, f32[512,128]{1,0:T(8,128)S(1)} %copy-done.39, f32[512,128]{1,0:T(8,128)S(1)} %copy-done.41, ...), custom_call_target="tpu_custom_call" | custom-call | tf_op jit(solution)/shard_map/pallas_call | solution.py:762
  159.3 10.2 %collective-permute-done.30.refs_2_ = bf16[128,2048]{1,0:T(8,128)(2,1)S(1)} collective-permute-done((bf16[128,2048]{1,0:T(8,128)(2,1)S(1)}, bf16[128,2048]{1,0:T(8,128)(2,1)S(1)}, u32[]{:S(2)}, u32[]{:S(2)}) %collective-permute-start.30) | collective-permute-done | bytes 524320 | tf_op jit(solution)/shard_map/ppermute | solution.py:553
  169.6 11.7 %collective-permute-done.31.refs_3_ = bf16[128,2048]{1,0:T(8,128)(2,1)S(1)} collective-permute-done((bf16[128,2048]{1,0:T(8,128)(2,1)S(1)}, bf16[128,2048]{1,0:T(8,128)(2,1)S(1)}, u32[]{:S(2)}, u32[]{:S(2)}) %collective-permute-start.31) | collective-permute-done | bytes 524320 | tf_op jit(solution)/shard_map/ppermute | solution.py:553
  192.7 10.6 %collective-permute-done.39.refs_6_.refs_26_ = bf16[80,2048]{1,0:T(8,128)(2,1)S(1)} collective-permute-done((bf16[80,2048]{1,0:T(8,128)(2,1)S(1)}, bf16[80,2048]{1,0:T(8,128)(2,1)S(1)}, u32[]{:S(2)}, u32[]{:S(2)}) %collective-permute-start.39) | collective-permute-done | bytes 327712 | tf_op jit(solution)/shard_map/ppermute | solution.py:553
  229.3 6.4 %collective-permute-done.47.refs_2_ = bf16[80,2176]{1,0:T(8,128)(2,1)S(1)} collective-permute-done((bf16[80,2176]{1,0:T(8,128)(2,1)S(1)}, bf16[80,2176]{1,0:T(8,128)(2,1)S(1)}, u32[]{:S(2)}, u32[]{:S(2)}) %collective-permute-start.47) | collective-permute-done | bytes 348192 | tf_op jit(solution)/shard_map/ppermute | solution.py:553
  242.1 11.0 %shard_map.274 = (bf16[80,2176]{1,0:T(8,128)(2,1)S(1)}, bf16[80,2176]{1,0:T(8,128)(2,1)S(1)}, bf16[80,2176]{1,0:T(8,128)(2,1)S(1)}, bf16[80,2176]{1,0:T(8,128)(2...) custom-call(s32[1]{0:T(128)} %bitcast.36.me, ...), custom_call_target="tpu_custom_call" | custom-call | flops 11000000512 | bytes 22000000 | tf_op jit(solution)/shard_map/pallas_call | solution.py:828
  262.5 6.5 %collective-permute-done.55.refs_1_.refs_9_ = bf16[80,2176]{1,0:T(8,128)(2,1)S(1)} collective-permute-done((bf16[80,2176]{1,0:T(8,128)(2,1)S(1)}, bf16[80,2176]{1,0:T(8,128)(2,1)S(1)}, u32[]{:S(2)}, u32[]{:S(2)}) %collective-permute-start.55) | collective-permute-done | bytes 348192 | tf_op jit(solution)/shard_map/ppermute | solution.py:553
  277.8 11.0 %shard_map.276 = (bf16[80,2176]{1,0:T(8,128)(2,1)S(1)}, bf16[80,2176]{1,0:T(8,128)(2,1)S(1)}, bf16[80,2176]{1,0:T(8,128)(2,1)S(1)}, bf16[80,2176]{1,0:T(8,128)(2...) custom-call(s32[1]{0:T(128)} %bitcast.36.me, ...), custom_call_target="tpu_custom_call" | custom-call | flops 11000000512 | bytes 22000000 | tf_op jit(solution)/shard_map/pallas_call | solution.py:828
  302.4 8.5 %collective-permute-start.66 = (bf16[80,2176]{1,0:T(8,128)(2,1)S(1)}, bf16[80,2176]{1,0:T(8,128)(2,1)S(1)}, u32[]{:S(2)}, u32[]{:S(2)}) collective-permute-start(bf16[80,2176]{1,0:T(8,128)(2,1)S(1)} %get-tuple-element.1040), channel_id=1, source_target_pairs={{0,6},{1,7},{2,4},{3,5},{4,2},{5,3},{6,0},{7,1},{8,14},{9,15},{10,... | collective-permute-start | bytes 1044488 | tf_op jit(solution)/shard_map/ppermute | solution.py:553
  311.0 11.4 %shard_map.278 = (bf16[80,2176]{1,0:T(8,128)(2,1)S(1)}, bf16[80,2176]{1,0:T(8,128)(2,1)S(1)}, bf16[80,2176]{1,0:T(8,128)(2,1)S(1)}, bf16[80,2176]{1,0:T(8,128)(2...) custom-call(s32[1]{0:T(128)} %bitcast.36.me, ...), custom_call_target="tpu_custom_call" | custom-call | flops 11000000512 | bytes 22000000 | tf_op jit(solution)/shard_map/pallas_call | solution.py:828
  328.3 11.0 %shard_map.280 = (bf16[80,2176]{1,0:T(8,128)(2,1)S(1)}, bf16[80,2176]{1,0:T(8,128)(2,1)S(1)}, bf16[80,2176]{1,0:T(8,128)(2,1)S(1)}, bf16[80,2176]{1,0:T(8,128)(2...) custom-call(s32[1]{0:T(128)} %bitcast.36.me, ...), custom_call_target="tpu_custom_call" | custom-call | flops 11000000512 | bytes 22000000 | tf_op jit(solution)/shard_map/pallas_call | solution.py:828
  356.0 7.8 %collective-permute-done.73.refs_2_ = bf16[80,2176]{1,0:T(8,128)(2,1)S(1)} collective-permute-done((bf16[80,2176]{1,0:T(8,128)(2,1)S(1)}, bf16[80,2176]{1,0:T(8,128)(2,1)S(1)}, u32[]{:S(2)}, u32[]{:S(2)}) %collective-permute-start.73) | collective-permute-done | bytes 348192 | tf_op jit(solution)/shard_map/ppermute | solution.py:553
  370.9 7.0 %collective-permute-done.78.refs_1_ = bf16[80,2048]{1,0:T(8,128)(2,1)S(1)} collective-permute-done((bf16[80,2048]{1,0:T(8,128)(2,1)S(1)}, bf16[80,2048]{1,0:T(8,128)(2,1)S(1)}, u32[]{:S(2)}, u32[]{:S(2)}) %collective-permute-start.78) | collective-permute-done | bytes 327712 | tf_op jit(solution)/shard_map/ppermute | solution.py:553
  377.9 7.2 %collective-permute-done.79.refs_2_ = bf16[80,2048]{1,0:T(8,128)(2,1)S(1)} collective-permute-done((bf16[80,2048]{1,0:T(8,128)(2,1)S(1)}, bf16[80,2048]{1,0:T(8,128)(2,1)S(1)}, u32[]{:S(2)}, u32[]{:S(2)}) %collective-permute-start.79) | collective-permute-done | bytes 327712 | tf_op jit(solution)/shard_map/ppermute | solution.py:553
  391.0 7.0 %collective-permute-done.82.refs_1_ = bf16[80,2048]{1,0:T(8,128)(2,1)S(1)} collective-permute-done((bf16[80,2048]{1,0:T(8,128)(2,1)S(1)}, bf16[80,2048]{1,0:T(8,128)(2,1)S(1)}, u32[]{:S(2)}, u32[]{:S(2)}) %collective-permute-start.82) | collective-permute-done | bytes 327712 | tf_op jit(solution)/shard_map/ppermute | solution.py:553
  398.7 6.7 %collective-permute-done.83.refs_2_ = bf16[80,2048]{1,0:T(8,128)(2,1)S(1)} collective-permute-done((bf16[80,2048]{1,0:T(8,128)(2,1)S(1)}, bf16[80,2048]{1,0:T(8,128)(2,1)S(1)}, u32[]{:S(2)}, u32[]{:S(2)}) %collective-permute-start.83) | collective-permute-done | bytes 327712 | tf_op jit(solution)/shard_map/ppermute | solution.py:553
  419.8 20.7 %shard_map.290 = (f32[2048,768]{1,0:T(8,128)}, f32[2048,768]{1,0:T(8,128)}, f32[768,2048]{1,0:T(8,128)}) custom-call(bf16[80,2176]{1,0:T(8,128)(2,1)} %copy-done.91, bf16[80,2176]{1,0:T(8,128)(2,1)} %copy-done.92, bf16[80,2176]{1,0:T(8,128)(2,1)} %copy-done.93, bf16[80,2176]{1,0:T(8,128)(2,1)} %copy-done.94, bf16[80,2176]{1,0:T(8,128)(2,1)} %copy-done.95, ...), custom_call_target="tpu_custom_call" | custom-call | flops 20000000000 | bytes 40000000 | tf_op jit(solution)/shard_map/pallas_call | solution.py:924
  456.0 9.9 %shard_map.292 = (bf16[512,1280]{1,0:T(8,128)(2,1)S(1)}, f32[2,128]{1,0:T(2,128)S(1)}) custom-call(f32[512,1280]{1,0:T(8,128)S(1)} %shard_map.265.front, bf16[512,1024]{1,0:T(8,128)(2,1)S(1)} %copy-done.90, bf16[512,128]{1,0:T(8,128)(2,1)S(1)} %copy-done.140, bf16[512,128]{1,0:T(8,128)(2,1)S(1)} %copy-done.142, ...), custom_call_target="tpu_custom_call" | custom-call | flops 17999998976 | bytes 36000000 | tf_op jit(solution)/shard_map/pallas_call | solution.py:979
  467.3 10.7 %collective-permute-done.94.refs_2_ = bf16[128,2048]{1,0:T(8,128)(2,1)S(1)} collective-permute-done((bf16[128,2048]{1,0:T(8,128)(2,1)S(1)}, bf16[128,2048]{1,0:T(8,128)(2,1)S(1)}, u32[]{:S(2)}, u32[]{:S(2)}) %collective-permute-start.94) | collective-permute-done | bytes 524320 | tf_op jit(solution)/shard_map/ppermute | solution.py:553
  488.1 6.4 %collective-permute-done.100.refs_3_ = bf16[80,2048]{1,0:T(8,128)(2,1)S(1)} collective-permute-done((bf16[80,2048]{1,0:T(8,128)(2,1)S(1)}, bf16[80,2048]{1,0:T(8,128)(2,1)S(1)}, u32[]{:S(2)}, u32[]{:S(2)}) %collective-permute-start.100) | collective-permute-done | bytes 327712 | tf_op jit(solution)/shard_map/ppermute | solution.py:553
  494.4 6.0 collective-permute-done.98.refs_1_
  509.1 6.6 %shard_map.296 = (bf16[128,2048]{1,0:T(8,128)(2,1)S(1)}, bf16[128,2048]{1,0:T(8,128)(2,1)S(1)}, bf16[128,2048]{1,0:T(8,128)(2,1)S(1)}, bf16[128,2048]{1,0:T(8,128)(2,1)S(1)}) custom-call(s32[1]{0:T(128)} %bitcast.31.my_outer, bf16[512,1280]{1,0:T(8,128)(2,1)S(1)} %get-tuple-element.1517.grad, bf16[256,1408]{1,0:T(8,128)(2,1)S(1)} %copy-done.8, ...), custom_call_target="tpu_custom_call" | custom-call | tf_op jit(solution)/shard_map/pallas_call | solution.py:1057
  520.2 12.9 %collective-permute-done.103.first = bf16[128,2048]{1,0:T(8,128)(2,1)} collective-permute-done((bf16[128,2048]{1,0:T(8,128)(2,1)}, bf16[128,2048]{1,0:T(8,128)(2,1)}, u32[]{:S(2)}, u32[]{:S(2)}) %collective-permute-start.103) | collective-permute-done | bytes 524320 | tf_op jit(solution)/shard_map/ppermute | solution.py:558
  550.1 11.6 %collective-permute-done.107 = bf16[128,2048]{1,0:T(8,128)(2,1)S(1)} collective-permute-done((bf16[128,2048]{1,0:T(8,128)(2,1)S(1)}, bf16[128,2048]{1,0:T(8,128)(2,1)S(1)}, u32[]{:S(2)}, u32[]{:S(2)}) %collective-permute-start.107) | collective-permute-done | bytes 524320 | tf_op jit(solution)/shard_map/ppermute | solution.py:558
  565.8 6.7 %collective-permute-done.106.first = bf16[256,1280]{1,0:T(8,128)(2,1)S(1)} collective-permute-done((bf16[256,1280]{1,0:T(8,128)(2,1)S(1)}, bf16[256,1280]{1,0:T(8,128)(2,1)S(1)}, u32[]{:S(2)}, u32[]{:S(2)}) %collective-permute-start.106) | collective-permute-done | bytes 655392 | tf_op jit(solution)/shard_map/ppermute | solution.py:558
  586.6 11.4 %collective-permute-done.115 = bf16[128,2048]{1,0:T(8,128)(2,1)S(1)} collective-permute-done((bf16[128,2048]{1,0:T(8,128)(2,1)S(1)}, bf16[128,2048]{1,0:T(8,128)(2,1)S(1)}, u32[]{:S(2)}, u32[]{:S(2)}) %collective-permute-start.115) | collective-permute-done | bytes 524320 | tf_op jit(solution)/shard_map/ppermute | solution.py:558
  598.1 7.1 %collective-permute-done.114 = bf16[256,1280]{1,0:T(8,128)(2,1)S(1)} collective-permute-done((bf16[256,1280]{1,0:T(8,128)(2,1)S(1)}, bf16[256,1280]{1,0:T(8,128)(2,1)S(1)}, u32[]{:S(2)}, u32[]{:S(2)}) %collective-permute-start.114) | collective-permute-done | bytes 655392 | tf_op jit(solution)/shard_map/ppermute | solution.py:558
  (712 shorter events, 311.7 us)
Async XLA Ops:
  19.3 36.1 %collective-permute-start.8 = (bf16[256,1408]{1,0:T(8,128)(2,1)S(1)}, bf16[256,1408]{1,0:T(8,128)(2,1)S(1)}, u32[]{:S(2)}, u32[]{:S(2)}) collective-permute-start(bf16[256,1408]{1,0:T(8,128)(2,1)S(1)} %constant_dynamic-update-slice_fusion.refs_0_), channel_id=1, source_target_pairs={{0,8},{1,9},{2,10},{3,11},{4,12},{5,13},{6,14},{7,15},{8,16},{9,17... | collective-permute-start | bytes 2162696 | tf_op jit(solution)/shard_map/ppermute | solution.py:558
  21.0 34.5 %collective-permute-start.9 = (bf16[256,1408]{1,0:T(8,128)(2,1)S(1)}, bf16[256,1408]{1,0:T(8,128)(2,1)S(1)}, u32[]{:S(2)}, u32[]{:S(2)}) collective-permute-start(bf16[256,1408]{1,0:T(8,128)(2,1)S(1)} %constant_dynamic-update-slice_fusion.refs_0_), channel_id=1, source_target_pairs={{0,1},{1,0},{2,3},{3,2},{4,5},{5,4},{6,7},{7,6},{8,9},{9,8},{10,11... | collective-permute-start | bytes 2162696 | tf_op jit(solution)/shard_map/ppermute | solution.py:548
  21.3 32.4 %collective-permute-start.5 = (bf16[128,2048]{1,0:T(8,128)(2,1)S(1)}, bf16[128,2048]{1,0:T(8,128)(2,1)}, u32[]{:S(2)}, u32[]{:S(2)}) collective-permute-start(bf16[128,2048]{1,0:T(8,128)(2,1)S(1)} %copy-done.5), channel_id=1, source_target_pairs={{0,2},{1,3},{2,0},{3,1},{4,6},{5,7},{6,4},{7,5},{8,10},{9,11},{10,... | collective-permute-start | bytes 1572872 | tf_op jit(solution)/shard_map/ppermute | solution.py:553
  22.5 32.9 %collective-permute-start.6 = (bf16[128,2048]{1,0:T(8,128)(2,1)S(1)}, bf16[128,2048]{1,0:T(8,128)(2,1)}, u32[]{:S(2)}, u32[]{:S(2)}) collective-permute-start(bf16[128,2048]{1,0:T(8,128)(2,1)S(1)} %copy-done.5), channel_id=1, source_target_pairs={{0,4},{1,5},{2,6},{3,7},{4,0},{5,1},{6,2},{7,3},{8,12},{9,13},{10,... | collective-permute-start | bytes 1572872 | tf_op jit(solution)/shard_map/ppermute | solution.py:553
  55.4 31.5 %collective-permute-start.15 = (bf16[256,1408]{1,0:T(8,128)(2,1)S(1)}, bf16[256,1408]{1,0:T(8,128)(2,1)S(1)}, u32[]{:S(2)}, u32[]{:S(2)}) collective-permute-start(bf16[256,1408]{1,0:T(8,128)(2,1)S(1)} %collective-permute-done.8.refs_1_), channel_id=1, source_target_pairs={{0,8},{1,9},{2,10},{3,11},{4,12},{5,13},{6,14},{7,15},{8,16},{9,17... | collective-permute-start | bytes 2162696 | tf_op jit(solution)/shard_map/ppermute | solution.py:558
  55.5 31.5 %collective-permute-start.16 = (bf16[256,1408]{1,0:T(8,128)(2,1)S(1)}, bf16[256,1408]{1,0:T(8,128)(2,1)S(1)}, u32[]{:S(2)}, u32[]{:S(2)}) collective-permute-start(bf16[256,1408]{1,0:T(8,128)(2,1)S(1)} %collective-permute-done.8.refs_1_), channel_id=1, source_target_pairs={{0,1},{1,0},{2,3},{3,2},{4,5},{5,4},{6,7},{7,6},{8,9},{9,8},{10,11... | collective-permute-start | bytes 2162696 | tf_op jit(solution)/shard_map/ppermute | solution.py:548
  58.5 28.5 %collective-permute-start.17 = (bf16[128,2048]{1,0:T(8,128)(2,1)}, bf16[128,2048]{1,0:T(8,128)(2,1)S(1)}, u32[]{:S(2)}, u32[]{:S(2)}) collective-permute-start(bf16[128,2048]{1,0:T(8,128)(2,1)} %collective-permute-done.10), channel_id=1, source_target_pairs={{0,8},{1,9},{2,10},{3,11},{4,12},{5,13},{6,14},{7,15},{8,16},{9,17... | collective-permute-start | bytes 1572872 | tf_op jit(solution)/shard_map/ppermute | solution.py:558
  88.3 30.9 %collective-permute-start.4 = (bf16[128,2176]{1,0:T(8,128)(2,1)S(1)}, bf16[128,2176]{1,0:T(8,128)(2,1)}, u32[]{:S(2)}, u32[]{:S(2)}) collective-permute-start(bf16[128,2176]{1,0:T(8,128)(2,1)S(1)} %pad_maximum_fusion.4.own), channel_id=1, source_target_pairs={{0,8},{1,9},{2,10},{3,11},{4,12},{5,13},{6,14},{7,15},{8,16},{9,17... | collective-permute-start | bytes 1671176 | tf_op jit(solution)/shard_map/ppermute | solution.py:558
  93.0 26.1 %collective-permute-start.18 = (bf16[128,2048]{1,0:T(8,128)(2,1)}, bf16[128,2048]{1,0:T(8,128)(2,1)S(1)}, u32[]{:S(2)}, u32[]{:S(2)}) collective-permute-start(bf16[128,2048]{1,0:T(8,128)(2,1)} %get-tuple-element.1594), channel_id=1, source_target_pairs={{0,2},{1,3},{2,0},{3,1},{4,6},{5,7},{6,4},{7,5},{8,10},{9,11},{10,... | collective-permute-start | bytes 1572872 | tf_op jit(solution)/shard_map/ppermute | solution.py:553
  94.5 24.6 %collective-permute-start.19 = (bf16[128,2048]{1,0:T(8,128)(2,1)}, bf16[128,2048]{1,0:T(8,128)(2,1)}, u32[]{:S(2)}, u32[]{:S(2)}) collective-permute-start(bf16[128,2048]{1,0:T(8,128)(2,1)} %get-tuple-element.1593), channel_id=1, source_target_pairs={{0,4},{1,5},{2,6},{3,7},{4,0},{5,1},{6,2},{7,3},{8,12},{9,13},{10,... | collective-permute-start | bytes 1572872 | tf_op jit(solution)/shard_map/ppermute | solution.py:553
  122.8 25.7 %collective-permute-start.25 = (bf16[512,2048]{1,0:T(8,128)(2,1)S(1)}, bf16[512,2048]{1,0:T(8,128)(2,1)S(1)}, u32[]{:S(2)}, u32[]{:S(2)}) collective-permute-start(bf16[512,2048]{1,0:T(8,128)(2,1)S(1)} %pad_maximum_fusion.1), channel_id=1, source_target_pairs={{0,1},{1,0},{2,3},{3,2},{4,5},{5,4},{6,7},{7,6},{8,9},{9,8},{10,11... | collective-permute-start | bytes 6291464 | tf_op jit(solution)/shard_map/ppermute | solution.py:548
  150.7 30.6 %collective-permute-start.33 = (bf16[128,2176]{1,0:T(8,128)(2,1)S(1)}, bf16[128,2176]{1,0:T(8,128)(2,1)S(1)}, u32[]{:S(2)}, u32[]{:S(2)}) collective-permute-start(bf16[128,2176]{1,0:T(8,128)(2,1)S(1)} %collective-permute-done.26.own), channel_id=1, source_target_pairs={{0,8},{1,9},{2,10},{3,11},{4,12},{5,13},{6,14},{7,15},{8,16},{9,17... | collective-permute-start | bytes 1671176 | tf_op jit(solution)/shard_map/ppermute | solution.py:558
  153.1 28.1 %collective-permute-start.34 = (bf16[128,2176]{1,0:T(8,128)(2,1)S(1)}, bf16[128,2176]{1,0:T(8,128)(2,1)S(1)}, u32[]{:S(2)}, u32[]{:S(2)}) collective-permute-start(bf16[128,2176]{1,0:T(8,128)(2,1)S(1)} %collective-permute-done.26.own), channel_id=1, source_target_pairs={{0,1},{1,0},{2,3},{3,2},{4,5},{5,4},{6,7},{7,6},{8,9},{9,8},{10,11... | collective-permute-start | bytes 1671176 | tf_op jit(solution)/shard_map/ppermute | solution.py:548
  156.0 25.3 %collective-permute-start.31 = (bf16[128,2048]{1,0:T(8,128)(2,1)S(1)}, bf16[128,2048]{1,0:T(8,128)(2,1)S(1)}, u32[]{:S(2)}, u32[]{:S(2)}) collective-permute-start(bf16[128,2048]{1,0:T(8,128)(2,1)S(1)} %get-tuple-element.1597), channel_id=1, source_target_pairs={{0,4},{1,5},{2,6},{3,7},{4,0},{5,1},{6,2},{7,3},{8,12},{9,13},{10,... | collective-permute-start | bytes 1572872 | tf_op jit(solution)/shard_map/ppermute | solution.py:553
  207.6 28.1 %collective-permute-start.41 = (bf16[128,2176]{1,0:T(8,128)(2,1)S(1)}, bf16[128,2176]{1,0:T(8,128)(2,1)S(1)}, u32[]{:S(2)}, u32[]{:S(2)}) collective-permute-start(bf16[128,2176]{1,0:T(8,128)(2,1)S(1)} %collective-permute-done.35.own), channel_id=1, source_target_pairs={{0,8},{1,9},{2,10},{3,11},{4,12},{5,13},{6,14},{7,15},{8,16},{9,17... | collective-permute-start | bytes 1671176 | tf_op jit(solution)/shard_map/ppermute | solution.py:558
  209.6 26.1 %collective-permute-start.42 = (bf16[128,2176]{1,0:T(8,128)(2,1)S(1)}, bf16[128,2176]{1,0:T(8,128)(2,1)S(1)}, u32[]{:S(2)}, u32[]{:S(2)}) collective-permute-start(bf16[128,2176]{1,0:T(8,128)(2,1)S(1)} %collective-permute-done.35.own), channel_id=1, source_target_pairs={{0,1},{1,0},{2,3},{3,2},{4,5},{5,4},{6,7},{7,6},{8,9},{9,8},{10,11... | collective-permute-start | bytes 1671176 | tf_op jit(solution)/shard_map/ppermute | solution.py:548
  260.2 28.7 %collective-permute-start.57 = (bf16[80,2176]{1,0:T(8,128)(2,1)S(1)}, bf16[80,2176]{1,0:T(8,128)(2,1)S(1)}, u32[]{:S(2)}, u32[]{:S(2)}) collective-permute-start(bf16[80,2176]{1,0:T(8,128)(2,1)S(1)} %get-tuple-element.993), channel_id=1, source_target_pairs={{0,6},{1,7},{2,4},{3,5},{4,2},{5,3},{6,0},{7,1},{8,14},{9,15},{10,... | collective-permute-start | bytes 1044488 | tf_op jit(solution)/shard_map/ppermute | solution.py:553
  261.4 29.1 %collective-permute-start.54 = (bf16[128,2176]{1,0:T(8,128)(2,1)S(1)}, bf16[128,2176]{1,0:T(8,128)(2,1)S(1)}, u32[]{:S(2)}, u32[]{:S(2)}) collective-permute-start(bf16[128,2176]{1,0:T(8,128)(2,1)S(1)} %collective-permute-done.49.own), channel_id=1, source_target_pairs={{0,1},{1,0},{2,3},{3,2},{4,5},{5,4},{6,7},{7,6},{8,9},{9,8},{10,11... | collective-permute-start | bytes 1671176 | tf_op jit(solution)/shard_map/ppermute | solution.py:548
  261.4 27.5 %collective-permute-start.58 = (bf16[80,2176]{1,0:T(8,128)(2,1)S(1)}, bf16[80,2176]{1,0:T(8,128)(2,1)S(1)}, u32[]{:S(2)}, u32[]{:S(2)}) collective-permute-start(bf16[80,2176]{1,0:T(8,128)(2,1)S(1)} %get-tuple-element.994), channel_id=1, source_target_pairs={{0,2},{1,3},{2,0},{3,1},{4,6},{5,7},{6,4},{7,5},{8,10},{9,11},{10,... | collective-permute-start | bytes 1044488 | tf_op jit(solution)/shard_map/ppermute | solution.py:553
  295.1 27.8 %collective-permute-start.67 = (bf16[128,2176]{1,0:T(8,128)(2,1)S(1)}, bf16[128,2176]{1,0:T(8,128)(2,1)S(1)}, u32[]{:S(2)}, u32[]{:S(2)}) collective-permute-start(bf16[128,2176]{1,0:T(8,128)(2,1)S(1)} %get-tuple-element.1051), channel_id=1, source_target_pairs={{0,1},{1,0},{2,3},{3,2},{4,5},{5,4},{6,7},{7,6},{8,9},{9,8},{10,11... | collective-permute-start | bytes 1671176 | tf_op jit(solution)/shard_map/ppermute | solution.py:548
  295.1 27.3 %collective-permute-start.63 = (bf16[80,2176]{1,0:T(8,128)(2,1)S(1)}, bf16[80,2176]{1,0:T(8,128)(2,1)S(1)}, u32[]{:S(2)}, u32[]{:S(2)}) collective-permute-start(bf16[80,2176]{1,0:T(8,128)(2,1)S(1)} %get-tuple-element.1037), channel_id=1, source_target_pairs={{0,6},{1,7},{2,4},{3,5},{4,2},{5,3},{6,0},{7,1},{8,14},{9,15},{10,... | collective-permute-start | bytes 1044488 | tf_op jit(solution)/shard_map/ppermute | solution.py:553
  296.4 26.1 %collective-permute-start.64 = (bf16[80,2176]{1,0:T(8,128)(2,1)S(1)}, bf16[80,2176]{1,0:T(8,128)(2,1)S(1)}, u32[]{:S(2)}, u32[]{:S(2)}) collective-permute-start(bf16[80,2176]{1,0:T(8,128)(2,1)S(1)} %get-tuple-element.1038), channel_id=1, source_target_pairs={{0,2},{1,3},{2,0},{3,1},{4,6},{5,7},{6,4},{7,5},{8,10},{9,11},{10,... | collective-permute-start | bytes 1044488 | tf_op jit(solution)/shard_map/ppermute | solution.py:553
  412.0 28.5 %collective-permute-start.87 = (bf16[128,2048]{1,0:T(8,128)(2,1)}, bf16[128,2048]{1,0:T(8,128)(2,1)}, u32[]{:S(2)}, u32[]{:S(2)}) collective-permute-start(bf16[128,2048]{1,0:T(8,128)(2,1)} %get-tuple-element.1375), channel_id=1, source_target_pairs={{0,2},{1,3},{2,0},{3,1},{4,6},{5,7},{6,4},{7,5},{8,10},{9,11},{10,... | collective-permute-start | bytes 1572872 | tf_op jit(solution)/shard_map/ppermute | solution.py:553
  412.9 27.6 %collective-permute-start.88 = (bf16[128,2048]{1,0:T(8,128)(2,1)}, bf16[128,2048]{1,0:T(8,128)(2,1)}, u32[]{:S(2)}, u32[]{:S(2)}) collective-permute-start(bf16[128,2048]{1,0:T(8,128)(2,1)} %get-tuple-element.1375), channel_id=1, source_target_pairs={{0,4},{1,5},{2,6},{3,7},{4,0},{5,1},{6,2},{7,3},{8,12},{9,13},{10,... | collective-permute-start | bytes 1572872 | tf_op jit(solution)/shard_map/ppermute | solution.py:553
  414.1 26.4 %collective-permute-start.89 = (bf16[128,2048]{1,0:T(8,128)(2,1)}, bf16[128,2048]{1,0:T(8,128)(2,1)}, u32[]{:S(2)}, u32[]{:S(2)}) collective-permute-start(bf16[128,2048]{1,0:T(8,128)(2,1)} %get-tuple-element.1375), channel_id=1, source_target_pairs={{0,6},{1,7},{2,4},{3,5},{4,2},{5,3},{6,0},{7,1},{8,14},{9,15},{10,... | collective-permute-start | bytes 1572872 | tf_op jit(solution)/shard_map/ppermute | solution.py:553
  417.7 24.6 %collective-permute-start.90 = (bf16[128,2048]{1,0:T(8,128)(2,1)}, bf16[128,2048]{1,0:T(8,128)(2,1)}, u32[]{:S(2)}, u32[]{:S(2)}) collective-permute-start(bf16[128,2048]{1,0:T(8,128)(2,1)} %add_convert_fusion.9), channel_id=1, source_target_pairs={{0,8},{1,9},{2,10},{3,11},{4,12},{5,13},{6,14},{7,15},{8,16},{9,17... | collective-permute-start | bytes 1572872 | tf_op jit(solution)/shard_map/ppermute | solution.py:558
  453.4 24.5 %collective-permute-start.94 = (bf16[128,2048]{1,0:T(8,128)(2,1)S(1)}, bf16[128,2048]{1,0:T(8,128)(2,1)S(1)}, u32[]{:S(2)}, u32[]{:S(2)}) collective-permute-start(bf16[128,2048]{1,0:T(8,128)(2,1)S(1)} %get-tuple-element.1589), channel_id=1, source_target_pairs={{0,4},{1,5},{2,6},{3,7},{4,0},{5,1},{6,2},{7,3},{8,12},{9,13},{10,... | collective-permute-start | bytes 1572872 | tf_op jit(solution)/shard_map/ppermute | solution.py:553
  503.0 30.1 %collective-permute-start.102 = (bf16[256,1280]{1,0:T(8,128)(2,1)}, bf16[256,1280]{1,0:T(8,128)(2,1)}, u32[]{:S(2)}, u32[]{:S(2)}) collective-permute-start(bf16[256,1280]{1,0:T(8,128)(2,1)} %get-tuple-element.1512), channel_id=1, source_target_pairs={{0,8},{1,9},{2,10},{3,11},{4,12},{5,13},{6,14},{7,15},{8,16},{9,17... | collective-permute-start | bytes 1966088 | tf_op jit(solution)/shard_map/ppermute | solution.py:558
  506.9 26.2 %collective-permute-start.103 = (bf16[128,2048]{1,0:T(8,128)(2,1)}, bf16[128,2048]{1,0:T(8,128)(2,1)}, u32[]{:S(2)}, u32[]{:S(2)}) collective-permute-start(bf16[128,2048]{1,0:T(8,128)(2,1)} %shard_map.295), channel_id=1, source_target_pairs={{0,8},{1,9},{2,10},{3,11},{4,12},{5,13},{6,14},{7,15},{8,16},{9,17... | collective-permute-start | bytes 1572872 | tf_op jit(solution)/shard_map/ppermute | solution.py:558
  537.9 25.0 %collective-permute-start.108 = (bf16[128,2048]{1,0:T(8,128)(2,1)}, bf16[128,2048]{1,0:T(8,128)(2,1)S(1)}, u32[]{:S(2)}, u32[]{:S(2)}) collective-permute-start(bf16[128,2048]{1,0:T(8,128)(2,1)} %copy-done.57), channel_id=1, source_target_pairs={{0,2},{1,3},{2,0},{3,1},{4,6},{5,7},{6,4},{7,5},{8,10},{9,11},{10,... | collective-permute-start | bytes 1572872 | tf_op jit(solution)/shard_map/ppermute | solution.py:553
  539.0 24.5 %collective-permute-start.109 = (bf16[128,2048]{1,0:T(8,128)(2,1)}, bf16[128,2048]{1,0:T(8,128)(2,1)S(1)}, u32[]{:S(2)}, u32[]{:S(2)}) collective-permute-start(bf16[128,2048]{1,0:T(8,128)(2,1)} %copy-done.56), channel_id=1, source_target_pairs={{0,4},{1,5},{2,6},{3,7},{4,0},{5,1},{6,2},{7,3},{8,12},{9,13},{10,... | collective-permute-start | bytes 1572872 | tf_op jit(solution)/shard_map/ppermute | solution.py:553
  545.6 26.9 %collective-permute-start.106 = (bf16[256,1280]{1,0:T(8,128)(2,1)S(1)}, bf16[256,1280]{1,0:T(8,128)(2,1)S(1)}, u32[]{:S(2)}, u32[]{:S(2)}) collective-permute-start(bf16[256,1280]{1,0:T(8,128)(2,1)S(1)} %shard_map.299), channel_id=1, source_target_pairs={{0,8},{1,9},{2,10},{3,11},{4,12},{5,13},{6,14},{7,15},{8,16},{9,17... | collective-permute-start | bytes 1966088 | tf_op jit(solution)/shard_map/ppermute | solution.py:558
  (268 other events, 5494.3 us)
